TPU v7x, 512 devices: a whole 4x4x16 slice. The times are simulated.
512 devices in a mesh: gx: 4 (over y_lo, core), gy: 4 (over x), gz: 32 (over y_hi, z).
Axes of the slice: x: 4, y: 4 (y_hi: 2, y_lo: 2; y = y_hi * 2 + y_lo), z: 16, core: 2. Of those that a mesh axis runs over, the one named last changes fastest.
Arguments:
- coarse: bfloat16 [16, 32, 8192], P('gx', 'gy', 'gz'), may hold values from -6 to 6
- skip_features: bfloat16 [32, 64, 8192], P('gx', 'gy', 'gz'), may hold values from -6 to 6
- pre_act: bfloat16 [32, 64, 8192], P('gx', 'gy', 'gz'), may hold values from -9 to 9
- cotangent: bfloat16 [3, 32, 64, 128], P(None, 'gx', 'gy', 'gz'), may hold values from -24 to 24
- weight_one: bfloat16 [27, 12288], replicated, may hold values from -0.078125 to 0.078125
- weight_out: bfloat16 [27, 3, 64], replicated, may hold values from -0.15625 to 0.15625
Outputs:
- coarse_grad: bfloat16 [16, 32, 8192], P('gx', 'gy', 'gz')
- skip_grad: bfloat16 [32, 64, 8192], P('gx', 'gy', 'gz')
- weight_one_grad: float32 [27, 12288], replicated
- weight_out_grad: float32 [27, 3, 64], replicated
All inputs are finite; a program needn't handle non-finite values.
Results may differ from a plain program's by a relative error of at most 0.0049.
Values may be sent and summed in bfloat16 or wider, within the bound.
No kernel may reach another device: no remote copies, remote signals or barrier semaphores. Data moves between devices by JAX's collectives and lax.ppermute only.
A program may use at most 64 MiB of HBM per device.

v0:
```python
import math

import jax
import jax.numpy as jnp
from jax import lax
from jax.sharding import PartitionSpec as P

C_UP = 128


root_half = 0.7071067811865476
inv_root_tau = 0.3989422804014327


def extended(array, sides, width):
    for axis, dim in sides:
        peers, length = (lax.axis_size(axis), array.shape[dim])
        up = [(i, (i + 1) % peers) for i in range(peers)]
        down = [(j, i) for i, j in up]
        last = lax.slice_in_dim(array, length - width, length, axis=dim)
        first = lax.slice_in_dim(array, 0, width, axis=dim)
        before = lax.ppermute(last, axis, up)
        after = lax.ppermute(first, axis, down)
        array = jnp.concatenate([before, array, after], axis=dim)
    return array


def gelu_value(values):
    return 0.5 * values * (1.0 + lax.erf(values * root_half))


def gelu_slope(values):
    return (
        0.5 * (1.0 + lax.erf(values * root_half))
        + values * jnp.exp(-0.5 * values * values) * inv_root_tau
    )


def to_channels(packed, channels):
    shaped = packed.reshape(packed.shape[0], packed.shape[1], packed.shape[2] // channels, channels)
    return jnp.transpose(shaped, (3, 0, 1, 2))


def from_channels(field):
    moved = jnp.transpose(field, (1, 2, 3, 0))
    return moved.reshape(moved.shape[0], moved.shape[1], moved.shape[2] * moved.shape[3])


def upsample(coarse):
    doubled = jnp.repeat(coarse, 2, axis=1)
    doubled = jnp.repeat(doubled, 2, axis=2)
    return jnp.repeat(doubled, 2, axis=3)


def window_at(padded, shift_x, shift_y, shift_z, grid_shape):
    size_x, size_y, size_z = grid_shape
    cut_piece = padded[
        :,
        1 + shift_x : 1 + shift_x + size_x,
        1 + shift_y : 1 + shift_y + size_y,
        1 + shift_z : 1 + shift_z + size_z,
    ]
    return cut_piece.reshape(padded.shape[0], size_x * size_y * size_z)


def stacked_taps(padded, direction, shift_x, grid_shape):
    return jnp.concatenate(
        [
            window_at(
                padded, direction * shift_x, direction * shift_y, direction * shift_z, grid_shape
            )
            for shift_y in (-1, 0, 1)
            for shift_z in (-1, 0, 1)
        ],
        axis=0,
    )


def contract_rows(left_side, right_side):
    return lax.dot_general(
        left_side, right_side, (((0,), (0,)), ((), ())), preferred_element_type=jnp.float32
    )


def contract_cells(left_side, right_side):
    return lax.dot_general(
        left_side, right_side, (((1,), (1,)), ((), ())), preferred_element_type=jnp.float32
    )


def grad_rims(grid_field):
    return extended(grid_field, (("gx", 1), ("gy", 2), ("gz", 3)), 1)


def input_rims(grid_field):
    return extended(grid_field, (("gx", 1), ("gy", 2), ("gz", 3)), 1)


def per_device(coarse, skip_features, pre_act, cotangent, weight_one, weight_out):
    tap_count = weight_out.shape[0]
    hid_channels = weight_out.shape[2]
    vel_channels = cotangent.shape[0]
    up_channels = C_UP
    coarse = to_channels(coarse, up_channels)
    skip_features = to_channels(skip_features, hid_channels)
    pre_act = to_channels(pre_act, hid_channels)
    weight_one = weight_one.reshape(tap_count, hid_channels, weight_one.shape[1] // hid_channels)
    grid_shape = skip_features.shape[1:]
    cell_count = grid_shape[0] * grid_shape[1] * grid_shape[2]
    in_channels = up_channels + hid_channels
    pre_float = pre_act.astype(jnp.float32).reshape(hid_channels, cell_count)
    hidden = gelu_value(pre_float).astype(jnp.bfloat16)
    rim_cot = grad_rims(cotangent)
    cot_back = jnp.concatenate(
        [stacked_taps(rim_cot, -1, shift_x, grid_shape) for shift_x in (-1, 0, 1)], axis=0
    )
    d_hidden = contract_rows(weight_out.reshape(tap_count * vel_channels, hid_channels), cot_back)
    rim_hidden = input_rims(hidden.reshape(hid_channels, *grid_shape))
    cot_flat = cotangent.reshape(vel_channels, cell_count)
    head_parts = []
    for shift_x in (-1, 0, 1):
        shifted = stacked_taps(rim_hidden, 1, shift_x, grid_shape)
        partial_value = contract_cells(cot_flat, shifted).reshape(vel_channels, 9, hid_channels)
        head_parts.append(jnp.transpose(partial_value, (1, 0, 2)))
    head_grad = jnp.concatenate(head_parts, axis=0)
    d_pre = (d_hidden * gelu_slope(pre_float)).astype(jnp.bfloat16)
    rim_pre = grad_rims(d_pre.reshape(hid_channels, *grid_shape))
    d_input = jnp.zeros((in_channels, cell_count), jnp.float32)
    body_parts = []
    for group_index, shift_x in enumerate((-1, 0, 1)):
        pre_back = stacked_taps(rim_pre, -1, shift_x, grid_shape)
        tap_rows = weight_one[9 * group_index : 9 * group_index + 9].reshape(
            9 * hid_channels, in_channels
        )
        d_input = d_input + contract_rows(tap_rows, pre_back)
    rim_coarse = extended(coarse, (("gx", 1), ("gy", 2), ("gz", 3)), 1)
    fine_coarse = upsample(rim_coarse)[:, 1:-1, 1:-1, 1:-1]
    rim_skip = input_rims(skip_features)
    rim_inputs = jnp.concatenate([fine_coarse, rim_skip], axis=0)
    for shift_x in (-1, 0, 1):
        for shift_y in (-1, 0, 1):
            shifted = jnp.concatenate(
                [
                    window_at(rim_inputs, shift_x, shift_y, shift_z, grid_shape)
                    for shift_z in (-1, 0, 1)
                ],
                axis=0,
            )
            partial_value = contract_cells(d_pre, shifted).reshape(hid_channels, 3, in_channels)
            body_parts.append(jnp.transpose(partial_value, (1, 0, 2)))
    body_grad = jnp.concatenate(body_parts, axis=0)
    summed_body, summed_head = lax.psum((body_grad, head_grad), ("gx", "gy", "gz"))
    total_cells = cell_count * lax.axis_size("gx") * lax.axis_size("gy") * lax.axis_size("gz")
    norm_factor = 1.0 / math.sqrt(total_cells)
    size_x, size_y, size_z = grid_shape
    skip_grad = (
        d_input[up_channels:]
        .reshape(in_channels - up_channels, size_x, size_y, size_z)
        .astype(jnp.bfloat16)
    )
    coarse_grad = (
        d_input[:up_channels]
        .reshape(up_channels, size_x // 2, 2, size_y // 2, 2, size_z // 2, 2)
        .sum(axis=(2, 4, 6))
        .astype(jnp.bfloat16)
    )
    body_out = (summed_body * norm_factor).reshape(tap_count, hid_channels * in_channels)
    return (
        from_channels(coarse_grad),
        from_channels(skip_grad),
        body_out,
        summed_head * norm_factor,
    )


def solution(mesh):
    in_specs = (
        P("gx", "gy", "gz"),
        P("gx", "gy", "gz"),
        P("gx", "gy", "gz"),
        P(None, "gx", "gy", "gz"),
        P(),
        P(),
    )
    out_specs = (P("gx", "gy", "gz"), P("gx", "gy", "gz"), P(), P())
    return jax.shard_map(
        per_device, mesh=mesh, in_specs=in_specs, out_specs=out_specs, check_vma=False
    )
```

profile of v0, /device:TPU:1, one launch (start us, length us, event | category | flops | bytes accessed | tf_op | source)
XLA Modules:
  0.0 827.4 jit_solution(11305838592156521752)
XLA Ops:
  8.4 4.6 collective-permute-start.24
  13.0 6.1 collective-permute-start.25
  19.9 1.9 collective-permute-start
  21.8 3.6 collective-permute-start.1
  26.1 1.9 collective-permute-start.12
  31.8 1.9 collective-permute-start.2
  33.7 4.6 collective-permute-start.3
  39.4 11.6 %collective-permute-start.4 = (bf16[3,10,18,1]{2,3,1,0:T(2,128)(2,1)S(1)}, bf16[3,10,18,1]{2,3,1,0:T(2,128)(2,1)S(1)}, u32[]{:S(2)}, u32[]{:S(2)}) collective-permute-start(bf16[3,10,18,1]{2,3,1,0:T(2,128)(2,1)S(1)} %get-tuple-element.144), channel_id=1, source_target_pairs={{1,0},{2,1},{3,2},{4,3},{5,4},{6,5},{7,6},{8,7},{9,8},{10,9},{11,1... | collective-permute-start | bytes 3248 | tf_op jit(solution)/shard_map/ppermute | solution.py:23
  51.1 1.9 collective-permute-start.5
  55.7 2.6 collective-permute-start.13
  59.1 3.8 collective-permute-start.18
  72.1 3.1 collective-permute-start.14
  75.3 3.4 collective-permute-start.15
  78.7 2.4 collective-permute-start.19
  81.1 3.2 collective-permute-start.6
  84.4 1.9 collective-permute-start.7
  86.3 1.9 collective-permute-start.16
  89.1 7.0 collective-permute-start.17
  96.1 1.9 collective-permute-start.26
  98.1 4.6 collective-permute-start.27
  102.7 1.9 collective-permute-start.20
  105.4 4.6 collective-permute-start.21
  110.0 2.1 collective-permute-start.8
  113.9 4.6 collective-permute-start.9
  118.4 1.9 collective-permute-start.28
  122.1 7.0 collective-permute-start.29
  129.1 1.9 collective-permute-start.22
  135.6 7.0 collective-permute-start.23
  142.5 1.9 collective-permute-start.10
  145.1 3.4 collective-permute-start.11
  149.1 3.8 fusion.76
  153.0 1.9 fusion.77
  155.3 2.1 fusion.78
  159.2 1.6 copy.230
  179.3 105.0 %psum.15 = f32[27,3,64]{2,0,1:T(8,128)} all-reduce(f32[27,3,64]{2,0,1:T(8,128)S(1)} %pad_maximum_fusion.14), channel_id=1, replica_groups=mesh['gx'=4,'gy'=4,'gz'=32] {'gx','gy','gz'}, use_global_device_ids=true, to_apply=%region_2.0 | all-reduce | flops 5184 | bytes 41472 | tf_op jit(solution)/shard_map/psum | solution.py:152
  284.3 1.8 reshape.508
  286.1 1.9 reshape.509
  287.9 1.8 reshape.510
  289.7 2.2 fusion.33
  291.9 1.7 reshape.511
  294.5 1.9 reshape.505
  297.3 2.2 fusion.27
  299.4 1.8 reshape.507
  302.1 1.9 reshape.501
  308.0 1.9 reshape.496
  309.9 1.9 reshape.497
  311.7 2.1 fusion.15
  313.8 1.8 reshape.499
  321.6 1.8 reshape.512
  323.5 1.8 reshape.513
  325.3 1.8 reshape.514
  327.1 2.1 fusion.39
  329.2 1.8 reshape.515
  331.0 1.8 reshape.516
  332.8 1.8 reshape.517
  334.6 1.8 reshape.518
  336.4 2.1 fusion.45
  338.5 1.7 reshape.519
  340.3 1.8 reshape.520
  343.9 2.2 fusion.51
  346.0 1.8 reshape.523
  371.9 445.1 %all-reduce.2.cloned.1.call-done = f32[27,64,192]{2,1,0:T(8,128)} async-done(((f32[27,64,192]{2,1,0:T(8,128)}), f32[27,64,192]{2,1,0:T(8,128)}) %all-reduce.2.cloned.1.call-update) | async-done | bytes 1327120 | tf_op jit(solution)/shard_map/psum | solution.py:152
  817.0 1.6 broadcast_multiply_fusion
  818.7 1.9 reshape.524
  (296 shorter events, 89.7 us)
Async XLA Ops:
  7.2 23.0 %copy-start.34 = (bf16[8,16,256]{2,1,0:T(8,128)(2,1)S(1)}, bf16[8,16,256]{2,1,0:T(8,128)(2,1)}, u32[]{:S(2)}) copy-start(bf16[8,16,256]{2,1,0:T(8,128)(2,1)} %param.7) | copy-start | bytes 196612
  7.2 23.1 %copy-start.1 = (bf16[27,12288]{1,0:T(8,128)(2,1)S(1)}, bf16[27,12288]{1,0:T(8,128)(2,1)}, u32[]{:S(2)}) copy-start(bf16[27,12288]{1,0:T(8,128)(2,1)} %param.10) | copy-start | bytes 1990660
  7.2 809.9 %all-reduce.2.cloned.1.call-start = ((), (), s32[]{:S(2)}) async-start(), calls=%async_computation | async-start | bytes 3538944 | tf_op jit(solution)/shard_map/psum | solution.py:152
  8.4 75.9 %collective-permute-start.24 = (bf16[64,1,16,4]{0,3,2,1:T(4,128)(2,1)S(1)}, bf16[64,1,16,4]{0,3,2,1:T(4,128)(2,1)S(1)}, u32[]{:S(2)}, u32[]{:S(2)}) collective-permute-start(bf16[64,1,16,4]{0,3,2,1:T(4,128)(2,1)S(1)} %get-tuple-element.104), channel_id=1, source_target_pairs={{0,128},{128,256},{256,384},{384,0},{1,129},{129,257},{257,385},{3... | collective-permute-start | bytes 24584 | tf_op jit(solution)/shard_map/ppermute | solution.py:22
  13.0 73.2 %collective-permute-start.25 = (bf16[64,1,16,4]{0,3,2,1:T(4,128)(2,1)S(1)}, bf16[64,1,16,4]{0,3,2,1:T(4,128)(2,1)S(1)}, u32[]{:S(2)}, u32[]{:S(2)}) collective-permute-start(bf16[64,1,16,4]{0,3,2,1:T(4,128)(2,1)S(1)} %get-tuple-element.105), channel_id=1, source_target_pairs={{128,0},{256,128},{384,256},{0,384},{129,1},{257,129},{385,257},{1... | collective-permute-start | bytes 24584 | tf_op jit(solution)/shard_map/ppermute | solution.py:23
  19.9 11.7 %collective-permute-start = (bf16[3,1,16,4]{2,3,1,0:T(4,128)(2,1)S(1)}, bf16[3,1,16,4]{2,3,1,0:T(4,128)(2,1)S(1)}, u32[]{:S(2)}, u32[]{:S(2)}) collective-permute-start(bf16[3,1,16,4]{2,3,1,0:T(4,128)(2,1)S(1)} %get-tuple-element.153), channel_id=1, source_target_pairs={{0,128},{128,256},{256,384},{384,0},{1,129},{129,257},{257,385},{3... | collective-permute-start | bytes 1160 | tf_op jit(solution)/shard_map/ppermute | solution.py:22
  21.8 9.9 %collective-permute-start.1 = (bf16[3,1,16,4]{2,3,1,0:T(4,128)(2,1)S(1)}, bf16[3,1,16,4]{2,3,1,0:T(4,128)(2,1)S(1)}, u32[]{:S(2)}, u32[]{:S(2)}) collective-permute-start(bf16[3,1,16,4]{2,3,1,0:T(4,128)(2,1)S(1)} %get-tuple-element.152), channel_id=1, source_target_pairs={{128,0},{256,128},{384,256},{0,384},{129,1},{257,129},{385,257},{1... | collective-permute-start | bytes 1160 | tf_op jit(solution)/shard_map/ppermute | solution.py:23
  26.1 45.9 %collective-permute-start.12 = (bf16[128,1,8,2]{0,2,3,1:T(8,128)(2,1)S(1)}, bf16[128,1,8,2]{0,2,3,1:T(8,128)(2,1)S(1)}, u32[]{:S(2)}, u32[]{:S(2)}) collective-permute-start(bf16[128,1,8,2]{0,2,3,1:T(8,128)(2,1)S(1)} %get-tuple-element.154), channel_id=1, source_target_pairs={{0,128},{128,256},{256,384},{384,0},{1,129},{129,257},{257,385},{3... | collective-permute-start | bytes 12296 | tf_op jit(solution)/shard_map/ppermute | solution.py:22
  29.2 41.6 %copy-start.28 = (bf16[3,512]{1,0:T(4,128)(2,1)}, bf16[3,512]{1,0:T(4,128)(2,1)S(1)}, u32[]{:S(2)}) copy-start(bf16[3,512]{1,0:T(4,128)(2,1)S(1)} %reshape.434) | copy-start | bytes 9220
  29.3 42.4 %copy-start.18 = (f32[64,512]{1,0:T(8,128)}, f32[64,512]{1,0:T(8,128)S(1)}, u32[]{:S(2)}) copy-start(f32[64,512]{1,0:T(8,128)S(1)} %copy.204) | copy-start | bytes 393220
  31.8 7.3 collective-permute-start.2
  33.7 5.6 collective-permute-start.3
  39.4 16.2 %collective-permute-start.4 = (bf16[3,10,18,1]{2,3,1,0:T(2,128)(2,1)S(1)}, bf16[3,10,18,1]{2,3,1,0:T(2,128)(2,1)S(1)}, u32[]{:S(2)}, u32[]{:S(2)}) collective-permute-start(bf16[3,10,18,1]{2,3,1,0:T(2,128)(2,1)S(1)} %get-tuple-element.144), channel_id=1, source_target_pairs={{1,0},{2,1},{3,2},{4,3},{5,4},{6,5},{7,6},{8,7},{9,8},{10,9},{11,1... | collective-permute-start | bytes 3248 | tf_op jit(solution)/shard_map/ppermute | solution.py:23
  51.1 8.1 collective-permute-start.5
  55.7 16.4 %collective-permute-start.13 = (bf16[128,1,8,2]{0,2,3,1:T(8,128)(2,1)S(1)}, bf16[128,1,8,2]{0,2,3,1:T(8,128)(2,1)S(1)}, u32[]{:S(2)}, u32[]{:S(2)}) collective-permute-start(bf16[128,1,8,2]{0,2,3,1:T(8,128)(2,1)S(1)} %get-tuple-element.155), channel_id=1, source_target_pairs={{128,0},{256,128},{384,256},{0,384},{129,1},{257,129},{385,257},{1... | collective-permute-start | bytes 12296 | tf_op jit(solution)/shard_map/ppermute | solution.py:23
  59.1 29.9 %collective-permute-start.18 = (bf16[64,1,16,4]{0,3,2,1:T(4,128)(2,1)S(1)}, bf16[64,1,16,4]{0,3,2,1:T(4,128)(2,1)S(1)}, u32[]{:S(2)}, u32[]{:S(2)}) collective-permute-start(bf16[64,1,16,4]{0,3,2,1:T(4,128)(2,1)S(1)} %get-tuple-element.106), channel_id=1, source_target_pairs={{0,128},{128,256},{256,384},{384,0},{1,129},{129,257},{257,385},{3... | collective-permute-start | bytes 24584 | tf_op jit(solution)/shard_map/ppermute | solution.py:22
  67.0 5.2 copy-start.25
  72.0 41.5 %copy-start.21 = (bf16[64,512]{1,0:T(8,128)(2,1)}, bf16[64,512]{1,0:T(8,128)(2,1)S(1)}, u32[]{:S(2)}) copy-start(bf16[64,512]{1,0:T(8,128)(2,1)S(1)} %fusion.2) | copy-start | bytes 196612
  72.1 6.5 collective-permute-start.14
  75.3 5.8 collective-permute-start.15
  78.7 17.4 %collective-permute-start.19 = (bf16[64,1,16,4]{0,3,2,1:T(4,128)(2,1)S(1)}, bf16[64,1,16,4]{0,3,2,1:T(4,128)(2,1)S(1)}, u32[]{:S(2)}, u32[]{:S(2)}) collective-permute-start(bf16[64,1,16,4]{0,3,2,1:T(4,128)(2,1)S(1)} %get-tuple-element.107), channel_id=1, source_target_pairs={{128,0},{256,128},{384,256},{0,384},{129,1},{257,129},{385,257},{1... | collective-permute-start | bytes 24584 | tf_op jit(solution)/shard_map/ppermute | solution.py:23
  81.1 17.0 %collective-permute-start.6 = (bf16[64,1,16,4]{0,3,2,1:T(4,128)(2,1)S(1)}, bf16[64,1,16,4]{0,3,2,1:T(4,128)(2,1)S(1)}, u32[]{:S(2)}, u32[]{:S(2)}) collective-permute-start(bf16[64,1,16,4]{0,3,2,1:T(4,128)(2,1)S(1)} %get-tuple-element.110), channel_id=1, source_target_pairs={{0,128},{128,256},{256,384},{384,0},{1,129},{129,257},{257,385},{3... | collective-permute-start | bytes 24584 | tf_op jit(solution)/shard_map/ppermute | solution.py:22
  84.4 18.3 %collective-permute-start.7 = (bf16[64,1,16,4]{0,3,2,1:T(4,128)(2,1)S(1)}, bf16[64,1,16,4]{0,3,2,1:T(4,128)(2,1)S(1)}, u32[]{:S(2)}, u32[]{:S(2)}) collective-permute-start(bf16[64,1,16,4]{0,3,2,1:T(4,128)(2,1)S(1)} %get-tuple-element.111), channel_id=1, source_target_pairs={{128,0},{256,128},{384,256},{0,384},{129,1},{257,129},{385,257},{1... | collective-permute-start | bytes 24584 | tf_op jit(solution)/shard_map/ppermute | solution.py:23
  86.3 49.3 %collective-permute-start.16 = (bf16[128,6,10,1]{0,2,3,1:T(8,128)(2,1)S(1)}, bf16[128,6,10,1]{0,2,3,1:T(8,128)(2,1)S(1)}, u32[]{:S(2)}, u32[]{:S(2)}) collective-permute-start(bf16[128,6,10,1]{0,2,3,1:T(8,128)(2,1)S(1)} %get-tuple-element.138), channel_id=1, source_target_pairs={{0,1},{1,2},{2,3},{3,4},{4,5},{5,6},{6,7},{7,8},{8,9},{9,10},{10,1... | collective-permute-start | bytes 46088 | tf_op jit(solution)/shard_map/ppermute | solution.py:22
  89.1 53.4 %collective-permute-start.17 = (bf16[128,6,10,1]{0,2,3,1:T(8,128)(2,1)S(1)}, bf16[128,6,10,1]{0,2,3,1:T(8,128)(2,1)S(1)}, u32[]{:S(2)}, u32[]{:S(2)}) collective-permute-start(bf16[128,6,10,1]{0,2,3,1:T(8,128)(2,1)S(1)} %get-tuple-element.139), channel_id=1, source_target_pairs={{1,0},{2,1},{3,2},{4,3},{5,4},{6,5},{7,6},{8,7},{9,8},{10,9},{11,1... | collective-permute-start | bytes 46088 | tf_op jit(solution)/shard_map/ppermute | solution.py:23
  96.1 9.4 %collective-permute-start.26 = (bf16[64,10,1,4]{0,3,2,1:T(4,128)(2,1)S(1)}, bf16[64,10,1,4]{0,3,2,1:T(4,128)(2,1)S(1)}, u32[]{:S(2)}, u32[]{:S(2)}) collective-permute-start(bf16[64,10,1,4]{0,3,2,1:T(4,128)(2,1)S(1)} %get-tuple-element.94), channel_id=1, source_target_pairs={{0,32},{32,64},{64,96},{96,0},{1,33},{33,65},{65,97},{97,1},{2,34}... | collective-permute-start | bytes 15368 | tf_op jit(solution)/shard_map/ppermute | solution.py:22
  98.1 12.0 %collective-permute-start.27 = (bf16[64,10,1,4]{0,3,2,1:T(4,128)(2,1)S(1)}, bf16[64,10,1,4]{0,3,2,1:T(4,128)(2,1)S(1)}, u32[]{:S(2)}, u32[]{:S(2)}) collective-permute-start(bf16[64,10,1,4]{0,3,2,1:T(4,128)(2,1)S(1)} %get-tuple-element.95), channel_id=1, source_target_pairs={{32,0},{64,32},{96,64},{0,96},{33,1},{65,33},{97,65},{1,97},{34,2}... | collective-permute-start | bytes 15368 | tf_op jit(solution)/shard_map/ppermute | solution.py:23
  102.6 30.5 %copy-start.19 = (bf16[64,1,16,4]{0,3,2,1:T(4,128)(2,1)}, bf16[64,1,16,4]{0,3,2,1:T(4,128)(2,1)S(1)}, u32[]{:S(2)}) copy-start(bf16[64,1,16,4]{0,3,2,1:T(4,128)(2,1)S(1)} %collective-permute-done.7) | copy-start | bytes 24580
  102.7 11.2 %collective-permute-start.20 = (bf16[64,10,1,4]{0,3,2,1:T(4,128)(2,1)S(1)}, bf16[64,10,1,4]{0,3,2,1:T(4,128)(2,1)S(1)}, u32[]{:S(2)}, u32[]{:S(2)}) collective-permute-start(bf16[64,10,1,4]{0,3,2,1:T(4,128)(2,1)S(1)} %get-tuple-element.96), channel_id=1, source_target_pairs={{0,32},{32,64},{64,96},{96,0},{1,33},{33,65},{65,97},{97,1},{2,34}... | collective-permute-start | bytes 15368 | tf_op jit(solution)/shard_map/ppermute | solution.py:22
  105.4 13.0 %collective-permute-start.21 = (bf16[64,10,1,4]{0,3,2,1:T(4,128)(2,1)S(1)}, bf16[64,10,1,4]{0,3,2,1:T(4,128)(2,1)S(1)}, u32[]{:S(2)}, u32[]{:S(2)}) collective-permute-start(bf16[64,10,1,4]{0,3,2,1:T(4,128)(2,1)S(1)} %get-tuple-element.97), channel_id=1, source_target_pairs={{32,0},{64,32},{96,64},{0,96},{33,1},{65,33},{97,65},{1,97},{34,2}... | collective-permute-start | bytes 15368 | tf_op jit(solution)/shard_map/ppermute | solution.py:23
  110.0 12.1 %collective-permute-start.8 = (bf16[64,10,1,4]{0,3,2,1:T(4,128)(2,1)S(1)}, bf16[64,10,1,4]{0,3,2,1:T(4,128)(2,1)S(1)}, u32[]{:S(2)}, u32[]{:S(2)}) collective-permute-start(bf16[64,10,1,4]{0,3,2,1:T(4,128)(2,1)S(1)} %get-tuple-element.100), channel_id=1, source_target_pairs={{0,32},{32,64},{64,96},{96,0},{1,33},{33,65},{65,97},{97,1},{2,34}... | collective-permute-start | bytes 15368 | tf_op jit(solution)/shard_map/ppermute | solution.py:22
  113.9 15.3 %collective-permute-start.9 = (bf16[64,10,1,4]{0,3,2,1:T(4,128)(2,1)S(1)}, bf16[64,10,1,4]{0,3,2,1:T(4,128)(2,1)S(1)}, u32[]{:S(2)}, u32[]{:S(2)}) collective-permute-start(bf16[64,10,1,4]{0,3,2,1:T(4,128)(2,1)S(1)} %get-tuple-element.101), channel_id=1, source_target_pairs={{32,0},{64,32},{96,64},{0,96},{33,1},{65,33},{97,65},{1,97},{34,2}... | collective-permute-start | bytes 15368 | tf_op jit(solution)/shard_map/ppermute | solution.py:23
  118.4 36.4 %collective-permute-start.28 = (bf16[64,10,18,1]{0,3,2,1:T(2,128)(2,1)S(1)}, bf16[64,10,18,1]{0,3,2,1:T(2,128)(2,1)S(1)}, u32[]{:S(2)}, u32[]{:S(2)}) collective-permute-start(bf16[64,10,18,1]{0,3,2,1:T(2,128)(2,1)S(1)} %get-tuple-element.73), channel_id=1, source_target_pairs={{0,1},{1,2},{2,3},{3,4},{4,5},{5,6},{6,7},{7,8},{8,9},{9,10},{10,1... | collective-permute-start | bytes 69128 | tf_op jit(solution)/shard_map/ppermute | solution.py:22
  122.1 12.7 %copy-start.30 = (bf16[64,10,1,4]{0,3,2,1:T(4,128)(2,1)}, bf16[64,10,1,4]{0,3,2,1:T(4,128)(2,1)S(1)}, u32[]{:S(2)}) copy-start(bf16[64,10,1,4]{0,3,2,1:T(4,128)(2,1)S(1)} %collective-permute-done.8) | copy-start | bytes 15364
  122.1 32.7 %collective-permute-start.29 = (bf16[64,10,18,1]{0,3,2,1:T(2,128)(2,1)S(1)}, bf16[64,10,18,1]{0,3,2,1:T(2,128)(2,1)S(1)}, u32[]{:S(2)}, u32[]{:S(2)}) collective-permute-start(bf16[64,10,18,1]{0,3,2,1:T(2,128)(2,1)S(1)} %get-tuple-element.72), channel_id=1, source_target_pairs={{1,0},{2,1},{3,2},{4,3},{5,4},{6,5},{7,6},{8,7},{9,8},{10,9},{11,1... | collective-permute-start | bytes 69128 | tf_op jit(solution)/shard_map/ppermute | solution.py:23
  129.1 5.7 copy-start.32
  129.1 16.0 %collective-permute-start.22 = (bf16[64,10,18,1]{0,3,2,1:T(2,128)(2,1)S(1)}, bf16[64,10,18,1]{0,3,2,1:T(2,128)(2,1)S(1)}, u32[]{:S(2)}, u32[]{:S(2)}) collective-permute-start(bf16[64,10,18,1]{0,3,2,1:T(2,128)(2,1)S(1)} %get-tuple-element.74), channel_id=1, source_target_pairs={{0,1},{1,2},{2,3},{3,4},{4,5},{5,6},{6,7},{7,8},{8,9},{9,10},{10,1... | collective-permute-start | bytes 69128 | tf_op jit(solution)/shard_map/ppermute | solution.py:22
  135.6 13.0 %collective-permute-start.23 = (bf16[64,10,18,1]{0,3,2,1:T(2,128)(2,1)S(1)}, bf16[64,10,18,1]{0,3,2,1:T(2,128)(2,1)S(1)}, u32[]{:S(2)}, u32[]{:S(2)}) collective-permute-start(bf16[64,10,18,1]{0,3,2,1:T(2,128)(2,1)S(1)} %get-tuple-element.75), channel_id=1, source_target_pairs={{1,0},{2,1},{3,2},{4,3},{5,4},{6,5},{7,6},{8,7},{9,8},{10,9},{11,1... | collective-permute-start | bytes 69128 | tf_op jit(solution)/shard_map/ppermute | solution.py:23
  142.5 210.0 %collective-permute-start.10 = (bf16[64,10,18,1]{0,3,2,1:T(2,128)(2,1)}, bf16[64,10,18,1]{0,3,2,1:T(2,128)(2,1)}, u32[]{:S(2)}, u32[]{:S(2)}) collective-permute-start(bf16[64,10,18,1]{0,3,2,1:T(2,128)(2,1)} %get-tuple-element.79), channel_id=1, source_target_pairs={{1,0},{2,1},{3,2},{4,3},{5,4},{6,5},{7,6},{8,7},{9,8},{10,9},{11,1... | collective-permute-start | bytes 69128 | tf_op jit(solution)/shard_map/ppermute | solution.py:23
  145.1 207.4 %collective-permute-start.11 = (bf16[64,10,18,1]{0,3,2,1:T(2,128)(2,1)}, bf16[64,10,18,1]{0,3,2,1:T(2,128)(2,1)}, u32[]{:S(2)}, u32[]{:S(2)}) collective-permute-start(bf16[64,10,18,1]{0,3,2,1:T(2,128)(2,1)} %get-tuple-element.78), channel_id=1, source_target_pairs={{0,1},{1,2},{2,3},{3,4},{4,5},{5,6},{6,7},{7,8},{8,9},{9,10},{10,1... | collective-permute-start | bytes 69128 | tf_op jit(solution)/shard_map/ppermute | solution.py:22
  155.3 2.1 copy-start.15
  157.4 1.5 copy-start.29
  159.1 15.8 %copy-start.24 = (bf16[64,512]{1,0:T(8,128)(2,1)S(1)}, bf16[64,512]{1,0:T(8,128)(2,1)}, u32[]{:S(2)}) copy-start(bf16[64,512]{1,0:T(8,128)(2,1)} %copy.236) | copy-start | bytes 196612
  160.9 15.9 %copy-start.14 = (bf16[64,8,16,4]{0,3,2,1:T(4,128)(2,1)S(1)}, bf16[64,8,16,4]{0,3,2,1:T(4,128)(2,1)}, u32[]{:S(2)}) copy-start(bf16[64,8,16,4]{0,3,2,1:T(4,128)(2,1)} %get-tuple-element.175) | copy-start | bytes 196612
  178.2 111.5 %copy-start.22 = (bf16[64,512]{1,0:T(8,128)(2,1)S(1)}, bf16[64,512]{1,0:T(8,128)(2,1)}, u32[]{:S(2)}) copy-start(bf16[64,512]{1,0:T(8,128)(2,1)} %copy-done.21) | copy-start | bytes 196612
  286.1 7.6 copy-start.8
  289.7 6.6 copy-start.7
  294.5 6.7 copy-start.6
  297.3 6.7 copy-start.5
  302.1 5.1 copy-start.2
  308.0 7.6 copy-start.4
  309.9 6.6 copy-start.3
  343.9 7.1 copy-start.10
  346.0 5.0 copy-start.9
  347.8 3.2 copy-start.11
  347.8 3.3 copy-start.12
  348.9 2.3 copy-start.13
  349.9 1.3 copy-start.26
  351.1 1.4 copy-start.20
  351.1 1.4 copy-start.31
  351.1 1.4 copy-start.33
  355.1 8.4 %copy-start.23 = (bf16[64,512]{1,0:T(8,128)(2,1)S(1)}, bf16[64,512]{1,0:T(8,128)(2,1)}, u32[]{:S(2)}) copy-start(bf16[64,512]{1,0:T(8,128)(2,1)} %copy-done.21) | copy-start | bytes 196612
  366.5 1.4 copy-start.16
  366.5 1.4 copy-start.17
  (2 other events, 2.4 us)
Sparse Core Ops, SparseCore 0:
  352.6 464.3 all-reduce.1
where the time goes:
time: 830 us; the launch traced here: 827 us
  waiting for transfers between devices  446 us (54%)
  local copies, waits for them, and re-layouts  122 us (15%)
  starting transfers between devices  110 us (13%)
  blocking collectives  105 us (13%)
  matrix products  17.9 us (2%)
  between operations  15.4 us (2%)
  other arithmetic  10.2 us (1%)
    psum x1, waiting for transfers between devices, per_device(): lax.psum((body_grad, head_grad), ('gx', 'gy', 'gz'))  445 us
    psum x1, blocking collectives, per_device(): lax.psum((body_grad, head_grad), ('gx', 'gy', 'gz'))  105 us
    ppermute x15, starting transfers between devices, extended(): after = lax.ppermute(first, axis, down)  72.8 us
    reshape x70, local copies, waits for them, and re-layouts, window_at(): return cut_piece.reshape(padded.shape[0], size_x * size_y * size_z)  55.2 us
    ppermute x15, starting transfers between devices, extended(): before = lax.ppermute(last, axis, up)  37.4 us
    slice x35, local copies, waits for them, and re-layouts, window_at(): padded[:, 1 + shift_x:1 + shift_x + size_x, 1 + shift_y:1 + shift_y + siz...  19.5 us
    unnamed x96, local copies, waits for them, and re-layouts  16.8 us
  transfers between devices with their start and end apart: 31, of which 3 were waited for; matrix products, arithmetic and copies ran while one was open for 18% of the time, Pallas kernels for 0%

commit v1 on v0

--- a/solution.py
+++ b/solution.py
@@ -92,8 +92,34 @@
     return extended(grid_field, (("gx", 1), ("gy", 2), ("gz", 3)), 1)
 
 
-def input_rims(grid_field):
-    return extended(grid_field, (("gx", 1), ("gy", 2), ("gz", 3)), 1)
+def packed_parts(body_grad, head_grad, parts, rows):
+    body = body_grad.reshape(parts, -1)
+    head = head_grad.reshape(parts, -1)
+    room = rows * 128 - body.shape[1] - head.shape[1]
+    flat = jnp.concatenate([body, head, jnp.zeros((parts, room), jnp.float32)], axis=1)
+    return flat.reshape(parts, rows, 128)
+
+
+def sum_everywhere(body_grad, head_grad):
+    plane = ("gx", "gy")
+    parts = lax.axis_size("gx") * lax.axis_size("gy")
+    deep = lax.axis_size("gz")
+    per_part = (body_grad.size + head_grad.size) // parts
+    rows = -(-per_part // (128 * deep)) * deep
+    packed = packed_parts(body_grad, head_grad, parts, rows).astype(jnp.bfloat16)
+    traded = lax.all_to_all(packed, plane, 0, 0)
+    mine = jnp.sum(traded.astype(jnp.float32), axis=0)
+    deep_parts = mine.reshape(deep, rows // deep, 128)
+    deep_traded = lax.all_to_all(deep_parts, "gz", 0, 0)
+    total = jnp.sum(deep_traded, axis=0).astype(jnp.bfloat16)
+    column = lax.all_gather(total, "gz", axis=0, tiled=True)
+    full = lax.all_gather(column, plane, axis=0)
+    flat = full.reshape(parts, rows * 128).astype(jnp.float32)
+    body_part = body_grad.size // parts
+    head_part = head_grad.size // parts
+    body = flat[:, :body_part].reshape(body_grad.shape)
+    head = flat[:, body_part : body_part + head_part].reshape(head_grad.shape)
+    return body, head
 
 
 def per_device(coarse, skip_features, pre_act, cotangent, weight_one, weight_out):
@@ -115,17 +141,12 @@
         [stacked_taps(rim_cot, -1, shift_x, grid_shape) for shift_x in (-1, 0, 1)], axis=0
     )
     d_hidden = contract_rows(weight_out.reshape(tap_count * vel_channels, hid_channels), cot_back)
-    rim_hidden = input_rims(hidden.reshape(hid_channels, *grid_shape))
-    cot_flat = cotangent.reshape(vel_channels, cell_count)
-    head_parts = []
-    for shift_x in (-1, 0, 1):
-        shifted = stacked_taps(rim_hidden, 1, shift_x, grid_shape)
-        partial_value = contract_cells(cot_flat, shifted).reshape(vel_channels, 9, hid_channels)
-        head_parts.append(jnp.transpose(partial_value, (1, 0, 2)))
-    head_grad = jnp.concatenate(head_parts, axis=0)
+    head_grad = contract_cells(cot_back, hidden).reshape(tap_count, vel_channels, hid_channels)
     d_pre = (d_hidden * gelu_slope(pre_float)).astype(jnp.bfloat16)
     rim_pre = grad_rims(d_pre.reshape(hid_channels, *grid_shape))
     d_input = jnp.zeros((in_channels, cell_count), jnp.float32)
+    fine_coarse = upsample(coarse)
+    inputs = jnp.concatenate([fine_coarse, skip_features], axis=0).reshape(in_channels, cell_count)
     body_parts = []
     for group_index, shift_x in enumerate((-1, 0, 1)):
         pre_back = stacked_taps(rim_pre, -1, shift_x, grid_shape)
@@ -133,23 +154,11 @@
             9 * hid_channels, in_channels
         )
         d_input = d_input + contract_rows(tap_rows, pre_back)
-    rim_coarse = extended(coarse, (("gx", 1), ("gy", 2), ("gz", 3)), 1)
-    fine_coarse = upsample(rim_coarse)[:, 1:-1, 1:-1, 1:-1]
-    rim_skip = input_rims(skip_features)
-    rim_inputs = jnp.concatenate([fine_coarse, rim_skip], axis=0)
-    for shift_x in (-1, 0, 1):
-        for shift_y in (-1, 0, 1):
-            shifted = jnp.concatenate(
-                [
-                    window_at(rim_inputs, shift_x, shift_y, shift_z, grid_shape)
-                    for shift_z in (-1, 0, 1)
-                ],
-                axis=0,
-            )
-            partial_value = contract_cells(d_pre, shifted).reshape(hid_channels, 3, in_channels)
-            body_parts.append(jnp.transpose(partial_value, (1, 0, 2)))
+        body_parts.append(
+            contract_cells(pre_back, inputs).reshape(9, hid_channels, in_channels)
+        )
     body_grad = jnp.concatenate(body_parts, axis=0)
-    summed_body, summed_head = lax.psum((body_grad, head_grad), ("gx", "gy", "gz"))
+    summed_body, summed_head = sum_everywhere(body_grad, head_grad)
     total_cells = cell_count * lax.axis_size("gx") * lax.axis_size("gy") * lax.axis_size("gz")
     norm_factor = 1.0 / math.sqrt(total_cells)
     size_x, size_y, size_z = grid_shape

time: 830 us -> 250 us (0.30)
  waiting for transfers between devices: 446 us -> 23.4 us
  local copies, waits for them, and re-layouts: 122 us -> 48.3 us
  starting transfers between devices: 110 us -> 64.5 us
  between operations: 15.4 us -> 1.35 us
  matrix products: 17.9 us -> 5.04 us
    psum x1 -> x0, waiting for transfers between devices: 445 us -> none  [per_device(): lax.psum((body_grad, head_grad), ('gx', 'gy', 'gz'))]
    psum x1 -> x0, blocking collectives: 105 us -> none  [per_device(): lax.psum((body_grad, head_grad), ('gx', 'gy', 'gz'))]
    all_gather x0 -> x2, blocking collectives: none -> 104 us  [the longest x1 57.2 us: sum_everywhere(): column = lax.all_gather(total, 'gz', axis=0, tiled=True)]
    reshape x70 -> x35, local copies, waits for them, and re-layouts: 55.2 us -> 11 us  [window_at(): return cut_piece.reshape(padded.shape[0], size_x * size_y * size_z)]
    ppermute x15 -> x6, starting transfers between devices: 72.8 us -> 33.3 us  [extended(): after = lax.ppermute(first, axis, down)]
    ppermute x15 -> x6, starting transfers between devices: 37.4 us -> 17.4 us  [extended(): before = lax.ppermute(last, axis, up)]
    all_to_all x0 -> x2, waiting for transfers between devices: none -> 19.2 us  [the longest x1 13.5 us: sum_everywhere(): deep_traded = lax.all_to_all(deep_parts, 'gz', 0, 0)]
    reshape x13 -> x2, local copies, waits for them, and re-layouts: 16 us -> 1.64 us  [the longest x1 0.97 us: packed_parts(): body = body_grad.reshape(parts, -1)]
  transfers between devices with their start and end apart: 31 -> 14, of which waited for: 3 -> 5; matrix products, arithmetic and copies ran while one was open for 18% -> 9% of each run, Pallas kernels for 0% -> 0%
where the time goes in v1:
time: 250 us; the launch traced here: 248 us
  blocking collectives  104 us (42%)
  starting transfers between devices  64.5 us (26%)
  local copies, waits for them, and re-layouts  48.3 us (19%)
  waiting for transfers between devices  23.4 us (9%)
  matrix products  5.04 us (2%)
    all_gather x1, blocking collectives, sum_everywhere(): column = lax.all_gather(total, 'gz', axis=0, tiled=True)  57.2 us
    all_gather x1, blocking collectives, sum_everywhere(): full = lax.all_gather(column, plane, axis=0)  46.5 us
    ppermute x6, starting transfers between devices, extended(): after = lax.ppermute(first, axis, down)  33.3 us
    ppermute x6, starting transfers between devices, extended(): before = lax.ppermute(last, axis, up)  17.4 us
    all_to_all x1, waiting for transfers between devices, sum_everywhere(): deep_traded = lax.all_to_all(deep_parts, 'gz', 0, 0)  13.5 us
    reshape x35, local copies, waits for them, and re-layouts, window_at(): return cut_piece.reshape(padded.shape[0], size_x * size_y * size_z)  11 us
    slice x31, local copies, waits for them, and re-layouts, window_at(): padded[:, 1 + shift_x:1 + shift_x + size_x, 1 + shift_y:1 + shift_y + siz...  9.74 us
    unnamed x34, local copies, waits for them, and re-layouts  7.32 us
  transfers between devices with their start and end apart: 14, of which 5 were waited for; matrix products, arithmetic and copies ran while one was open for 9% of the time, Pallas kernels for 0%

profile of v1, /device:TPU:1, one launch (start us, length us, event | category | flops | bytes accessed | tf_op | source)
XLA Modules:
  0.0 248.4 jit_solution(15972002548728710920)
XLA Ops:
  0.6 0.8 fusion.23
  1.4 4.6 %collective-permute-start = (bf16[3,1,16,4]{2,3,1,0:T(4,128)(2,1)S(1)}, bf16[3,1,16,4]{2,3,1,0:T(4,128)(2,1)S(1)}, u32[]{:S(2)}, u32[]{:S(2)}) collective-permute-start(bf16[3,1,16,4]{2,3,1,0:T(4,128)(2,1)S(1)} %get-tuple-element.88), channel_id=1, source_target_pairs={{0,128},{128,256},{256,384},{384,0},{1,129},{129,257},{257,385},{3... | collective-permute-start | bytes 1160 | tf_op jit(solution)/shard_map/ppermute | solution.py:22
  6.0 6.1 %collective-permute-start.1 = (bf16[3,1,16,4]{2,3,1,0:T(4,128)(2,1)S(1)}, bf16[3,1,16,4]{2,3,1,0:T(4,128)(2,1)S(1)}, u32[]{:S(2)}, u32[]{:S(2)}) collective-permute-start(bf16[3,1,16,4]{2,3,1,0:T(4,128)(2,1)S(1)} %get-tuple-element.87), channel_id=1, source_target_pairs={{128,0},{256,128},{384,256},{0,384},{129,1},{257,129},{385,257},{1... | collective-permute-start | bytes 1160 | tf_op jit(solution)/shard_map/ppermute | solution.py:23
  12.1 1.0 copy.78
  13.3 0.8 copy.92
  14.0 1.0 reshape.326
  15.2 1.0 reshape.318
  16.1 0.7 copy.111
  16.8 0.7 copy.109
  17.8 0.8 copy.110
  18.7 1.9 collective-permute-start.3
  20.6 3.4 %collective-permute-start.2 = (bf16[3,10,1,4]{2,3,1,0:T(4,128)(2,1)S(1)}, bf16[3,10,1,4]{2,3,1,0:T(4,128)(2,1)S(1)}, u32[]{:S(2)}, u32[]{:S(2)}) collective-permute-start(bf16[3,10,1,4]{2,3,1,0:T(4,128)(2,1)S(1)} %get-tuple-element.82), channel_id=1, source_target_pairs={{0,32},{32,64},{64,96},{96,0},{1,33},{33,65},{65,97},{97,1},{2,34}... | collective-permute-start | bytes 728 | tf_op jit(solution)/shard_map/ppermute | solution.py:22
  24.8 1.6 collective-permute-done.2
  26.6 1.9 collective-permute-start.5
  28.5 11.7 %collective-permute-start.4 = (bf16[3,10,18,1]{2,3,1,0:T(2,128)(2,1)S(1)}, bf16[3,10,18,1]{2,3,1,0:T(2,128)(2,1)S(1)}, u32[]{:S(2)}, u32[]{:S(2)}) collective-permute-start(bf16[3,10,18,1]{2,3,1,0:T(2,128)(2,1)S(1)} %get-tuple-element.81), channel_id=1, source_target_pairs={{1,0},{2,1},{3,2},{4,3},{5,4},{6,5},{7,6},{8,7},{9,8},{10,9},{11,1... | collective-permute-start | bytes 3248 | tf_op jit(solution)/shard_map/ppermute | solution.py:23
  50.8 0.9 concatenate.126
  52.1 4.5 %collective-permute-start.7 = (bf16[64,1,16,4]{0,3,2,1:T(4,128)(2,1)S(1)}, bf16[64,1,16,4]{0,3,2,1:T(4,128)(2,1)S(1)}, u32[]{:S(2)}, u32[]{:S(2)}) collective-permute-start(bf16[64,1,16,4]{0,3,2,1:T(4,128)(2,1)S(1)} %get-tuple-element.50), channel_id=1, source_target_pairs={{128,0},{256,128},{384,256},{0,384},{129,1},{257,129},{385,257},{1... | collective-permute-start | bytes 24584 | tf_op jit(solution)/shard_map/ppermute | solution.py:23
  56.6 2.2 collective-permute-start.6
  59.2 0.4 collective-permute-done.6
  59.7 1.9 collective-permute-start.9
  61.6 3.4 %collective-permute-start.8 = (bf16[64,10,1,4]{0,3,2,1:T(4,128)(2,1)S(1)}, bf16[64,10,1,4]{0,3,2,1:T(4,128)(2,1)S(1)}, u32[]{:S(2)}, u32[]{:S(2)}) collective-permute-start(bf16[64,10,1,4]{0,3,2,1:T(4,128)(2,1)S(1)} %get-tuple-element.45), channel_id=1, source_target_pairs={{0,32},{32,64},{64,96},{96,0},{1,33},{33,65},{65,97},{97,1},{2,34}... | collective-permute-start | bytes 15368 | tf_op jit(solution)/shard_map/ppermute | solution.py:22
  65.1 2.1 collective-permute-done.8
  67.6 1.9 collective-permute-start.11
  69.5 7.2 %collective-permute-start.10 = (bf16[64,10,18,1]{0,3,2,1:T(2,128)(2,1)S(1)}, bf16[64,10,18,1]{0,3,2,1:T(2,128)(2,1)S(1)}, u32[]{:S(2)}, u32[]{:S(2)}) collective-permute-start(bf16[64,10,18,1]{0,3,2,1:T(2,128)(2,1)S(1)} %get-tuple-element.36), channel_id=1, source_target_pairs={{1,0},{2,1},{3,2},{4,3},{5,4},{6,5},{7,6},{8,7},{9,8},{10,9},{11,1... | collective-permute-start | bytes 69128 | tf_op jit(solution)/shard_map/ppermute | solution.py:23
  77.1 0.8 fusion.16
  77.9 0.7 copy.99
  78.7 0.7 copy.104
  79.4 0.5 maximum_maximum_fusion
  79.9 1.1 fusion.14
  81.0 1.1 fusion.13
  82.1 1.0 copy.100
  83.1 1.0 copy.101
  84.1 0.8 constant_dynamic-update-slice_fusion.10
  85.0 1.6 copy.102
  86.6 0.7 copy.103
  87.3 0.7 copy.105
  88.1 1.3 concatenate.137
  89.6 0.8 constant_dynamic-update-slice_fusion.6
  90.5 0.8 constant_dynamic-update-slice_fusion.5
  91.3 0.8 constant_dynamic-update-slice_fusion.4
  92.2 1.0 convolution_convert_fusion
  93.2 1.1 convolution_convert_fusion.1
  94.3 0.5 concatenate.134
  95.4 0.4 copy-done.4
  96.0 1.0 reshape.319
  97.3 1.0 copy.116
  98.4 7.1 %all-to-all-start = ((bf16[16,192,128]{2,1,0:T(8,128)(2,1)}), bf16[16,192,128]{2,1,0:T(8,128)(2,1)S(1)}, u32[]{:S(2)}, u32[]{:S(2)}) async-start(bf16[16,192,128]{2,1,0:T(8,128)(2,1)} %bitcast.79), calls=%async_computation | async-start | bytes 1572864 | tf_op jit(solution)/shard_map/all_to_all | solution.py:110
  105.5 1.1 fusion.12
  106.6 1.4 reshape.301
  107.9 2.1 reshape.292
  110.0 1.1 reshape.311
  111.1 1.5 fusion.24
  112.6 5.7 %all-to-all-done = bf16[16,192,128]{2,1,0:T(8,128)(2,1)S(1)} async-done(((bf16[16,192,128]{2,1,0:T(8,128)(2,1)}), bf16[16,192,128]{2,1,0:T(8,128)(2,1)S(1)}, u32[]{:S(2)}, u32[]{:S(2)}) %all-to-all-start) | async-done | bytes 786464 | tf_op jit(solution)/shard_map/all_to_all | solution.py:110
  118.4 0.7 reshape.320
  119.1 6.7 %all-to-all-start.1 = ((f32[32,6,128]{2,1,0:T(8,128)}), f32[32,6,128]{2,1,0:T(8,128)S(1)}, u32[]{:S(2)}, u32[]{:S(2)}) async-start(f32[32,6,128]{2,1,0:T(8,128)} %reshape.320), calls=%async_computation.1 | async-start | bytes 262144 | tf_op jit(solution)/shard_map/all_to_all | solution.py:113
  125.8 0.4 convolution_add_fusion.1
  126.2 0.4 fusion
  126.9 0.6 reshape.313
  127.6 0.8 reshape.314
  128.4 13.5 %all-to-all-done.1 = f32[32,6,128]{2,1,0:T(8,128)S(1)} async-done(((f32[32,6,128]{2,1,0:T(8,128)}), f32[32,6,128]{2,1,0:T(8,128)S(1)}, u32[]{:S(2)}, u32[]{:S(2)}) %all-to-all-start.1) | async-done | bytes 98336 | tf_op jit(solution)/shard_map/all_to_all | solution.py:113
  142.0 57.2 %all-gather.1 = bf16[32,6,128]{2,1,0:T(8,128)(2,1)S(1)} all-gather(bf16[1,6,128]{2,1,0:T(8,128)(2,1)S(1)} %bitcast.178), channel_id=1, replica_groups=mesh['gx'=4,'gy'=4,'gz'=32] {'gz'}, dimensions={0}, use_global_device_ids=true | all-gather | bytes 50688 | tf_op jit(solution)/shard_map/all_gather | solution.py:115
  199.2 46.5 %all-gather = bf16[3072,128]{1,0:T(8,128)(2,1)S(1)} all-gather(bf16[192,128]{1,0:T(8,128)(2,1)S(1)} %reshape.331), channel_id=2, replica_groups=mesh['gx'=4,'gy'=4,'gz'=32] {'gx','gy'}, dimensions={0}, use_global_device_ids=true | all-gather | bytes 835584 | tf_op jit(solution)/shard_map/all_gather | solution.py:116
  246.1 1.5 mul.66
  247.7 0.6 copy.115
  (131 shorter events, 16.4 us)
Async XLA Ops:
  0.6 17.9 %copy-start.8 = (bf16[3,8,16,4]{2,3,1,0:T(4,128)(2,1)S(1)}, bf16[3,8,16,4]{2,3,1,0:T(4,128)(2,1)}, u32[]{:S(2)}) copy-start(bf16[3,8,16,4]{2,3,1,0:T(4,128)(2,1)} %param.9) | copy-start | bytes 9220
  1.4 17.1 %collective-permute-start = (bf16[3,1,16,4]{2,3,1,0:T(4,128)(2,1)S(1)}, bf16[3,1,16,4]{2,3,1,0:T(4,128)(2,1)S(1)}, u32[]{:S(2)}, u32[]{:S(2)}) collective-permute-start(bf16[3,1,16,4]{2,3,1,0:T(4,128)(2,1)S(1)} %get-tuple-element.88), channel_id=1, source_target_pairs={{0,128},{128,256},{256,384},{384,0},{1,129},{129,257},{257,385},{3... | collective-permute-start | bytes 1160 | tf_op jit(solution)/shard_map/ppermute | solution.py:22
  6.0 12.5 %collective-permute-start.1 = (bf16[3,1,16,4]{2,3,1,0:T(4,128)(2,1)S(1)}, bf16[3,1,16,4]{2,3,1,0:T(4,128)(2,1)S(1)}, u32[]{:S(2)}, u32[]{:S(2)}) collective-permute-start(bf16[3,1,16,4]{2,3,1,0:T(4,128)(2,1)S(1)} %get-tuple-element.87), channel_id=1, source_target_pairs={{128,0},{256,128},{384,256},{0,384},{129,1},{257,129},{385,257},{1... | collective-permute-start | bytes 1160 | tf_op jit(solution)/shard_map/ppermute | solution.py:23
  18.7 6.1 %collective-permute-start.3 = (bf16[3,10,1,4]{2,3,1,0:T(4,128)(2,1)S(1)}, bf16[3,10,1,4]{2,3,1,0:T(4,128)(2,1)S(1)}, u32[]{:S(2)}, u32[]{:S(2)}) collective-permute-start(bf16[3,10,1,4]{2,3,1,0:T(4,128)(2,1)S(1)} %get-tuple-element.83), channel_id=1, source_target_pairs={{32,0},{64,32},{96,64},{0,96},{33,1},{65,33},{97,65},{1,97},{34,2}... | collective-permute-start | bytes 728 | tf_op jit(solution)/shard_map/ppermute | solution.py:23
  20.6 5.8 %collective-permute-start.2 = (bf16[3,10,1,4]{2,3,1,0:T(4,128)(2,1)S(1)}, bf16[3,10,1,4]{2,3,1,0:T(4,128)(2,1)S(1)}, u32[]{:S(2)}, u32[]{:S(2)}) collective-permute-start(bf16[3,10,1,4]{2,3,1,0:T(4,128)(2,1)S(1)} %get-tuple-element.82), channel_id=1, source_target_pairs={{0,32},{32,64},{64,96},{96,0},{1,33},{33,65},{65,97},{97,1},{2,34}... | collective-permute-start | bytes 728 | tf_op jit(solution)/shard_map/ppermute | solution.py:22
  26.6 16.3 %collective-permute-start.5 = (bf16[3,10,18,1]{2,3,1,0:T(2,128)(2,1)S(1)}, bf16[3,10,18,1]{2,3,1,0:T(2,128)(2,1)S(1)}, u32[]{:S(2)}, u32[]{:S(2)}) collective-permute-start(bf16[3,10,18,1]{2,3,1,0:T(2,128)(2,1)S(1)} %get-tuple-element.80), channel_id=1, source_target_pairs={{0,1},{1,2},{2,3},{3,4},{4,5},{5,6},{6,7},{7,8},{8,9},{9,10},{10,1... | collective-permute-start | bytes 3248 | tf_op jit(solution)/shard_map/ppermute | solution.py:22
  28.5 14.4 %collective-permute-start.4 = (bf16[3,10,18,1]{2,3,1,0:T(2,128)(2,1)S(1)}, bf16[3,10,18,1]{2,3,1,0:T(2,128)(2,1)S(1)}, u32[]{:S(2)}, u32[]{:S(2)}) collective-permute-start(bf16[3,10,18,1]{2,3,1,0:T(2,128)(2,1)S(1)} %get-tuple-element.81), channel_id=1, source_target_pairs={{1,0},{2,1},{3,2},{4,3},{5,4},{6,5},{7,6},{8,7},{9,8},{10,9},{11,1... | collective-permute-start | bytes 3248 | tf_op jit(solution)/shard_map/ppermute | solution.py:23
  52.1 7.1 %collective-permute-start.7 = (bf16[64,1,16,4]{0,3,2,1:T(4,128)(2,1)S(1)}, bf16[64,1,16,4]{0,3,2,1:T(4,128)(2,1)S(1)}, u32[]{:S(2)}, u32[]{:S(2)}) collective-permute-start(bf16[64,1,16,4]{0,3,2,1:T(4,128)(2,1)S(1)} %get-tuple-element.50), channel_id=1, source_target_pairs={{128,0},{256,128},{384,256},{0,384},{129,1},{257,129},{385,257},{1... | collective-permute-start | bytes 24584 | tf_op jit(solution)/shard_map/ppermute | solution.py:23
  56.6 3.1 %collective-permute-start.6 = (bf16[64,1,16,4]{0,3,2,1:T(4,128)(2,1)S(1)}, bf16[64,1,16,4]{0,3,2,1:T(4,128)(2,1)S(1)}, u32[]{:S(2)}, u32[]{:S(2)}) collective-permute-start(bf16[64,1,16,4]{0,3,2,1:T(4,128)(2,1)S(1)} %get-tuple-element.49), channel_id=1, source_target_pairs={{0,128},{128,256},{256,384},{384,0},{1,129},{129,257},{257,385},{3... | collective-permute-start | bytes 24584 | tf_op jit(solution)/shard_map/ppermute | solution.py:22
  59.7 5.5 %collective-permute-start.9 = (bf16[64,10,1,4]{0,3,2,1:T(4,128)(2,1)S(1)}, bf16[64,10,1,4]{0,3,2,1:T(4,128)(2,1)S(1)}, u32[]{:S(2)}, u32[]{:S(2)}) collective-permute-start(bf16[64,10,1,4]{0,3,2,1:T(4,128)(2,1)S(1)} %get-tuple-element.46), channel_id=1, source_target_pairs={{32,0},{64,32},{96,64},{0,96},{33,1},{65,33},{97,65},{1,97},{34,2}... | collective-permute-start | bytes 15368 | tf_op jit(solution)/shard_map/ppermute | solution.py:23
  61.6 5.6 %collective-permute-start.8 = (bf16[64,10,1,4]{0,3,2,1:T(4,128)(2,1)S(1)}, bf16[64,10,1,4]{0,3,2,1:T(4,128)(2,1)S(1)}, u32[]{:S(2)}, u32[]{:S(2)}) collective-permute-start(bf16[64,10,1,4]{0,3,2,1:T(4,128)(2,1)S(1)} %get-tuple-element.45), channel_id=1, source_target_pairs={{0,32},{32,64},{64,96},{96,0},{1,33},{33,65},{65,97},{97,1},{2,34}... | collective-permute-start | bytes 15368 | tf_op jit(solution)/shard_map/ppermute | solution.py:22
  67.6 11.8 %collective-permute-start.11 = (bf16[64,10,18,1]{0,3,2,1:T(2,128)(2,1)S(1)}, bf16[64,10,18,1]{0,3,2,1:T(2,128)(2,1)S(1)}, u32[]{:S(2)}, u32[]{:S(2)}) collective-permute-start(bf16[64,10,18,1]{0,3,2,1:T(2,128)(2,1)S(1)} %get-tuple-element.35), channel_id=1, source_target_pairs={{0,1},{1,2},{2,3},{3,4},{4,5},{5,6},{6,7},{7,8},{8,9},{9,10},{10,1... | collective-permute-start | bytes 69128 | tf_op jit(solution)/shard_map/ppermute | solution.py:22
  69.5 9.9 %collective-permute-start.10 = (bf16[64,10,18,1]{0,3,2,1:T(2,128)(2,1)S(1)}, bf16[64,10,18,1]{0,3,2,1:T(2,128)(2,1)S(1)}, u32[]{:S(2)}, u32[]{:S(2)}) collective-permute-start(bf16[64,10,18,1]{0,3,2,1:T(2,128)(2,1)S(1)} %get-tuple-element.36), channel_id=1, source_target_pairs={{1,0},{2,1},{3,2},{4,3},{5,4},{6,5},{7,6},{8,7},{9,8},{10,9},{11,1... | collective-permute-start | bytes 69128 | tf_op jit(solution)/shard_map/ppermute | solution.py:23
  89.3 2.8 %copy-start.6 = (bf16[64,512]{1,0:T(8,128)(2,1)S(1)}, bf16[64,512]{1,0:T(8,128)(2,1)}, u32[]{:S(2)}) copy-start(bf16[64,512]{1,0:T(8,128)(2,1)} %copy.105) | copy-start | bytes 196612
  89.3 2.8 %copy-start.7 = (bf16[128,512]{1,0:T(8,128)(2,1)S(1)}, bf16[128,512]{1,0:T(8,128)(2,1)}, u32[]{:S(2)}) copy-start(bf16[128,512]{1,0:T(8,128)(2,1)} %copy.110) | copy-start | bytes 393220
  89.4 2.8 %copy-start.9 = (bf16[64,512]{1,0:T(8,128)(2,1)S(1)}, bf16[64,512]{1,0:T(8,128)(2,1)}, u32[]{:S(2)}) copy-start(bf16[64,512]{1,0:T(8,128)(2,1)} %copy.111) | copy-start | bytes 196612
  92.1 2.1 copy-start.3
  94.8 1.0 copy-start.4
  94.8 1.0 copy-start.5
  97.3 8.2 %copy-start = (bf16[27,12288]{1,0:T(8,128)(2,1)S(1)}, bf16[27,12288]{1,0:T(8,128)(2,1)}, u32[]{:S(2)}) copy-start(bf16[27,12288]{1,0:T(8,128)(2,1)} %param.10) | copy-start | bytes 1990660
  98.4 19.9 %all-to-all-start = ((bf16[16,192,128]{2,1,0:T(8,128)(2,1)}), bf16[16,192,128]{2,1,0:T(8,128)(2,1)S(1)}, u32[]{:S(2)}, u32[]{:S(2)}) async-start(bf16[16,192,128]{2,1,0:T(8,128)(2,1)} %bitcast.79), calls=%async_computation | async-start | bytes 1572864 | tf_op jit(solution)/shard_map/all_to_all | solution.py:110
  111.1 14.6 %copy-start.2 = (bf16[576,192]{1,0:T(8,128)(2,1)S(1)}, bf16[576,192]{1,0:T(8,128)(2,1)}, u32[]{:S(2)}) copy-start(bf16[576,192]{1,0:T(8,128)(2,1)} %reshape.292) | copy-start | bytes 663556
  112.6 13.6 %copy-start.1 = (bf16[576,192]{1,0:T(8,128)(2,1)S(1)}, bf16[576,192]{1,0:T(8,128)(2,1)}, u32[]{:S(2)}) copy-start(bf16[576,192]{1,0:T(8,128)(2,1)} %reshape.311) | copy-start | bytes 663556
  119.1 22.9 %all-to-all-start.1 = ((f32[32,6,128]{2,1,0:T(8,128)}), f32[32,6,128]{2,1,0:T(8,128)S(1)}, u32[]{:S(2)}, u32[]{:S(2)}) async-start(f32[32,6,128]{2,1,0:T(8,128)} %reshape.320), calls=%async_computation.1 | async-start | bytes 262144 | tf_op jit(solution)/shard_map/all_to_all | solution.py:113

commit v2 on v0

v2 whole, which is shorter than its diff:
```python
import jax
import jax.numpy as jnp
from jax import lax
from jax.experimental import pallas as pl
from jax.experimental.pallas import tpu as pltpu
from jax.sharding import Mesh, PartitionSpec as P

C_UP = 128
C_HID = 64
C_VEL = 3
SIZE_X, SIZE_Y, SIZE_Z = 8, 16, 4
CELLS = SIZE_X * SIZE_Y * SIZE_Z
NORM = 1.0 / 512.0
F32, BF16 = jnp.float32, jnp.bfloat16

GZ = ("gzh", "gzm", "gzl")
FIRST = ("gx", "gyl")
SECOND = ("gyh", "gzl")
THIRD = ("gzh", "gzm")
PACK_ROWS = 3072
TAP_ROWS = 336

root_half = 0.7071067811865476
inv_root_tau = 0.3989422804014327


def gelu_value(values):
    return 0.5 * values * (1.0 + lax.erf(values * root_half))


def gelu_slope(values):
    return (
        0.5 * (1.0 + lax.erf(values * root_half))
        + values * jnp.exp(-0.5 * values * values) * inv_root_tau
    )


def from_both(to_next, to_previous, axis):
    peers = lax.axis_size(axis)
    up = [(i, (i + 1) % peers) for i in range(peers)]
    down = [(j, i) for i, j in up]
    return lax.ppermute(to_next, axis, up), lax.ppermute(to_previous, axis, down)


def extended_fields(pre_act, cotangent):
    cot = jnp.transpose(cotangent, (1, 2, 3, 0)).reshape(SIZE_X, SIZE_Y, SIZE_Z * C_VEL)
    fill = jnp.zeros((SIZE_X, SIZE_Y, 58), BF16)
    high = jnp.concatenate([pre_act[..., 192:], cot[..., 6:], fill], axis=-1)
    low = jnp.concatenate([pre_act[..., :64], cot[..., :6], fill], axis=-1)
    before, after = from_both(high, low, GZ)
    fill = jnp.zeros((SIZE_X, SIZE_Y, 104), BF16)
    field = jnp.concatenate(
        [before[..., :64], pre_act, after[..., :64], before[..., 64:70], cot, after[..., 64:70], fill],
        axis=-1,
    )
    before, after = from_both(field[6:], field[:2], "gx")
    field = jnp.concatenate([before, field, after], axis=0)
    before, after = from_both(field[:, 14:], field[:, :2], ("gyh", "gyl"))
    fill = jnp.zeros((SIZE_X + 4, 12, 512), BF16)
    return jnp.concatenate([before, field, after, fill], axis=1)


def head_matrix(weight_out):
    taps = weight_out.reshape(9, 3, C_VEL, C_HID)[:, ::-1].reshape(9, 9, C_HID)
    columns = [jnp.pad(taps, ((0, 0), (3 * z, 23 - 3 * z), (0, 0))) for z in range(6)]
    return jnp.concatenate(columns, axis=2)


def input_matrix(weight_one):
    taps = weight_one.reshape(9, 3, C_HID, 192)[:, ::-1].reshape(9, 192, 192)
    wide = jnp.concatenate([taps, taps[..., C_UP:]], axis=2)
    return jnp.pad(wide, ((0, 0), (0, 64), (0, 0)))


def low_half(shape):
    return lax.broadcasted_iota(jnp.int32, shape, len(shape) - 1) < 64


def rolled(values, shift):
    flat = values.reshape(-1, values.shape[-1])
    return pltpu.roll(flat, shift, 1).reshape(values.shape)


def gradient_kernel(
    field_ref, pre_ref, skip_ref, coarse_ref, head_ref, pack_ref, window_ref, cot_s, pre_s, in_s
):
    cot_s[:, 0:8, :] = jnp.zeros((12, 8, 128), F32)
    cot_s[:, 8:40, :] = field_ref[:, :, 384:512].astype(F32)
    total = jnp.zeros((240, 384), F32)
    for a in (-1, 0, 1):
        for b in (-1, 0, 1):
            moved = cot_s[1 - a : 11 - a, 8 - b : 32 - b, :].reshape(240, 128).astype(BF16)
            total = total + jnp.dot(
                moved[:, :32], head_ref[3 * (a + 1) + b + 1], preferred_element_type=F32
            )
    pre_wide = field_ref[1:11, :, 0:384].astype(F32)[:, :24].reshape(240, 384)
    d_pre = (total * gelu_slope(pre_wide)).astype(BF16).astype(F32)
    pre_s[:, :, 0:384] = d_pre.reshape(10, 24, 384)
    pre_s[:, :, 384:512] = cot_s[1:11, 8:32, :]

    half = low_half((10, 16, 128))
    for b in (-1, 0, 1):
        moved = pre_s[:, 2 - b : 18 - b, :]
        shifted = rolled(moved[:, :, :384], 320)
        for z in range(SIZE_Z):
            source, start = (moved, 64 * z) if z % 2 == 0 else (shifted, 64 * z - 64)
            low = source[:, :, start : start + 128]
            high = source[:, :, start + 128 : start + 256]
            cot = rolled(moved[:, :, 384:512], 61 - 3 * z)
            window_ref[b + 1, z, :, :, 0:128] = low.astype(BF16)
            window_ref[b + 1, z, :, :, 128:256] = jnp.where(half, high, cot).astype(BF16)

    hidden = gelu_value(pre_ref[...].astype(F32))
    skip = skip_ref[...].astype(F32)
    half = low_half((8, 16, 128))
    for z in range(SIZE_Z):
        pair = slice(128 * (z // 2), 128 * (z // 2) + 128)
        if z % 2 == 0:
            second = jnp.where(half, skip[:, :, pair], rolled(hidden[:, :, pair], 64))
        else:
            second = jnp.where(half, rolled(skip[:, :, pair], 64), hidden[:, :, pair])
        in_s[z, :, :, 128:256] = second.astype(BF16)
        for x in range(SIZE_X):
            in_s[z, x, :, 0:128] = coarse_ref[x // 2, :, pair]

    inputs = in_s[...].reshape(CELLS, 256)
    half = low_half((64, 128))
    for a in (-1, 0, 1):
        for b in (-1, 0, 1):
            window = window_ref[b + 1, :, 1 - a : 9 - a].reshape(CELLS, 256)
            result = lax.dot_general(
                window, inputs, (((0,), (0,)), ((), ())), preferred_element_type=F32
            )
            start = TAP_ROWS * (3 * (a + 1) + b + 1)
            pair = jnp.where(half, result[0:64, 128:256], rolled(result[64:128, 128:256], 64))
            pack_ref[start : start + 192, :] = result[0:192, 0:128].astype(BF16)
            pack_ref[start + 192 : start + 256, :] = pair.astype(BF16)
            pack_ref[start + 256 : start + 336, :] = result[128:208, 128:256].astype(BF16)
    pack_ref[9 * TAP_ROWS : PACK_ROWS, :] = jnp.zeros((PACK_ROWS - 9 * TAP_ROWS, 128), BF16)


def input_kernel(window_ref, weight_ref, skip_ref, coarse_ref, sum_s):
    windows = [
        window_ref[b + 1, :, 1 - a : 9 - a].reshape(CELLS, 256)
        for a in (-1, 0, 1)
        for b in (-1, 0, 1)
    ]
    total = jnp.dot(
        jnp.concatenate(windows, axis=1),
        weight_ref[...].reshape(9 * 256, 256),
        preferred_element_type=F32,
    ).reshape(SIZE_Z, SIZE_X, SIZE_Y, 256)
    half = low_half((8, 16, 128))
    for pair in range(2):
        even, odd = total[2 * pair], total[2 * pair + 1]
        lanes = slice(128 * pair, 128 * pair + 128)
        skip_ref[:, :, lanes] = jnp.where(half, even[..., 128:], odd[..., 128:]).astype(BF16)
        both = (even[..., :128] + odd[..., :128]).reshape(4, 2, 16, 128)
        sum_s[...] = (both[:, 0] + both[:, 1]).reshape(64, 128)
        summed = sum_s[pl.ds(0, 32, stride=2), :] + sum_s[pl.ds(1, 32, stride=2), :]
        coarse_ref[:, lanes] = summed.astype(BF16)


def traded(parts, axes):
    return lax.all_to_all(parts, axes, 0, 0)


def spread(part, axes):
    peers = lax.axis_size(axes)
    return traded(jnp.broadcast_to(part[None], (peers, *part.shape)), axes)


def sum_everywhere(packed):
    first = traded(packed.reshape(8, 384, 128), FIRST)
    first = jnp.sum(first.astype(F32), axis=0)
    second = jnp.sum(traded(first.reshape(8, 48, 128), SECOND), axis=0)
    third = jnp.sum(spread(second, THIRD), axis=0)
    fourth = spread(third.astype(BF16), SECOND).reshape(384, 128)
    return spread(fourth, FIRST).reshape(PACK_ROWS, 128)


def unpacked(packed):
    taps = packed[: 9 * TAP_ROWS].reshape(9, TAP_ROWS, 128).astype(F32) * NORM
    up = taps[:, :192].reshape(9, 3, C_HID, C_UP)
    pair = taps[:, 192:256]
    third = taps[:, 256:320, :64]
    skip = jnp.stack([pair[..., :64], pair[..., 64:], third], axis=1)
    body = jnp.concatenate([up, skip], axis=-1)[:, ::-1].reshape(27, C_HID * 192)
    head = taps[:, 320:329, 64:].reshape(9, 3, C_VEL, C_HID)[:, ::-1].reshape(27, C_VEL, C_HID)
    return body, head


def per_device(coarse, skip_features, pre_act, cotangent, weight_one, weight_out):
    field = extended_fields(pre_act, cotangent)
    packed, window = pl.pallas_call(
        gradient_kernel,
        out_shape=(
            jax.ShapeDtypeStruct((PACK_ROWS, 128), BF16),
            jax.ShapeDtypeStruct((3, SIZE_Z, 10, 16, 256), BF16),
        ),
        scratch_shapes=[
            pltpu.VMEM((12, 40, 128), F32),
            pltpu.VMEM((10, 24, 512), F32),
            pltpu.VMEM((SIZE_Z, SIZE_X, SIZE_Y, 256), BF16),
        ],
        compiler_params=pltpu.CompilerParams(vmem_limit_bytes=32 * 2**20),
        cost_estimate=pl.CostEstimate(
            flops=700_000_000, bytes_accessed=3_000_000, transcendentals=200_000
        ),
    )(field, pre_act, skip_features, jnp.repeat(coarse, 2, axis=1), head_matrix(weight_out))
    skip_grad, coarse_grad = pl.pallas_call(
        input_kernel,
        out_shape=(
            jax.ShapeDtypeStruct((SIZE_X, SIZE_Y, 256), BF16),
            jax.ShapeDtypeStruct((32, 256), BF16),
        ),
        scratch_shapes=[pltpu.VMEM((64, 128), F32)],
        compiler_params=pltpu.CompilerParams(vmem_limit_bytes=32 * 2**20),
        cost_estimate=pl.CostEstimate(
            flops=700_000_000, bytes_accessed=3_000_000, transcendentals=0
        ),
    )(window, input_matrix(weight_one))
    body, head = unpacked(sum_everywhere(packed))
    return coarse_grad.reshape(4, 8, 256), skip_grad, body, head


def solution(mesh):
    names = ("gx", "gyh", "gyl", "gzh", "gzm", "gzl")
    split = Mesh(mesh.devices.reshape(4, 2, 2, 2, 4, 4), names)
    field = P("gx", ("gyh", "gyl"), GZ)
    return jax.shard_map(
        per_device,
        mesh=split,
        in_specs=(field, field, field, P(None, "gx", ("gyh", "gyl"), GZ), P(), P()),
        out_specs=(field, field, P(), P()),
        check_vma=False,
    )
```

time: 830 us -> 134 us (0.16)
  waiting for transfers between devices: 446 us -> 18 us
  local copies, waits for them, and re-layouts: 122 us -> 9.52 us
  starting transfers between devices: 110 us -> 39.4 us
  blocking collectives: 105 us -> 59.3 us
  matrix products: 17.9 us -> 0 us
  between operations: 15.4 us -> 0.93 us
    psum x1 -> x0, waiting for transfers between devices: 445 us -> none  [per_device(): lax.psum((body_grad, head_grad), ('gx', 'gy', 'gz'))]
    psum x1 -> x0, blocking collectives: 105 us -> none  [per_device(): lax.psum((body_grad, head_grad), ('gx', 'gy', 'gz'))]
    ppermute x30 -> x6, starting transfers between devices: 110 us -> 29.2 us  [the longest x3 19.9 us: from_both(): lax.ppermute(to_previous, axis, down)]
    reshape x91 -> x7, local copies, waits for them, and re-layouts: 73.9 us -> 3.91 us  [the longest x1 1.93 us: unpacked(): jnp.concatenate([up, skip], axis=-1)[:, ::-1].reshape(27, C_HID * 192)]
    all_to_all x0 -> x4, blocking collectives: none -> 59.3 us  [traded(): return lax.all_to_all(parts, axes, 0, 0)]
    slice x52 -> x8, local copies, waits for them, and re-layouts: 22.7 us -> 1.34 us  [the longest x2 0.94 us: extended_fields(): low = jnp.concatenate([pre_act[..., :64], cot[..., :6], fill], axis=-1)]
    dot_general x16 -> x0, matrix products: 17.9 us -> none  [the longest x12 16.6 us: contract_cells(): lax.dot_general(left_side, right_side, (((1,), (1,)), ((), ())), preferre...]
    unnamed x96 -> x10, local copies, waits for them, and re-layouts: 16.8 us -> 1.39 us
  transfers between devices with their start and end apart: 31 -> 7, of which waited for: 3 -> 4; matrix products, arithmetic and copies ran while one was open for 18% -> 2% of each run, Pallas kernels for 0% -> 1%
where the time goes in v2:
time: 134 us; the launch traced here: 133 us
  blocking collectives  59.3 us (44%)
  starting transfers between devices  39.4 us (29%)
  waiting for transfers between devices  18 us (13%)
  local copies, waits for them, and re-layouts  9.52 us (7%)
  Pallas kernels  3.58 us (3%)
  other arithmetic  2.14 us (2%)
    all_to_all x4, blocking collectives, traded(): return lax.all_to_all(parts, axes, 0, 0)  59.3 us
    ppermute x3, starting transfers between devices, from_both(): lax.ppermute(to_previous, axis, down)  19.9 us
    all_to_all x1, starting transfers between devices, traded(): return lax.all_to_all(parts, axes, 0, 0)  10.1 us
    ppermute x3, starting transfers between devices, from_both(): lax.ppermute(to_next, axis, up)  9.34 us
    all_to_all x1, waiting for transfers between devices, traded(): return lax.all_to_all(parts, axes, 0, 0)  8.46 us
    ppermute x3, waiting for transfers between devices, from_both(): lax.ppermute(to_next, axis, up)  6.26 us
    ppermute x3, waiting for transfers between devices, from_both(): lax.ppermute(to_previous, axis, down)  3.26 us
  transfers between devices with their start and end apart: 7, of which 4 were waited for; matrix products, arithmetic and copies ran while one was open for 2% of the time, Pallas kernels for 1%

profile of v2, /device:TPU:1, one launch (start us, length us, event | category | flops | bytes accessed | tf_op | source)
XLA Modules:
  0.0 132.8 jit_solution(4125287430211825178)
XLA Ops:
  0.6 0.0 copy-start.3
  0.6 0.7 copy.21
  1.4 0.1 copy.22
  1.5 0.1 fusion.6
  1.6 0.9 fusion.4
  2.5 0.1 pad.56.clone
  2.6 0.0 copy-start
  2.6 0.0 copy-start.1
  2.6 0.1 maximum_maximum_fusion.2
  2.7 14.6 %collective-permute-start.1 = (bf16[8,16,128]{2,1,0:T(8,128)(2,1)S(1)}, bf16[8,16,128]{2,1,0:T(8,128)(2,1)S(1)}, u32[]{:S(2)}, u32[]{:S(2)}) collective-permute-start(bf16[8,16,128]{2,1,0:T(8,128)(2,1)S(1)} %get-tuple-element.37), channel_id=1, source_target_pairs={{1,0},{2,1},{3,2},{4,3},{5,4},{6,5},{7,6},{8,7},{9,8},{10,9},{11,1... | collective-permute-start | bytes 98312 | tf_op jit(solution)/shard_map/ppermute | solution.py:42
  17.3 1.9 %collective-permute-start = (bf16[8,16,128]{2,1,0:T(8,128)(2,1)S(1)}, bf16[8,16,128]{2,1,0:T(8,128)(2,1)S(1)}, u32[]{:S(2)}, u32[]{:S(2)}) collective-permute-start(bf16[8,16,128]{2,1,0:T(8,128)(2,1)S(1)} %get-tuple-element.38), channel_id=1, source_target_pairs={{0,1},{1,2},{2,3},{3,4},{4,5},{5,6},{6,7},{7,8},{8,9},{9,10},{10,1... | collective-permute-start | bytes 98312 | tf_op jit(solution)/shard_map/ppermute | solution.py:42
  19.2 0.0 collective-permute-done.1
  19.2 0.1 slice.84
  19.3 6.3 %collective-permute-done = bf16[8,16,128]{2,1,0:T(8,128)(2,1)S(1)} collective-permute-done((bf16[8,16,128]{2,1,0:T(8,128)(2,1)S(1)}, bf16[8,16,128]{2,1,0:T(8,128)(2,1)S(1)}, u32[]{:S(2)}, u32[]{:S(2)}) %collective-permute-start) | collective-permute-done | bytes 32800 | tf_op jit(solution)/shard_map/ppermute | solution.py:42
  25.5 0.1 slice.83
  25.6 1.0 concatenate.26
  26.6 4.3 %collective-permute-start.2 = (bf16[2,16,512]{2,1,0:T(8,128)(2,1)S(1)}, bf16[2,16,512]{2,1,0:T(8,128)(2,1)S(1)}, u32[]{:S(2)}, u32[]{:S(2)}) collective-permute-start(bf16[2,16,512]{2,1,0:T(8,128)(2,1)S(1)} %get-tuple-element.25), channel_id=1, source_target_pairs={{0,128},{128,256},{256,384},{384,0},{1,129},{129,257},{257,385},{3... | collective-permute-start | bytes 98312 | tf_op jit(solution)/shard_map/ppermute | solution.py:42
  30.9 1.9 %collective-permute-start.3 = (bf16[2,16,512]{2,1,0:T(8,128)(2,1)S(1)}, bf16[2,16,512]{2,1,0:T(8,128)(2,1)S(1)}, u32[]{:S(2)}, u32[]{:S(2)}) collective-permute-start(bf16[2,16,512]{2,1,0:T(8,128)(2,1)S(1)} %get-tuple-element.26), channel_id=1, source_target_pairs={{128,0},{256,128},{384,256},{0,384},{129,1},{257,129},{385,257},{1... | collective-permute-start | bytes 98312 | tf_op jit(solution)/shard_map/ppermute | solution.py:42
  32.9 0.8 copy.28
  33.7 0.0 collective-permute-done.2
  33.7 2.5 %collective-permute-done.3 = bf16[2,16,512]{2,1,0:T(8,128)(2,1)S(1)} collective-permute-done((bf16[2,16,512]{2,1,0:T(8,128)(2,1)S(1)}, bf16[2,16,512]{2,1,0:T(8,128)(2,1)S(1)}, u32[]{:S(2)}, u32[]{:S(2)}) %collective-permute-start.3) | collective-permute-done | bytes 32800 | tf_op jit(solution)/shard_map/ppermute | solution.py:42
  36.2 3.1 %collective-permute-start.4 = (bf16[12,2,512]{2,1,0:T(2,128)(2,1)S(1)}, bf16[12,2,512]{2,1,0:T(2,128)(2,1)S(1)}, u32[]{:S(2)}, u32[]{:S(2)}) collective-permute-start(bf16[12,2,512]{2,1,0:T(2,128)(2,1)S(1)} %get-tuple-element.23), channel_id=1, source_target_pairs={{0,32},{32,64},{64,96},{96,0},{1,33},{33,65},{65,97},{97,1},{2,34}... | collective-permute-start | bytes 73736 | tf_op jit(solution)/shard_map/ppermute | solution.py:42
  39.3 3.4 %collective-permute-start.5 = (bf16[12,2,512]{2,1,0:T(2,128)(2,1)S(1)}, bf16[12,2,512]{2,1,0:T(2,128)(2,1)S(1)}, u32[]{:S(2)}, u32[]{:S(2)}) collective-permute-start(bf16[12,2,512]{2,1,0:T(2,128)(2,1)S(1)} %get-tuple-element.24), channel_id=1, source_target_pairs={{32,0},{64,32},{96,64},{0,96},{33,1},{65,33},{97,65},{1,97},{34,2}... | collective-permute-start | bytes 73736 | tf_op jit(solution)/shard_map/ppermute | solution.py:42
  42.7 0.1 fusion.5
  42.8 0.1 pad.47.clone
  42.9 0.0 copy-done.3
  42.9 0.2 concatenate.29.head_ref
  43.1 0.0 collective-permute-done.4
  43.1 0.8 collective-permute-done.5
  43.9 0.2 maximum_maximum_fusion.field_ref
  44.1 0.0 copy-done
  44.1 0.0 copy-done.1
  44.1 2.1 %shard_map.93 = (bf16[3072,128]{1,0:T(8,128)(2,1)S(1)}, bf16[3,4,10,16,256]{4,3,2,1,0:T(8,128)(2,1)S(1)}) custom-call(bf16[12,32,512]{2,1,0:T(8,128)(2,1)S(1)} %maximum_maximum_fusion.field_ref, bf16[8,16,256]{2,1,0:T(8,128)(2,1)S(1)} %copy-done, bf16[8,16,256]{2,1,0:T(8,128)(2,1)S(1)} %copy-done.1, bf16[4,16,256]{2,1,0:T(8,128)(2,1)S(1)} %reshape.60.coarse_ref, ...), custom_call_target="tpu_custom_call" | custom-call | flops 700000000 | bytes 3000000 | tf_op jit(solution)/shard_map/pallas_call | solution.py:195
  46.3 15.6 %all_to_all.25 = bf16[8,384,128]{2,1,0:T(8,128)(2,1)S(1)} all-to-all(bf16[8,384,128]{2,1,0:T(8,128)(2,1)S(1)} %bitcast.23), channel_id=1, replica_groups=mesh['gx'=4,'gyh'=2,'gyl'=2,'gzh'=2,'gzm'=4,'gzl'=4] {'gx','gyl'}, dimensions={0} | all-to-all | bytes 1572864 | tf_op jit(solution)/shard_map/all_to_all | solution.py:165
  61.8 0.1 convert_reduce_fusion
  61.9 12.6 %all_to_all.26 = f32[8,48,128]{2,1,0:T(8,128)S(1)} all-to-all(f32[8,48,128]{2,1,0:T(8,128)S(1)} %bitcast.30), channel_id=1, replica_groups=mesh['gx'=4,'gyh'=2,'gyl'=2,'gzh'=2,'gzm'=4,'gzl'=4] {'gyh','gzl'}, dimensions={0} | all-to-all | bytes 393216 | tf_op jit(solution)/shard_map/all_to_all | solution.py:165
  74.5 20.1 %all_to_all.27 = f32[8,48,128]{2,1,0:T(8,128)S(1)} all-to-all(f32[8,48,128]{2,1,0:T(8,128)S(1)} %broadcast_in_dim.35), channel_id=1, replica_groups=mesh['gx'=4,'gyh'=2,'gyl'=2,'gzh'=2,'gzm'=4,'gzl'=4] {'gzh','gzm'}, dimensions={0} | all-to-all | bytes 393216 | tf_op jit(solution)/shard_map/all_to_all | solution.py:165
  94.6 0.0 copy-start.2
  94.6 11.1 %all_to_all.28 = bf16[8,48,128]{2,1,0:T(8,128)(2,1)S(1)} all-to-all(bf16[8,48,128]{2,1,0:T(8,128)(2,1)S(1)} %broadcast_in_dim.36), channel_id=1, replica_groups=mesh['gx'=4,'gyh'=2,'gyl'=2,'gzh'=2,'gzm'=4,'gzl'=4] {'gyh','gzl'}, dimensions={0} | all-to-all | bytes 196608 | tf_op jit(solution)/shard_map/all_to_all | solution.py:165
  105.7 1.0 broadcast_in_dim.38
  106.7 10.1 %all-to-all-start.4 = ((bf16[8,384,128]{2,1,0:T(8,128)(2,1)}), bf16[8,384,128]{2,1,0:T(8,128)(2,1)}, u32[]{:S(2)}, u32[]{:S(2)}) async-start(bf16[8,384,128]{2,1,0:T(8,128)(2,1)} %broadcast_in_dim.38), calls=%async_computation.4 | async-start | bytes 1572864 | tf_op jit(solution)/shard_map/all_to_all | solution.py:165
  116.9 0.0 copy-done.2
  116.9 1.0 reshape.63
  117.9 0.1 rev.13
  118.0 0.1 slice.87
  118.1 0.3 fusion.2.weight_ref
  118.4 1.4 %shard_map.94 = (bf16[8,16,256]{2,1,0:T(8,128)(2,1)}, bf16[32,256]{1,0:T(8,128)(2,1)}) custom-call(bf16[3,4,10,16,256]{4,3,2,1,0:T(8,128)(2,1)S(1)} %get-tuple-element.8.window_ref, bf16[9,256,256]{2,1,0:T(8,128)(2,1)S(1)} %fusion.2.weight_ref), custom_call_target="tpu_custom_call" | custom-call | flops 700000000 | bytes 3000000 | tf_op jit(solution)/shard_map/pallas_call | solution.py:211
  119.8 8.5 %all-to-all-done.4 = bf16[8,384,128]{2,1,0:T(8,128)(2,1)} async-done(((bf16[8,384,128]{2,1,0:T(8,128)(2,1)}), bf16[8,384,128]{2,1,0:T(8,128)(2,1)}, u32[]{:S(2)}, u32[]{:S(2)}) %all-to-all-start.4) | async-done | bytes 786464 | tf_op jit(solution)/shard_map/all_to_all | solution.py:165
  128.3 1.2 convert_multiply_fusion
  129.5 0.1 slice.93
  129.6 0.1 slice.89
  129.7 0.2 slice_bitcast_fusion.2
  129.9 0.6 copy.27
  130.5 0.1 pad_maximum_fusion
  130.6 0.2 rev.14
  130.8 1.9 %reshape.70 = f32[27,12288]{1,0:T(8,128)} reshape(f32[9,3,64,192]{3,2,1,0:T(8,128)S(1)} %rev.14) | data formatting | bytes 2654208 | tf_op jit(solution)/shard_map/reshape | solution.py:188
  (15 shorter events, 0.2 us)
Async XLA Ops:
  0.6 42.3 %copy-start.3 = (bf16[4,8,256]{2,1,0:T(8,128)(2,1)S(1)}, bf16[4,8,256]{2,1,0:T(8,128)(2,1)}, u32[]{:S(2)}) copy-start(bf16[4,8,256]{2,1,0:T(8,128)(2,1)} %param.6) | copy-start | bytes 49156
  2.6 41.5 %copy-start = (bf16[8,16,256]{2,1,0:T(8,128)(2,1)S(1)}, bf16[8,16,256]{2,1,0:T(8,128)(2,1)}, u32[]{:S(2)}) copy-start(bf16[8,16,256]{2,1,0:T(8,128)(2,1)} %pre_ref.1) | copy-start | bytes 196612
  2.6 41.5 %copy-start.1 = (bf16[8,16,256]{2,1,0:T(8,128)(2,1)S(1)}, bf16[8,16,256]{2,1,0:T(8,128)(2,1)}, u32[]{:S(2)}) copy-start(bf16[8,16,256]{2,1,0:T(8,128)(2,1)} %skip_ref.1) | copy-start | bytes 196612
  2.7 16.5 %collective-permute-start.1 = (bf16[8,16,128]{2,1,0:T(8,128)(2,1)S(1)}, bf16[8,16,128]{2,1,0:T(8,128)(2,1)S(1)}, u32[]{:S(2)}, u32[]{:S(2)}) collective-permute-start(bf16[8,16,128]{2,1,0:T(8,128)(2,1)S(1)} %get-tuple-element.37), channel_id=1, source_target_pairs={{1,0},{2,1},{3,2},{4,3},{5,4},{6,5},{7,6},{8,7},{9,8},{10,9},{11,1... | collective-permute-start | bytes 98312 | tf_op jit(solution)/shard_map/ppermute | solution.py:42
  17.3 8.3 %collective-permute-start = (bf16[8,16,128]{2,1,0:T(8,128)(2,1)S(1)}, bf16[8,16,128]{2,1,0:T(8,128)(2,1)S(1)}, u32[]{:S(2)}, u32[]{:S(2)}) collective-permute-start(bf16[8,16,128]{2,1,0:T(8,128)(2,1)S(1)} %get-tuple-element.38), channel_id=1, source_target_pairs={{0,1},{1,2},{2,3},{3,4},{4,5},{5,6},{6,7},{7,8},{8,9},{9,10},{10,1... | collective-permute-start | bytes 98312 | tf_op jit(solution)/shard_map/ppermute | solution.py:42
  26.6 7.0 %collective-permute-start.2 = (bf16[2,16,512]{2,1,0:T(8,128)(2,1)S(1)}, bf16[2,16,512]{2,1,0:T(8,128)(2,1)S(1)}, u32[]{:S(2)}, u32[]{:S(2)}) collective-permute-start(bf16[2,16,512]{2,1,0:T(8,128)(2,1)S(1)} %get-tuple-element.25), channel_id=1, source_target_pairs={{0,128},{128,256},{256,384},{384,0},{1,129},{129,257},{257,385},{3... | collective-permute-start | bytes 98312 | tf_op jit(solution)/shard_map/ppermute | solution.py:42
  30.9 5.2 %collective-permute-start.3 = (bf16[2,16,512]{2,1,0:T(8,128)(2,1)S(1)}, bf16[2,16,512]{2,1,0:T(8,128)(2,1)S(1)}, u32[]{:S(2)}, u32[]{:S(2)}) collective-permute-start(bf16[2,16,512]{2,1,0:T(8,128)(2,1)S(1)} %get-tuple-element.26), channel_id=1, source_target_pairs={{128,0},{256,128},{384,256},{0,384},{129,1},{257,129},{385,257},{1... | collective-permute-start | bytes 98312 | tf_op jit(solution)/shard_map/ppermute | solution.py:42
  36.2 6.9 %collective-permute-start.4 = (bf16[12,2,512]{2,1,0:T(2,128)(2,1)S(1)}, bf16[12,2,512]{2,1,0:T(2,128)(2,1)S(1)}, u32[]{:S(2)}, u32[]{:S(2)}) collective-permute-start(bf16[12,2,512]{2,1,0:T(2,128)(2,1)S(1)} %get-tuple-element.23), channel_id=1, source_target_pairs={{0,32},{32,64},{64,96},{96,0},{1,33},{33,65},{65,97},{97,1},{2,34}... | collective-permute-start | bytes 73736 | tf_op jit(solution)/shard_map/ppermute | solution.py:42
  39.3 4.6 %collective-permute-start.5 = (bf16[12,2,512]{2,1,0:T(2,128)(2,1)S(1)}, bf16[12,2,512]{2,1,0:T(2,128)(2,1)S(1)}, u32[]{:S(2)}, u32[]{:S(2)}) collective-permute-start(bf16[12,2,512]{2,1,0:T(2,128)(2,1)S(1)} %get-tuple-element.24), channel_id=1, source_target_pairs={{32,0},{64,32},{96,64},{0,96},{33,1},{65,33},{97,65},{1,97},{34,2}... | collective-permute-start | bytes 73736 | tf_op jit(solution)/shard_map/ppermute | solution.py:42
  94.6 22.3 %copy-start.2 = (bf16[27,12288]{1,0:T(8,128)(2,1)S(1)}, bf16[27,12288]{1,0:T(8,128)(2,1)}, u32[]{:S(2)}) copy-start(bf16[27,12288]{1,0:T(8,128)(2,1)} %param.10) | copy-start | bytes 1990660
  106.7 21.5 %all-to-all-start.4 = ((bf16[8,384,128]{2,1,0:T(8,128)(2,1)}), bf16[8,384,128]{2,1,0:T(8,128)(2,1)}, u32[]{:S(2)}, u32[]{:S(2)}) async-start(bf16[8,384,128]{2,1,0:T(8,128)(2,1)} %broadcast_in_dim.38), calls=%async_computation.4 | async-start | bytes 1572864 | tf_op jit(solution)/shard_map/all_to_all | solution.py:165

commit v3 on v2

v3 whole, which is shorter than its diff:
```python
import jax
import jax.numpy as jnp
import numpy as np
from jax import lax
from jax.experimental import pallas as pl
from jax.experimental.pallas import tpu as pltpu
from jax.sharding import Mesh, PartitionSpec as P

C_UP = 128
C_HID = 64
C_VEL = 3
SIZE_X, SIZE_Y, SIZE_Z = 8, 16, 4
CELLS = SIZE_X * SIZE_Y * SIZE_Z
NORM = 1.0 / 512.0
F32, BF16 = jnp.float32, jnp.bfloat16

GX, GY, GZ = "gx", "gy", ("gzh", "gzm", "gzl")
PLANE = ("gx", "gy")
NEAR = ("gzh", "gzl")
FAR = "gzm"
BLOCKS = 16
OWN = C_HID // BLOCKS
ROWS = 6 * OWN
SHARE = (32, OWN * 192)
HIGHEST = lax.Precision.HIGHEST


root_half = 0.7071067811865476
inv_root_tau = 0.3989422804014327


def gelu_value(values):
    return 0.5 * values * (1.0 + lax.erf(values * root_half))


def gelu_slope(values):
    return (
        0.5 * (1.0 + lax.erf(values * root_half))
        + values * jnp.exp(-0.5 * values * values) * inv_root_tau
    )


def from_both(to_next, to_previous, axis):
    peers = lax.axis_size(axis)
    up = [(i, (i + 1) % peers) for i in range(peers)]
    down = [(j, i) for i, j in up]
    return lax.ppermute(to_next, axis, up), lax.ppermute(to_previous, axis, down)


def depth_rims(pre_act, cotangent):
    pre = pre_act.reshape(128, SIZE_Z * C_HID).T
    cot = jnp.transpose(cotangent, (3, 0, 1, 2)).reshape(SIZE_Z * C_VEL, 128)
    fill = jnp.zeros((10, 128), BF16)
    high = jnp.concatenate([pre[192:], cot[6:], fill], axis=0)
    low = jnp.concatenate([pre[:64], cot[:6], fill], axis=0)
    before, after = from_both(high, low, GZ)
    pre = jnp.concatenate([before[:64], pre, after[:64]], axis=0)
    cot = jnp.concatenate([before[64:70], cot, after[64:70]], axis=0)
    return pre, cot


def plane_shares(pre, cot):
    own = jnp.transpose(pre.reshape(6, BLOCKS, OWN, 128), (1, 0, 2, 3)).reshape(BLOCKS, ROWS, 128)
    parts = jnp.concatenate([own, jnp.broadcast_to(cot[None], (BLOCKS, 24, 128))], axis=1)
    return traded(parts, PLANE)


def plane_inputs(coarse, skip_features):
    part = jnp.concatenate([coarse.reshape(32, 256), skip_features.reshape(128, 256)], axis=0)
    return spread(part, PLANE)


def side_field(pre, cot):
    fill = jnp.zeros((104, 128), BF16)
    return jnp.concatenate([pre, cot, fill], axis=0).T.reshape(SIZE_X, SIZE_Y, 512)


def with_x_rims(field):
    before, after = from_both(field[6:], field[:2], GX)
    return jnp.concatenate([before, field, after], axis=0)


def with_y_rims(field):
    before, after = from_both(field[:, 14:], field[:, :2], GY)
    fill = jnp.zeros((SIZE_X + 4, 12, 512), BF16)
    return jnp.concatenate([before, field, after, fill], axis=1)


def head_matrix(weight_out):
    taps = weight_out.reshape(9, 3, C_VEL, C_HID)[:, ::-1].reshape(9, 9, C_HID)
    columns = [jnp.pad(taps, ((0, 0), (3 * z, 23 - 3 * z), (0, 0))) for z in range(6)]
    return jnp.concatenate(columns, axis=2)


def own_head_matrix(head):
    place = lax.axis_index(GX) * lax.axis_size(GY) + lax.axis_index(GY)
    split = head[:, :24].reshape(9, 24, 6, BLOCKS, OWN)
    own = lax.dynamic_index_in_dim(split, place, 3, keepdims=False)
    return jnp.transpose(own, (2, 3, 0, 1)).reshape(ROWS, 216)


def choices():
    tap_rows = np.zeros((2, 2, OWN, 32, 216), np.float32)
    head_columns = np.zeros((9, 8, C_VEL, SIZE_Z, 128), np.float32)
    for tap in range(27):
        pair, c = tap // 3, tap % 3 - 1
        for z in range(SIZE_Z):
            for own in range(OWN):
                row = ROWS * pair + OWN * (z + 1 - c) + own
                tap_rows[z // 2, z % 2, own, tap, row] = 1.0
            for o in range(C_VEL):
                head_columns[pair, z + 2 - c, o, z, C_VEL * tap + o] = 1.0
    head_rows = np.zeros((32, 6, OWN), np.float32)
    for own in range(OWN):
        head_rows[27 + own, 1:5, own] = 1.0
    double = np.zeros((SIZE_X, SIZE_Y, SIZE_X // 2, SIZE_Y // 2), np.float32)
    for x in range(SIZE_X):
        for y in range(SIZE_Y):
            double[x, y, x // 2, y // 2] = 1.0
    return (
        jnp.asarray(tap_rows.reshape(2, 256, 216), BF16),
        jnp.asarray(head_columns.reshape(216, 512)),
        jnp.asarray(head_rows.reshape(32, ROWS)),
        jnp.asarray(double.reshape(128, 32), BF16),
    )


def input_matrix(weight_one):
    taps = weight_one.reshape(9, 3, C_HID, 192)[:, ::-1].reshape(9, 192, 192)
    wide = jnp.concatenate([taps, taps[..., C_UP:]], axis=2)
    return jnp.pad(wide, ((0, 0), (0, 64), (0, 0)))


def low_half(shape):
    return lax.broadcasted_iota(jnp.int32, shape, len(shape) - 1) < 64


def rolled(values, shift):
    flat = values.reshape(-1, values.shape[-1])
    return pltpu.roll(flat, shift, 1).reshape(values.shape)


def moved_y(blocks, b, lane):
    if b == 0:
        return blocks
    out = []
    for at in range(BLOCKS):
        gx, gy = at // 4, at % 4
        there = blocks[4 * gx + (gy - b) % 4]
        edge = lane % 16 == (0 if b == 1 else 15)
        out.append(
            jnp.where(edge, pltpu.roll(there, -15 * b % 128, 1), pltpu.roll(blocks[at], b % 128, 1))
        )
    return out


def moved_x(blocks, a, lane):
    if a == 0:
        return blocks
    turned = [pltpu.roll(block, 16 * a % 128, 1) for block in blocks]
    edge = lane // 16 == (0 if a == 1 else 7)
    return [
        jnp.where(edge, turned[4 * ((at // 4 - a) % 4) + at % 4], turned[at])
        for at in range(BLOCKS)
    ]


def stack_moved(blocks, stack_ref):
    lane = lax.broadcasted_iota(jnp.int32, (ROWS, 128), 1)
    for b in (-1, 0, 1):
        rows = moved_y(blocks, b, lane)
        for a in (-1, 0, 1):
            start = ROWS * (3 * (a + 1) + b + 1)
            for at, block in enumerate(moved_x(rows, a, lane)):
                stack_ref[start : start + ROWS, 128 * at : 128 * at + 128] = block


def share_kernel(
    data_ref, input_ref, head_ref, tap_ref, column_ref, row_ref, double_ref, share_ref, stack_s, in_s
):
    for at in range(BLOCKS):
        rows = slice(128 * at, 128 * at + 128)
        fine = jnp.dot(double_ref[...], input_ref[at, 0:32, :], preferred_element_type=F32)
        for pair in range(2):
            lanes = slice(128 * pair, 128 * pair + 128)
            in_s[pair, rows, 0:128] = fine[:, lanes].astype(BF16)
            in_s[pair, rows, 128:256] = input_ref[at, 32:160, lanes]

    blocks = [data_ref[at].astype(F32) for at in range(BLOCKS)]
    stack_moved([block[ROWS:48] for block in blocks], stack_s)
    cot = stack_s[...].astype(BF16)
    pre = jnp.concatenate([block[0:ROWS] for block in blocks], axis=1)
    d_hidden = jnp.dot(head_ref[...], cot, preferred_element_type=F32)
    d_pre = (d_hidden * gelu_slope(pre)).astype(BF16).astype(F32)
    hidden = gelu_value(pre).astype(BF16)
    pairs = lax.dot_general(hidden, cot, (((1,), (1,)), ((), ())), preferred_element_type=F32)
    spans = jnp.dot(pairs, column_ref[...], precision=HIGHEST, preferred_element_type=F32)
    depth = lax.broadcasted_iota(jnp.int32, (ROWS, 128), 0) // OWN
    kept = jnp.zeros((ROWS, 128), F32)
    for z in range(SIZE_Z):
        kept = jnp.where(depth == z + 1, spans[:, 128 * z : 128 * z + 128], kept)
    head = jnp.dot(row_ref[...], kept, precision=HIGHEST, preferred_element_type=F32)

    stack_moved([d_pre[:, 128 * at : 128 * at + 128] for at in range(BLOCKS)], stack_s)
    back = stack_s[...].astype(BF16)
    total = jnp.zeros((256, 256), F32)
    for pair in range(2):
        taps = jnp.dot(tap_ref[pair], back, preferred_element_type=F32).astype(BF16)
        total = total + jnp.dot(taps, in_s[pair], preferred_element_type=F32)
    up = total[0:128, 0:128] + total[128:256, 0:128]
    skip = total[0:128, 128:256] + rolled(total[128:256, 128:256], 64)
    half = low_half((32, 128))
    for even in range(0, OWN, 2):
        first, second = slice(32 * even, 32 * even + 32), slice(32 * even + 32, 32 * even + 64)
        turned = rolled(up[second], 64)
        start = 192 * even
        share_ref[:, start : start + 128] = up[first] + head if even == 0 else up[first]
        share_ref[:, start + 128 : start + 256] = jnp.where(half, skip[first], turned)
        share_ref[:, start + 256 : start + 384] = jnp.where(half, turned, rolled(skip[second], 64))


def input_kernel(field_ref, head_ref, weight_ref, skip_ref, coarse_ref, cot_s, pre_s, window_s, sum_s):
    cot_s[:, 0:8, :] = jnp.zeros((12, 8, 128), F32)
    cot_s[:, 8:40, :] = field_ref[:, :, 384:512].astype(F32)
    total = jnp.zeros((240, 384), F32)
    for a in (-1, 0, 1):
        for b in (-1, 0, 1):
            moved = cot_s[1 - a : 11 - a, 8 - b : 32 - b, :].reshape(240, 128).astype(BF16)
            total = total + jnp.dot(
                moved[:, :32], head_ref[3 * (a + 1) + b + 1], preferred_element_type=F32
            )
    pre_wide = field_ref[1:11, :, 0:384].astype(F32)[:, :24].reshape(240, 384)
    d_pre = (total * gelu_slope(pre_wide)).astype(BF16).astype(F32)
    pre_s[...] = d_pre.reshape(10, 24, 384)

    half = low_half((10, 16, 128))
    for b in (-1, 0, 1):
        moved = pre_s[:, 2 - b : 18 - b, :]
        shifted = rolled(moved, 320)
        for z in range(SIZE_Z):
            source, start = (moved, 64 * z) if z % 2 == 0 else (shifted, 64 * z - 64)
            low = source[:, :, start : start + 128]
            high = jnp.where(half, source[:, :, start + 128 : start + 256], 0.0)
            window_s[b + 1, z, :, :, 0:128] = low.astype(BF16)
            window_s[b + 1, z, :, :, 128:256] = high.astype(BF16)

    windows = [
        window_s[b + 1, :, 1 - a : 9 - a].reshape(CELLS, 256)
        for a in (-1, 0, 1)
        for b in (-1, 0, 1)
    ]
    total = jnp.dot(
        jnp.concatenate(windows, axis=1),
        weight_ref[...].reshape(9 * 256, 256),
        preferred_element_type=F32,
    ).reshape(SIZE_Z, SIZE_X, SIZE_Y, 256)
    half = low_half((8, 16, 128))
    for pair in range(2):
        even, odd = total[2 * pair], total[2 * pair + 1]
        lanes = slice(128 * pair, 128 * pair + 128)
        skip_ref[:, :, lanes] = jnp.where(half, even[..., 128:], odd[..., 128:]).astype(BF16)
        both = (even[..., :128] + odd[..., :128]).reshape(4, 2, 16, 128)
        sum_s[...] = (both[:, 0] + both[:, 1]).reshape(64, 128)
        summed = sum_s[pl.ds(0, 32, stride=2), :] + sum_s[pl.ds(1, 32, stride=2), :]
        coarse_ref[:, lanes] = summed.astype(BF16)


def traded(parts, axes):
    return lax.all_to_all(parts, axes, 0, 0)


def spread(part, axes):
    peers = lax.axis_size(axes)
    return traded(jnp.broadcast_to(part[None], (peers, *part.shape)), axes)


def unpacked(shares):
    wide = shares.astype(F32) * NORM
    body = jnp.transpose(wide[:, :27], (1, 0, 2)).reshape(27, C_HID * 192)
    head = wide[:, 27:31, :81].reshape(C_HID, 27, C_VEL)
    return body, jnp.transpose(head, (1, 2, 0))


def per_device(coarse, skip_features, pre_act, cotangent, weight_one, weight_out):
    inputs = plane_inputs(coarse, skip_features)
    head = head_matrix(weight_out)
    pre, cot = depth_rims(pre_act, cotangent)
    data = plane_shares(pre, cot)
    share = pl.pallas_call(
        share_kernel,
        out_shape=jax.ShapeDtypeStruct(SHARE, F32),
        scratch_shapes=[
            pltpu.VMEM((216, 2048), F32),
            pltpu.VMEM((2, 2048, 256), BF16),
        ],
        compiler_params=pltpu.CompilerParams(vmem_limit_bytes=40 * 2**20),
        cost_estimate=pl.CostEstimate(
            flops=1_500_000_000, bytes_accessed=2_000_000, transcendentals=200_000
        ),
    )(data, inputs, own_head_matrix(head), *choices())
    field = side_field(pre, cot)
    near = jnp.sum(traded(share.reshape(4, 8, SHARE[1]), NEAR), axis=0)
    field, near = lax.optimization_barrier((field, near))
    field = with_x_rims(field)
    far = jnp.sum(spread(near.astype(BF16), FAR).astype(F32), axis=0)
    column = spread(far.astype(BF16), NEAR).reshape(SHARE)
    field, column = lax.optimization_barrier((field, column))
    body, head_grad = unpacked(spread(column, PLANE))
    skip_grad, coarse_grad = pl.pallas_call(
        input_kernel,
        out_shape=(
            jax.ShapeDtypeStruct((SIZE_X, SIZE_Y, 256), BF16),
            jax.ShapeDtypeStruct((32, 256), BF16),
        ),
        scratch_shapes=[
            pltpu.VMEM((12, 40, 128), F32),
            pltpu.VMEM((10, 24, 384), F32),
            pltpu.VMEM((3, SIZE_Z, 10, 16, 256), BF16),
            pltpu.VMEM((64, 128), F32),
        ],
        compiler_params=pltpu.CompilerParams(vmem_limit_bytes=32 * 2**20),
        cost_estimate=pl.CostEstimate(
            flops=700_000_000, bytes_accessed=3_000_000, transcendentals=100_000
        ),
    )(with_y_rims(field), head, input_matrix(weight_one))
    return coarse_grad.reshape(4, 8, 256), skip_grad, body, head_grad


def solution(mesh):
    names = ("gx", "gy", "gzh", "gzm", "gzl")
    split = Mesh(mesh.devices.reshape(4, 4, 2, 8, 2), names)
    field = P("gx", "gy", GZ)
    return jax.shard_map(
        per_device,
        mesh=split,
        in_specs=(field, field, field, P(None, "gx", "gy", GZ), P(), P()),
        out_specs=(field, field, P(), P()),
        check_vma=False,
    )
```

time: 134 us -> 133 us (level)
  blocking collectives: 59.3 us -> 0 us
  waiting for transfers between devices: 18 us -> 49.6 us
  starting transfers between devices: 39.4 us -> 57.8 us
  local copies, waits for them, and re-layouts: 9.52 us -> 14.7 us
  Pallas kernels: 3.58 us -> 6.71 us
    all_to_all x4 -> x0, blocking collectives: 59.3 us -> none  [traded(): return lax.all_to_all(parts, axes, 0, 0)]
    all_to_all x1 -> x6, waiting for transfers between devices: 8.46 us -> 40.6 us  [traded(): return lax.all_to_all(parts, axes, 0, 0)]
    all_to_all x1 -> x6, starting transfers between devices: 10.1 us -> 28.5 us  [traded(): return lax.all_to_all(parts, axes, 0, 0)]
    ppermute x3, waiting for transfers between devices: 3.26 us -> 0.01 us  [from_both(): lax.ppermute(to_previous, axis, down)]
    ppermute x3, waiting for transfers between devices: 6.26 us -> 8.99 us  [from_both(): lax.ppermute(to_next, axis, up)]
    broadcast_in_dim x3 -> x4, local copies, waits for them, and re-layouts: 1.01 us -> 3.42 us  [spread(): return traded(jnp.broadcast_to(part[None], (peers, *part.shape)), axes)]
    slice x7 -> x18, local copies, waits for them, and re-layouts: 1.26 us -> 3.4 us  [the longest x5 1.93 us: depth_rims(): low = jnp.concatenate([pre[:64], cot[:6], fill], axis=0)]
    unnamed x10 -> x37, local copies, waits for them, and re-layouts: 1.39 us -> 3.47 us
  transfers between devices with their start and end apart: 7 -> 12, of which waited for: 4 -> 7; matrix products, arithmetic and copies ran while one was open for 2% -> 4% of each run, Pallas kernels for 1% -> 2%
where the time goes in v3:
time: 133 us; the launch traced here: 132 us
  starting transfers between devices  57.8 us (43%)
  waiting for transfers between devices  49.6 us (37%)
  local copies, waits for them, and re-layouts  14.7 us (11%)
  Pallas kernels  6.71 us (5%)
  other arithmetic  2.46 us (2%)
    all_to_all x6, waiting for transfers between devices, traded(): return lax.all_to_all(parts, axes, 0, 0)  40.6 us
    all_to_all x6, starting transfers between devices, traded(): return lax.all_to_all(parts, axes, 0, 0)  28.5 us
    ppermute x3, starting transfers between devices, from_both(): lax.ppermute(to_previous, axis, down)  19.9 us
    ppermute x3, starting transfers between devices, from_both(): lax.ppermute(to_next, axis, up)  9.37 us
    ppermute x3, waiting for transfers between devices, from_both(): lax.ppermute(to_next, axis, up)  8.99 us
    pallas_call x1, Pallas kernels, per_device(): pl.pallas_call(share_kernel, out_shape=jax.ShapeDtypeStruct(SHARE, F32),...  4.16 us
    unnamed x37, local copies, waits for them, and re-layouts  3.47 us
    broadcast_in_dim x4, local copies, waits for them, and re-layouts, spread(): return traded(jnp.broadcast_to(part[None], (peers, *part.shape)), axes)  3.42 us
  transfers between devices with their start and end apart: 12, of which 7 were waited for; matrix products, arithmetic and copies ran while one was open for 4% of the time, Pallas kernels for 2%

profile of v3, /device:TPU:1, one launch (start us, length us, event | category | flops | bytes accessed | tf_op | source)
XLA Modules:
  0.0 132.3 jit_solution(8759202337477065900)
XLA Ops:
  0.7 0.8 fusion.7
  1.5 0.1 slice.60
  1.6 0.1 slice.56
  1.7 0.1 copy.76
  1.8 0.1 copy.78
  2.0 0.9 fusion.5
  2.8 0.1 pad.59.clone
  2.9 0.1 maximum_maximum_fusion.2
  3.0 14.6 %collective-permute-start.1 = (bf16[80,128]{0,1:T(8,128)(2,1)S(1)}, bf16[80,128]{0,1:T(8,128)(2,1)S(1)}, u32[]{:S(2)}, u32[]{:S(2)}) collective-permute-start(bf16[80,128]{0,1:T(8,128)(2,1)S(1)} %get-tuple-element.50), channel_id=1, source_target_pairs={{1,0},{2,1},{3,2},{4,3},{5,4},{6,5},{7,6},{8,7},{9,8},{10,9},{11,1... | collective-permute-start | bytes 61448 | tf_op jit(solution)/shard_map/ppermute | solution.py:47
  17.6 1.9 %collective-permute-start = (bf16[80,128]{0,1:T(8,128)(2,1)S(1)}, bf16[80,128]{0,1:T(8,128)(2,1)S(1)}, u32[]{:S(2)}, u32[]{:S(2)}) collective-permute-start(bf16[80,128]{0,1:T(8,128)(2,1)S(1)} %get-tuple-element.51), channel_id=1, source_target_pairs={{0,1},{1,2},{2,3},{3,4},{4,5},{5,6},{6,7},{7,8},{8,9},{9,10},{10,1... | collective-permute-start | bytes 61448 | tf_op jit(solution)/shard_map/ppermute | solution.py:47
  19.5 0.7 copy.79
  20.3 0.1 reshape.70
  20.4 0.1 slice.79
  20.5 0.1 copy.84
  20.5 5.3 %collective-permute-done = bf16[80,128]{0,1:T(8,128)(2,1)S(1)} collective-permute-done((bf16[80,128]{0,1:T(8,128)(2,1)S(1)}, bf16[80,128]{0,1:T(8,128)(2,1)S(1)}, u32[]{:S(2)}, u32[]{:S(2)}) %collective-permute-start) | collective-permute-done | bytes 20512 | tf_op jit(solution)/shard_map/ppermute | solution.py:47
  25.9 0.1 slice.78
  26.0 0.1 copy.83
  26.0 0.5 copy-done.12
  26.6 0.9 pad_maximum_fusion.2
  27.5 0.1 copy.81
  27.7 0.7 pad_maximum_fusion
  28.4 6.5 %all-to-all-start = ((bf16[16,48,128]{2,1,0:T(8,128)(2,1)}), bf16[16,48,128]{2,1,0:T(8,128)(2,1)S(1)}, u32[]{:S(2)}, u32[]{:S(2)}) async-start(bf16[16,48,128]{2,1,0:T(8,128)(2,1)} %pad_maximum_fusion), calls=%async_computation | async-start | bytes 393216 | tf_op jit(solution)/shard_map/all_to_all | solution.py:269
  35.0 6.7 %all-to-all-done.data_ref = bf16[16,48,128]{2,1,0:T(8,128)(2,1)S(1)} async-done(((bf16[16,48,128]{2,1,0:T(8,128)(2,1)}), bf16[16,48,128]{2,1,0:T(8,128)(2,1)S(1)}, u32[]{:S(2)}, u32[]{:S(2)}) %all-to-all-start) | async-done | bytes 196640 | tf_op jit(solution)/shard_map/all_to_all | solution.py:269
  41.7 1.2 broadcast_in_dim.19
  42.9 4.2 %all-to-all-start.1 = ((bf16[16,160,256]{2,1,0:T(8,128)(2,1)}), bf16[16,160,256]{2,1,0:T(8,128)(2,1)S(1)}, u32[]{:S(2)}, u32[]{:S(2)}) async-start(bf16[16,160,256]{2,1,0:T(8,128)(2,1)} %broadcast_in_dim.19), calls=%async_computation.1 | async-start | bytes 2621440 | tf_op jit(solution)/shard_map/all_to_all | solution.py:269
  47.1 0.0 copy-start.1
  47.2 0.1 fusion.6
  47.3 0.2 concatenate.41.head_ref
  47.5 0.5 copy.86
  48.0 0.1 reshape.79.head_ref
  48.2 17.5 %all-to-all-done.1.input_ref = bf16[16,160,256]{2,1,0:T(8,128)(2,1)S(1)} async-done(((bf16[16,160,256]{2,1,0:T(8,128)(2,1)}), bf16[16,160,256]{2,1,0:T(8,128)(2,1)S(1)}, u32[]{:S(2)}, u32[]{:S(2)}) %all-to-all-start.1) | async-done | bytes 1310752 | tf_op jit(solution)/shard_map/all_to_all | solution.py:269
  65.7 4.2 %shard_map.129 = f32[32,768]{1,0:T(8,128)} custom-call(bf16[16,48,128]{2,1,0:T(8,128)(2,1)S(1)} %all-to-all-done.data_ref, bf16[16,160,256]{2,1,0:T(8,128)(2,1)S(1)} %all-to-all-done.1.input_ref, bf16[24,216]{1,0:T(8,128)(2,1)S(1)} %reshape.79.head_ref, bf16[2,256,216]{2,1,0:T(8,128)(2,1)S(1)} %copy-done.1, f32[216,512]{1,0:T(8,128)S(1)} %copy-done, ...), custom_call_target="tpu_custom_call" | custom-call | flops 1500000000 | bytes 2000000 | tf_op jit(solution)/shard_map/pallas_call | solution.py:289
  69.9 3.3 %all-to-all-start.2 = ((f32[4,8,768]{2,1,0:T(8,128)}), f32[4,8,768]{2,1,0:T(8,128)S(1)}, u32[]{:S(2)}, u32[]{:S(2)}) async-start(f32[4,8,768]{2,1,0:T(8,128)} %bitcast.15), calls=%async_computation.2 | async-start | bytes 196608 | tf_op jit(solution)/shard_map/all_to_all | solution.py:269
  73.2 0.1 copy.80
  73.4 0.1 concatenate.36
  73.5 4.9 %all-to-all-done.2 = f32[4,8,768]{2,1,0:T(8,128)S(1)} async-done(((f32[4,8,768]{2,1,0:T(8,128)}), f32[4,8,768]{2,1,0:T(8,128)S(1)}, u32[]{:S(2)}, u32[]{:S(2)}) %all-to-all-start.2) | async-done | bytes 98336 | tf_op jit(solution)/shard_map/all_to_all | solution.py:269
  78.4 0.6 broadcast_in_dim.20
  79.1 3.4 %all-to-all-start.3 = ((bf16[8,8,768]{2,1,0:T(8,128)(2,1)}), bf16[8,8,768]{2,1,0:T(8,128)(2,1)S(1)}, u32[]{:S(2)}, u32[]{:S(2)}) async-start(bf16[8,8,768]{2,1,0:T(8,128)(2,1)} %broadcast_in_dim.20), calls=%async_computation.3 | async-start | bytes 196608 | tf_op jit(solution)/shard_map/all_to_all | solution.py:269
  82.5 4.2 %collective-permute-start.2 = (bf16[2,16,512]{2,1,0:T(8,128)(2,1)S(1)}, bf16[2,16,512]{2,1,0:T(8,128)(2,1)S(1)}, u32[]{:S(2)}, u32[]{:S(2)}) collective-permute-start(bf16[2,16,512]{2,1,0:T(8,128)(2,1)S(1)} %get-tuple-element.38), channel_id=1, source_target_pairs={{0,128},{128,256},{256,384},{384,0},{1,129},{129,257},{257,385},{3... | collective-permute-start | bytes 98312 | tf_op jit(solution)/shard_map/ppermute | solution.py:47
  86.7 1.9 %collective-permute-start.3 = (bf16[2,16,512]{2,1,0:T(8,128)(2,1)S(1)}, bf16[2,16,512]{2,1,0:T(8,128)(2,1)S(1)}, u32[]{:S(2)}, u32[]{:S(2)}) collective-permute-start(bf16[2,16,512]{2,1,0:T(8,128)(2,1)S(1)} %get-tuple-element.39), channel_id=1, source_target_pairs={{128,0},{256,128},{384,256},{0,384},{129,1},{257,129},{385,257},{1... | collective-permute-start | bytes 98312 | tf_op jit(solution)/shard_map/ppermute | solution.py:47
  88.6 6.4 %all-to-all-done.3 = bf16[8,8,768]{2,1,0:T(8,128)(2,1)S(1)} async-done(((bf16[8,8,768]{2,1,0:T(8,128)(2,1)}), bf16[8,8,768]{2,1,0:T(8,128)(2,1)S(1)}, u32[]{:S(2)}, u32[]{:S(2)}) %all-to-all-start.3) | async-done | bytes 98336 | tf_op jit(solution)/shard_map/all_to_all | solution.py:269
  95.1 0.6 broadcast_in_dim.21
  95.7 3.3 %all-to-all-start.4 = ((bf16[4,8,768]{2,1,0:T(8,128)(2,1)}), bf16[4,8,768]{2,1,0:T(8,128)(2,1)S(1)}, u32[]{:S(2)}, u32[]{:S(2)}) async-start(bf16[4,8,768]{2,1,0:T(8,128)(2,1)} %broadcast_in_dim.21), calls=%async_computation.4 | async-start | bytes 98304 | tf_op jit(solution)/shard_map/all_to_all | solution.py:269
  99.0 5.1 %all-to-all-done.4 = bf16[4,8,768]{2,1,0:T(8,128)(2,1)S(1)} async-done(((bf16[4,8,768]{2,1,0:T(8,128)(2,1)}), bf16[4,8,768]{2,1,0:T(8,128)(2,1)S(1)}, u32[]{:S(2)}, u32[]{:S(2)}) %all-to-all-start.4) | async-done | bytes 49184 | tf_op jit(solution)/shard_map/all_to_all | solution.py:269
  104.1 1.0 broadcast_in_dim.46
  105.1 7.8 %all-to-all-start.5 = ((bf16[16,32,768]{2,1,0:T(8,128)(2,1)}), bf16[16,32,768]{2,1,0:T(8,128)(2,1)S(1)}, u32[]{:S(2)}, u32[]{:S(2)}) async-start(bf16[16,32,768]{2,1,0:T(8,128)(2,1)} %broadcast_in_dim.46), calls=%async_computation.5 | async-start | bytes 1572864 | tf_op jit(solution)/shard_map/all_to_all | solution.py:269
  112.9 1.0 reshape.82
  113.9 0.1 rev.7
  114.0 0.1 slice.81
  114.1 3.3 %collective-permute-start.4 = (bf16[12,2,512]{2,1,0:T(2,128)(2,1)S(1)}, bf16[12,2,512]{2,1,0:T(2,128)(2,1)S(1)}, u32[]{:S(2)}, u32[]{:S(2)}) collective-permute-start(bf16[12,2,512]{2,1,0:T(2,128)(2,1)S(1)} %get-tuple-element.36), channel_id=1, source_target_pairs={{0,32},{32,64},{64,96},{96,0},{1,33},{33,65},{65,97},{97,1},{2,34}... | collective-permute-start | bytes 73736 | tf_op jit(solution)/shard_map/ppermute | solution.py:47
  117.4 3.4 %collective-permute-start.5 = (bf16[12,2,512]{2,1,0:T(2,128)(2,1)S(1)}, bf16[12,2,512]{2,1,0:T(2,128)(2,1)S(1)}, u32[]{:S(2)}, u32[]{:S(2)}) collective-permute-start(bf16[12,2,512]{2,1,0:T(2,128)(2,1)S(1)} %get-tuple-element.37), channel_id=1, source_target_pairs={{32,0},{64,32},{96,64},{0,96},{33,1},{65,33},{97,65},{1,97},{34,2}... | collective-permute-start | bytes 73736 | tf_op jit(solution)/shard_map/ppermute | solution.py:47
  120.8 0.3 fusion.2.weight_ref
  121.1 0.1 pad.40.clone
  121.2 3.7 %collective-permute-done.4 = bf16[12,2,512]{2,1,0:T(2,128)(2,1)S(1)} collective-permute-done((bf16[12,2,512]{2,1,0:T(2,128)(2,1)S(1)}, bf16[12,2,512]{2,1,0:T(2,128)(2,1)S(1)}, u32[]{:S(2)}, u32[]{:S(2)}) %collective-permute-start.4) | collective-permute-done | bytes 24608 | tf_op jit(solution)/shard_map/ppermute | solution.py:47
  124.9 0.2 maximum_maximum_fusion.field_ref
  125.1 2.6 %shard_map.130 = (bf16[8,16,256]{2,1,0:T(8,128)(2,1)}, bf16[32,256]{1,0:T(8,128)(2,1)}) custom-call(bf16[12,32,512]{2,1,0:T(8,128)(2,1)S(1)} %maximum_maximum_fusion.field_ref, bf16[9,32,384]{2,1,0:T(8,128)(2,1)S(1)} %concatenate.41.head_ref, bf16[9,256,256]{2,1,0:T(8,128)(2,1)S(1)} %fusion.2.weight_ref), custom_call_target="tpu_custom_call" | custom-call | flops 700000000 | bytes 3000000 | tf_op jit(solution)/shard_map/pallas_call | solution.py:309
  127.6 0.2 convert_multiply_fusion
  127.8 0.1 slice_bitcast_fusion
  128.0 0.8 copy.88
  128.7 0.2 pad.62
  128.9 2.1 %copy.92 = f32[4,8,16,768]{3,1,2,0:T(8,128)} copy(f32[4,8,16,768]{3,2,1,0:T(8,128)S(1)} %bitcast.39) | data formatting | bytes 3145728
  131.0 0.4 copy.89
  131.4 0.3 reshape.86
  131.7 0.6 copy.90
  (58 shorter events, 0.4 us)
Async XLA Ops:
  0.6 34.3 %copy-start.14 = (bf16[8,16,256]{2,1,0:T(8,128)(2,1)S(1)}, bf16[8,16,256]{2,1,0:T(8,128)(2,1)}, u32[]{:S(2)}) copy-start(bf16[8,16,256]{2,1,0:T(8,128)(2,1)} %param.11) | copy-start | bytes 196612
  0.6 34.3 %copy-start.16 = (bf16[4,8,256]{2,1,0:T(8,128)(2,1)S(1)}, bf16[4,8,256]{2,1,0:T(8,128)(2,1)}, u32[]{:S(2)}) copy-start(bf16[4,8,256]{2,1,0:T(8,128)(2,1)} %param.10) | copy-start | bytes 49156
  3.0 17.4 %collective-permute-start.1 = (bf16[80,128]{0,1:T(8,128)(2,1)S(1)}, bf16[80,128]{0,1:T(8,128)(2,1)S(1)}, u32[]{:S(2)}, u32[]{:S(2)}) collective-permute-start(bf16[80,128]{0,1:T(8,128)(2,1)S(1)} %get-tuple-element.50), channel_id=1, source_target_pairs={{1,0},{2,1},{3,2},{4,3},{5,4},{6,5},{7,6},{8,7},{9,8},{10,9},{11,1... | collective-permute-start | bytes 61448 | tf_op jit(solution)/shard_map/ppermute | solution.py:47
  17.6 8.3 %collective-permute-start = (bf16[80,128]{0,1:T(8,128)(2,1)S(1)}, bf16[80,128]{0,1:T(8,128)(2,1)S(1)}, u32[]{:S(2)}, u32[]{:S(2)}) collective-permute-start(bf16[80,128]{0,1:T(8,128)(2,1)S(1)} %get-tuple-element.51), channel_id=1, source_target_pairs={{0,1},{1,2},{2,3},{3,4},{4,5},{5,6},{6,7},{7,8},{8,9},{9,10},{10,1... | collective-permute-start | bytes 61448 | tf_op jit(solution)/shard_map/ppermute | solution.py:47
  20.4 6.2 %copy-start.6 = (bf16[80,128]{0,1:T(8,128)(2,1)}, bf16[80,128]{0,1:T(8,128)(2,1)S(1)}, u32[]{:S(2)}) copy-start(bf16[80,128]{0,1:T(8,128)(2,1)S(1)} %collective-permute-done.1) | copy-start | bytes 61444
  20.5 6.1 %copy-start.10 = (bf16[6,128]{0,1:T(8,128)(2,1)}, bf16[6,128]{0,1:T(8,128)(2,1)S(1)}, u32[]{:S(2)}) copy-start(bf16[6,128]{0,1:T(8,128)(2,1)S(1)} %slice.79) | copy-start | bytes 4612
  25.9 0.7 copy-start.8
  26.0 0.6 copy-start.12
  28.4 13.2 %all-to-all-start = ((bf16[16,48,128]{2,1,0:T(8,128)(2,1)}), bf16[16,48,128]{2,1,0:T(8,128)(2,1)S(1)}, u32[]{:S(2)}, u32[]{:S(2)}) async-start(bf16[16,48,128]{2,1,0:T(8,128)(2,1)} %pad_maximum_fusion), calls=%async_computation | async-start | bytes 393216 | tf_op jit(solution)/shard_map/all_to_all | solution.py:269
  42.9 4.3 %copy-start.15 = (bf16[27,3,64]{2,0,1:T(8,128)(2,1)S(1)}, bf16[27,3,64]{2,0,1:T(8,128)(2,1)}, u32[]{:S(2)}) copy-start(bf16[27,3,64]{2,0,1:T(8,128)(2,1)} %param.15) | copy-start | bytes 31108
  42.9 22.8 %all-to-all-start.1 = ((bf16[16,160,256]{2,1,0:T(8,128)(2,1)}), bf16[16,160,256]{2,1,0:T(8,128)(2,1)S(1)}, u32[]{:S(2)}, u32[]{:S(2)}) async-start(bf16[16,160,256]{2,1,0:T(8,128)(2,1)} %broadcast_in_dim.19), calls=%async_computation.1 | async-start | bytes 2621440 | tf_op jit(solution)/shard_map/all_to_all | solution.py:269
  47.1 18.6 %copy-start = (f32[216,512]{1,0:T(8,128)S(1)}, f32[216,512]{1,0:T(8,128)}, u32[]{:S(2)}) copy-start(f32[216,512]{1,0:T(8,128)} %constant.38.clone.column_ref) | copy-start | bytes 1327108
  47.1 18.6 %copy-start.1 = (bf16[2,256,216]{2,1,0:T(8,128)(2,1)S(1)}, bf16[2,256,216]{2,1,0:T(8,128)(2,1)}, u32[]{:S(2)}) copy-start(bf16[2,256,216]{2,1,0:T(8,128)(2,1)} %constant.37.clone.tap_ref) | copy-start | bytes 663556
  47.1 18.6 %copy-start.2 = (bf16[128,32]{1,0:T(8,128)(2,1)S(1)}, bf16[128,32]{1,0:T(8,128)(2,1)}, u32[]{:S(2)}) copy-start(bf16[128,32]{1,0:T(8,128)(2,1)} %constant.40.clone.double_ref) | copy-start | bytes 24580
  47.1 18.6 %copy-start.3 = (f32[32,24]{1,0:T(8,128)S(1)}, f32[32,24]{1,0:T(8,128)}, u32[]{:S(2)}) copy-start(f32[32,24]{1,0:T(8,128)} %constant.39.clone.row_ref) | copy-start | bytes 9220
  48.2 25.2 %copy-start.5 = (bf16[8,16,256]{2,1,0:T(8,128)(2,1)S(1)}, bf16[8,16,256]{2,1,0:T(8,128)(2,1)}, u32[]{:S(2)}) copy-start(bf16[8,16,256]{2,1,0:T(8,128)(2,1)} %param.12) | copy-start | bytes 196612
  48.2 25.2 %copy-start.7 = (bf16[80,128]{0,1:T(8,128)(2,1)S(1)}, bf16[80,128]{0,1:T(8,128)(2,1)}, u32[]{:S(2)}) copy-start(bf16[80,128]{0,1:T(8,128)(2,1)} %copy-done.6) | copy-start | bytes 61444
  48.2 25.1 %copy-start.9 = (bf16[80,128]{0,1:T(8,128)(2,1)S(1)}, bf16[80,128]{0,1:T(8,128)(2,1)}, u32[]{:S(2)}) copy-start(bf16[80,128]{0,1:T(8,128)(2,1)} %copy-done.8) | copy-start | bytes 61444
  48.2 25.1 %copy-start.11 = (bf16[6,128]{0,1:T(8,128)(2,1)S(1)}, bf16[6,128]{0,1:T(8,128)(2,1)}, u32[]{:S(2)}) copy-start(bf16[6,128]{0,1:T(8,128)(2,1)} %copy-done.10) | copy-start | bytes 4612
  48.2 25.1 %copy-start.13 = (bf16[6,128]{0,1:T(8,128)(2,1)S(1)}, bf16[6,128]{0,1:T(8,128)(2,1)}, u32[]{:S(2)}) copy-start(bf16[6,128]{0,1:T(8,128)(2,1)} %copy-done.12) | copy-start | bytes 4612
  69.9 8.6 %all-to-all-start.2 = ((f32[4,8,768]{2,1,0:T(8,128)}), f32[4,8,768]{2,1,0:T(8,128)S(1)}, u32[]{:S(2)}, u32[]{:S(2)}) async-start(f32[4,8,768]{2,1,0:T(8,128)} %bitcast.15), calls=%async_computation.2 | async-start | bytes 196608 | tf_op jit(solution)/shard_map/all_to_all | solution.py:269
  79.1 16.0 %all-to-all-start.3 = ((bf16[8,8,768]{2,1,0:T(8,128)(2,1)}), bf16[8,8,768]{2,1,0:T(8,128)(2,1)S(1)}, u32[]{:S(2)}, u32[]{:S(2)}) async-start(bf16[8,8,768]{2,1,0:T(8,128)(2,1)} %broadcast_in_dim.20), calls=%async_computation.3 | async-start | bytes 196608 | tf_op jit(solution)/shard_map/all_to_all | solution.py:269
  82.5 30.4 %copy-start.4 = (bf16[27,12288]{1,0:T(8,128)(2,1)S(1)}, bf16[27,12288]{1,0:T(8,128)(2,1)}, u32[]{:S(2)}) copy-start(bf16[27,12288]{1,0:T(8,128)(2,1)} %param.14) | copy-start | bytes 1990660
  82.5 16.5 %collective-permute-start.2 = (bf16[2,16,512]{2,1,0:T(8,128)(2,1)S(1)}, bf16[2,16,512]{2,1,0:T(8,128)(2,1)S(1)}, u32[]{:S(2)}, u32[]{:S(2)}) collective-permute-start(bf16[2,16,512]{2,1,0:T(8,128)(2,1)S(1)} %get-tuple-element.38), channel_id=1, source_target_pairs={{0,128},{128,256},{256,384},{384,0},{1,129},{129,257},{257,385},{3... | collective-permute-start | bytes 98312 | tf_op jit(solution)/shard_map/ppermute | solution.py:47
  86.7 12.3 %collective-permute-start.3 = (bf16[2,16,512]{2,1,0:T(8,128)(2,1)S(1)}, bf16[2,16,512]{2,1,0:T(8,128)(2,1)S(1)}, u32[]{:S(2)}, u32[]{:S(2)}) collective-permute-start(bf16[2,16,512]{2,1,0:T(8,128)(2,1)S(1)} %get-tuple-element.39), channel_id=1, source_target_pairs={{128,0},{256,128},{384,256},{0,384},{129,1},{257,129},{385,257},{1... | collective-permute-start | bytes 98312 | tf_op jit(solution)/shard_map/ppermute | solution.py:47
  95.7 8.4 %all-to-all-start.4 = ((bf16[4,8,768]{2,1,0:T(8,128)(2,1)}), bf16[4,8,768]{2,1,0:T(8,128)(2,1)S(1)}, u32[]{:S(2)}, u32[]{:S(2)}) async-start(bf16[4,8,768]{2,1,0:T(8,128)(2,1)} %broadcast_in_dim.21), calls=%async_computation.4 | async-start | bytes 98304 | tf_op jit(solution)/shard_map/all_to_all | solution.py:269
  105.1 22.6 %all-to-all-start.5 = ((bf16[16,32,768]{2,1,0:T(8,128)(2,1)}), bf16[16,32,768]{2,1,0:T(8,128)(2,1)S(1)}, u32[]{:S(2)}, u32[]{:S(2)}) async-start(bf16[16,32,768]{2,1,0:T(8,128)(2,1)} %broadcast_in_dim.46), calls=%async_computation.5 | async-start | bytes 1572864 | tf_op jit(solution)/shard_map/all_to_all | solution.py:269
  114.1 10.7 %collective-permute-start.4 = (bf16[12,2,512]{2,1,0:T(2,128)(2,1)S(1)}, bf16[12,2,512]{2,1,0:T(2,128)(2,1)S(1)}, u32[]{:S(2)}, u32[]{:S(2)}) collective-permute-start(bf16[12,2,512]{2,1,0:T(2,128)(2,1)S(1)} %get-tuple-element.36), channel_id=1, source_target_pairs={{0,32},{32,64},{64,96},{96,0},{1,33},{33,65},{65,97},{97,1},{2,34}... | collective-permute-start | bytes 73736 | tf_op jit(solution)/shard_map/ppermute | solution.py:47
  117.4 7.4 %collective-permute-start.5 = (bf16[12,2,512]{2,1,0:T(2,128)(2,1)S(1)}, bf16[12,2,512]{2,1,0:T(2,128)(2,1)S(1)}, u32[]{:S(2)}, u32[]{:S(2)}) collective-permute-start(bf16[12,2,512]{2,1,0:T(2,128)(2,1)S(1)} %get-tuple-element.37), channel_id=1, source_target_pairs={{32,0},{64,32},{96,64},{0,96},{33,1},{65,33},{97,65},{1,97},{34,2}... | collective-permute-start | bytes 73736 | tf_op jit(solution)/shard_map/ppermute | solution.py:47

commit v4 on v3

--- a/solution.py
+++ b/solution.py
@@ -48,31 +48,23 @@
 
 
 def depth_rims(pre_act, cotangent):
-    pre = pre_act.reshape(128, SIZE_Z * C_HID).T
     cot = jnp.transpose(cotangent, (3, 0, 1, 2)).reshape(SIZE_Z * C_VEL, 128)
-    fill = jnp.zeros((10, 128), BF16)
-    high = jnp.concatenate([pre[192:], cot[6:], fill], axis=0)
-    low = jnp.concatenate([pre[:64], cot[:6], fill], axis=0)
+    cot = jnp.pad(cot, ((0, 4), (0, 0)))
+    rows, high, low = pl.pallas_call(
+        turn_kernel,
+        out_shape=(
+            jax.ShapeDtypeStruct((272, 128), BF16),
+            jax.ShapeDtypeStruct((80, 128), BF16),
+            jax.ShapeDtypeStruct((80, 128), BF16),
+        ),
+    )(pre_act.reshape(128, SIZE_Z * C_HID), cot)
     before, after = from_both(high, low, GZ)
-    pre = jnp.concatenate([before[:64], pre, after[:64]], axis=0)
-    cot = jnp.concatenate([before[64:70], cot, after[64:70]], axis=0)
-    return pre, cot
-
-
-def plane_shares(pre, cot):
-    own = jnp.transpose(pre.reshape(6, BLOCKS, OWN, 128), (1, 0, 2, 3)).reshape(BLOCKS, ROWS, 128)
-    parts = jnp.concatenate([own, jnp.broadcast_to(cot[None], (BLOCKS, 24, 128))], axis=1)
-    return traded(parts, PLANE)
+    return before, rows, after
 
 
 def plane_inputs(coarse, skip_features):
     part = jnp.concatenate([coarse.reshape(32, 256), skip_features.reshape(128, 256)], axis=0)
     return spread(part, PLANE)
-
-
-def side_field(pre, cot):
-    fill = jnp.zeros((104, 128), BF16)
-    return jnp.concatenate([pre, cot, fill], axis=0).T.reshape(SIZE_X, SIZE_Y, 512)
 
 
 def with_x_rims(field):
@@ -97,6 +89,22 @@
     split = head[:, :24].reshape(9, 24, 6, BLOCKS, OWN)
     own = lax.dynamic_index_in_dim(split, place, 3, keepdims=False)
     return jnp.transpose(own, (2, 3, 0, 1)).reshape(ROWS, 216)
+
+
+def row_choices():
+    pre_at = lambda z, c: c if z < 0 else 352 + c if z > 3 else 80 + 64 * z + c
+    cot_at = lambda z, o: 76 + 3 * z + o if z < 0 else 404 + 3 * z + o if z > 3 else 336 + 3 * z + o
+    shares = np.zeros((BLOCKS, 48, 432), np.float32)
+    lanes = np.zeros((432, 512), np.float32)
+    for z in range(-1, 5):
+        for c in range(C_HID):
+            shares[c // OWN, OWN * (z + 1) + c % OWN, pre_at(z, c)] = 1.0
+            lanes[pre_at(z, c), C_HID * (z + 1) + c] = 1.0
+    for z in range(-2, 6):
+        for o in range(C_VEL):
+            shares[:, ROWS + C_VEL * (z + 2) + o, cot_at(z, o)] = 1.0
+            lanes[cot_at(z, o), 384 + C_VEL * (z + 2) + o] = 1.0
+    return jnp.asarray(shares.reshape(768, 432), BF16), jnp.asarray(lanes, BF16)
 
 
 def choices():
@@ -109,7 +117,7 @@
                 row = ROWS * pair + OWN * (z + 1 - c) + own
                 tap_rows[z // 2, z % 2, own, tap, row] = 1.0
             for o in range(C_VEL):
-                head_columns[pair, z + 2 - c, o, z, C_VEL * tap + o] = 1.0
+                head_columns[pair, z + 2 - c, o, z, 32 * o + tap] = 1.0
     head_rows = np.zeros((32, 6, OWN), np.float32)
     for own in range(OWN):
         head_rows[27 + own, 1:5, own] = 1.0
@@ -123,6 +131,52 @@
         jnp.asarray(head_rows.reshape(32, ROWS)),
         jnp.asarray(double.reshape(128, 32), BF16),
     )
+
+
+def head_channels():
+    rows = np.zeros((BLOCKS, 32, C_HID), np.float32)
+    for at in range(BLOCKS):
+        for own in range(OWN):
+            rows[at, 27 + own, OWN * at + own] = 1.0
+    return jnp.asarray(rows.reshape(512, C_HID), BF16)
+
+
+def turn_kernel(pre_ref, cot_ref, rows_ref, high_ref, low_ref):
+    turned = pre_ref[...].astype(F32).T.astype(BF16)
+    rows_ref[0:256, :] = turned
+    rows_ref[256:272, :] = cot_ref[...]
+    high_ref[0:64, :] = turned[192:256]
+    high_ref[64:80, :] = cot_ref[...]
+    low_ref[0:64, :] = turned[0:64]
+    low_ref[64:80, :] = cot_ref[...]
+
+
+def joined(before_ref, rows_ref, after_ref):
+    return jnp.concatenate([before_ref[...], rows_ref[...], after_ref[...]], axis=0)
+
+
+def parts_kernel(before_ref, rows_ref, after_ref, choice_ref, parts_ref):
+    rows = joined(before_ref, rows_ref, after_ref)
+    parts = jnp.dot(choice_ref[...], rows, preferred_element_type=F32)
+    parts_ref[...] = parts.astype(BF16).reshape(BLOCKS, 48, 128)
+
+
+def field_kernel(before_ref, rows_ref, after_ref, choice_ref, field_ref):
+    turned = joined(before_ref, rows_ref, after_ref).astype(F32).T.astype(BF16)
+    field = jnp.dot(turned, choice_ref[...], preferred_element_type=F32)
+    field_ref[...] = field.astype(BF16).reshape(SIZE_X, SIZE_Y, 512)
+
+
+def unpack_kernel(share_ref, choice_ref, body_ref, head_ref):
+    for at in range(BLOCKS):
+        wide = share_ref[at].astype(F32) * NORM
+        body_ref[:, 768 * at : 768 * at + 768] = wide[0:27]
+    rows = share_ref[:, :, 0:128].reshape(512, 128)
+    head = lax.dot_general(
+        rows, choice_ref[...], (((0,), (0,)), ((), ())), preferred_element_type=F32
+    )
+    for o in range(C_VEL):
+        head_ref[:, o, :] = head[32 * o : 32 * o + 27] * NORM
 
 
 def input_matrix(weight_one):
@@ -274,18 +328,16 @@
     return traded(jnp.broadcast_to(part[None], (peers, *part.shape)), axes)
 
 
-def unpacked(shares):
-    wide = shares.astype(F32) * NORM
-    body = jnp.transpose(wide[:, :27], (1, 0, 2)).reshape(27, C_HID * 192)
-    head = wide[:, 27:31, :81].reshape(C_HID, 27, C_VEL)
-    return body, jnp.transpose(head, (1, 2, 0))
-
-
 def per_device(coarse, skip_features, pre_act, cotangent, weight_one, weight_out):
     inputs = plane_inputs(coarse, skip_features)
     head = head_matrix(weight_out)
-    pre, cot = depth_rims(pre_act, cotangent)
-    data = plane_shares(pre, cot)
+    deep = depth_rims(pre_act, cotangent)
+    share_choice, field_choice = row_choices()
+    parts = pl.pallas_call(
+        parts_kernel, out_shape=jax.ShapeDtypeStruct((BLOCKS, 48, 128), BF16)
+    )(*deep, share_choice)
+    parts, inputs = lax.optimization_barrier((parts, inputs))
+    data = traded(parts, PLANE)
     share = pl.pallas_call(
         share_kernel,
         out_shape=jax.ShapeDtypeStruct(SHARE, F32),
@@ -298,14 +350,25 @@
             flops=1_500_000_000, bytes_accessed=2_000_000, transcendentals=200_000
         ),
     )(data, inputs, own_head_matrix(head), *choices())
-    field = side_field(pre, cot)
+    deep, share = lax.optimization_barrier((deep, share))
+    field = pl.pallas_call(
+        field_kernel, out_shape=jax.ShapeDtypeStruct((SIZE_X, SIZE_Y, 512), BF16)
+    )(*deep, field_choice)
+    field = with_x_rims(field)
     near = jnp.sum(traded(share.reshape(4, 8, SHARE[1]), NEAR), axis=0)
     field, near = lax.optimization_barrier((field, near))
-    field = with_x_rims(field)
+    field = with_y_rims(field)
     far = jnp.sum(spread(near.astype(BF16), FAR).astype(F32), axis=0)
     column = spread(far.astype(BF16), NEAR).reshape(SHARE)
     field, column = lax.optimization_barrier((field, column))
-    body, head_grad = unpacked(spread(column, PLANE))
+    body, head_grad = pl.pallas_call(
+        unpack_kernel,
+        out_shape=(
+            jax.ShapeDtypeStruct((27, C_HID * 192), F32),
+            jax.ShapeDtypeStruct((27, C_VEL, C_HID), F32),
+        ),
+        compiler_params=pltpu.CompilerParams(vmem_limit_bytes=16 * 2**20),
+    )(spread(column, PLANE), head_channels())
     skip_grad, coarse_grad = pl.pallas_call(
         input_kernel,
         out_shape=(
@@ -322,7 +385,7 @@
         cost_estimate=pl.CostEstimate(
             flops=700_000_000, bytes_accessed=3_000_000, transcendentals=100_000
         ),
-    )(with_y_rims(field), head, input_matrix(weight_one))
+    )(field, head, input_matrix(weight_one))
     return coarse_grad.reshape(4, 8, 256), skip_grad, body, head_grad
 
 

time: 133 us -> 122 us (0.917)
  waiting for transfers between devices: 49.6 us -> 30 us
  Pallas kernels: 6.71 us -> 14 us
  starting transfers between devices: 57.8 us -> 65 us
  local copies, waits for them, and re-layouts: 14.7 us -> 8.4 us
    all_to_all x6, starting transfers between devices: 28.5 us -> 42.3 us  [traded(): return lax.all_to_all(parts, axes, 0, 0)]
    all_to_all x6, waiting for transfers between devices: 40.6 us -> 28 us  [traded(): return lax.all_to_all(parts, axes, 0, 0)]
    ppermute x3, waiting for transfers between devices: 8.99 us -> 1 us  [from_both(): lax.ppermute(to_next, axis, up)]
    pallas_call x0 -> x4, Pallas kernels: none -> 7.31 us  [the longest x1 2.27 us: per_device(): pl.pallas_call(parts_kernel, out_shape=jax.ShapeDtypeStruct((BLOCKS, 48,...]
    ppermute x3, starting transfers between devices: 19.9 us -> 14.9 us  [from_both(): lax.ppermute(to_previous, axis, down)]
    slice x14 -> x0, local copies, waits for them, and re-layouts: 2.88 us -> none  [the longest x5 1.93 us: depth_rims(): low = jnp.concatenate([pre[:64], cot[:6], fill], axis=0)]
    unnamed x37 -> x21, local copies, waits for them, and re-layouts: 3.47 us -> 1.28 us
    concatenate x4 -> x0, other arithmetic: 1.75 us -> none  [the longest x1 0.94 us: depth_rims(): pre = jnp.concatenate([before[:64], pre, after[:64]], axis=0)]
  transfers between devices with their start and end apart: 12 -> 12, of which waited for: 7 -> 7; matrix products, arithmetic and copies ran while one was open for 4% -> 5% of each run, Pallas kernels for 2% -> 7%
where the time goes in v4:
time: 122 us; the launch traced here: 121 us
  starting transfers between devices  65 us (53%)
  waiting for transfers between devices  30 us (25%)
  Pallas kernels  14 us (11%)
  local copies, waits for them, and re-layouts  8.4 us (7%)
  other arithmetic  2.3 us (2%)
    all_to_all x6, starting transfers between devices, traded(): return lax.all_to_all(parts, axes, 0, 0)  42.3 us
    all_to_all x6, waiting for transfers between devices, traded(): return lax.all_to_all(parts, axes, 0, 0)  28 us
    ppermute x3, starting transfers between devices, from_both(): lax.ppermute(to_previous, axis, down)  14.9 us
    ppermute x3, starting transfers between devices, from_both(): lax.ppermute(to_next, axis, up)  7.75 us
    pallas_call x1, Pallas kernels, per_device(): pl.pallas_call(share_kernel, out_shape=jax.ShapeDtypeStruct(SHARE, F32),...  4.16 us
    broadcast_in_dim x4, local copies, waits for them, and re-layouts, spread(): return traded(jnp.broadcast_to(part[None], (peers, *part.shape)), axes)  3.42 us
    pallas_call x1, Pallas kernels, per_device(): pl.pallas_call(input_kernel, out_shape=(jax.ShapeDtypeStruct((SIZE_X, SIZ...  2.55 us
  transfers between devices with their start and end apart: 12, of which 7 were waited for; matrix products, arithmetic and copies ran while one was open for 5% of the time, Pallas kernels for 7%

profile of v4, /device:TPU:1, one launch (start us, length us, event | category | flops | bytes accessed | tf_op | source)
XLA Modules:
  0.0 120.6 jit_solution(6150735569864341520)
XLA Ops:
  0.6 0.8 pad_maximum_fusion.1
  1.5 1.2 broadcast_in_dim.10
  2.7 10.5 %all-to-all-start = ((bf16[16,160,256]{2,1,0:T(8,128)(2,1)}), bf16[16,160,256]{2,1,0:T(8,128)(2,1)S(1)}, u32[]{:S(2)}, u32[]{:S(2)}) async-start(bf16[16,160,256]{2,1,0:T(8,128)(2,1)} %broadcast_in_dim.10), calls=%async_computation | async-start | bytes 2621440 | tf_op jit(solution)/shard_map/all_to_all | solution.py:323
  13.2 0.0 copy-done.8
  13.2 0.1 reshape.52
  13.3 0.6 pad.32.cot_ref
  13.9 1.6 %shard_map.156 = (bf16[272,128]{1,0:T(8,128)(2,1)}, bf16[80,128]{1,0:T(8,128)(2,1)}, bf16[80,128]{1,0:T(8,128)(2,1)}) custom-call(bf16[128,256]{1,0:T(8,128)(2,1)} %bitcast.22, bf16[16,128]{1,0:T(8,128)(2,1)} %pad.32.cot_ref), custom_call_target="tpu_custom_call" | custom-call | tf_op jit(solution)/shard_map/pallas_call | solution.py:53
  15.5 1.9 %collective-permute-start = (bf16[80,128]{1,0:T(8,128)(2,1)}, bf16[80,128]{1,0:T(8,128)(2,1)S(1)}, u32[]{:S(2)}, u32[]{:S(2)}) collective-permute-start(bf16[80,128]{1,0:T(8,128)(2,1)} %get-tuple-element.21), channel_id=1, source_target_pairs={{0,1},{1,2},{2,3},{3,4},{4,5},{5,6},{6,7},{7,8},{8,9},{9,10},{10,1... | collective-permute-start | bytes 61448 | tf_op jit(solution)/shard_map/ppermute | solution.py:47
  17.4 9.9 %collective-permute-start.1 = (bf16[80,128]{1,0:T(8,128)(2,1)}, bf16[80,128]{1,0:T(8,128)(2,1)S(1)}, u32[]{:S(2)}, u32[]{:S(2)}) collective-permute-start(bf16[80,128]{1,0:T(8,128)(2,1)} %get-tuple-element.23), channel_id=1, source_target_pairs={{1,0},{2,1},{3,2},{4,3},{5,4},{6,5},{7,6},{8,7},{9,8},{10,9},{11,1... | collective-permute-start | bytes 61448 | tf_op jit(solution)/shard_map/ppermute | solution.py:47
  27.3 0.0 copy-done.9
  27.4 0.0 collective-permute-done.before_ref
  27.4 0.0 copy-start.6
  27.4 1.0 collective-permute-done.1.after_ref
  28.4 0.0 copy-done.6
  28.4 0.6 copy-done.7
  29.0 2.3 %shard_map.157 = bf16[16,48,128]{2,1,0:T(8,128)(2,1)} custom-call(bf16[80,128]{1,0:T(8,128)(2,1)} %copy-done.6, bf16[272,128]{1,0:T(8,128)(2,1)} %get-tuple-element.27.rows_ref, bf16[80,128]{1,0:T(8,128)(2,1)} %copy-done.7, bf16[768,432]{1,0:T(8,128)(2,1)} %constant.39.clone.choice_ref), custom_call_target="tpu_custom_call" | custom-call | tf_op jit(solution)/shard_map/pallas_call | solution.py:336
  31.3 0.9 all-to-all-done.input_ref
  32.3 5.0 %all-to-all-start.1 = ((bf16[16,48,128]{2,1,0:T(8,128)(2,1)}), bf16[16,48,128]{2,1,0:T(8,128)(2,1)S(1)}, u32[]{:S(2)}, u32[]{:S(2)}) async-start(bf16[16,48,128]{2,1,0:T(8,128)(2,1)} %shard_map.157), calls=%async_computation.1 | async-start | bytes 393216 | tf_op jit(solution)/shard_map/all_to_all | solution.py:323
  37.3 0.1 fusion.5
  37.3 0.0 copy-start.1
  37.4 0.0 copy-start.2
  37.4 0.0 copy-start.3
  37.4 0.0 copy-start.4
  37.4 0.2 concatenate.16.head_ref
  37.6 0.4 copy.27
  38.1 0.1 reshape.58.head_ref
  38.2 5.8 %all-to-all-done.1.data_ref = bf16[16,48,128]{2,1,0:T(8,128)(2,1)S(1)} async-done(((bf16[16,48,128]{2,1,0:T(8,128)(2,1)}), bf16[16,48,128]{2,1,0:T(8,128)(2,1)S(1)}, u32[]{:S(2)}, u32[]{:S(2)}) %all-to-all-start.1) | async-done | bytes 196640 | tf_op jit(solution)/shard_map/all_to_all | solution.py:323
  44.0 0.0 copy-done.1
  44.0 0.0 copy-done.2
  44.0 0.0 copy-done.3
  44.0 4.2 %shard_map.158 = f32[32,768]{1,0:T(8,128)} custom-call(bf16[16,48,128]{2,1,0:T(8,128)(2,1)S(1)} %all-to-all-done.1.data_ref, bf16[16,160,256]{2,1,0:T(8,128)(2,1)S(1)} %all-to-all-done.input_ref, bf16[24,216]{1,0:T(8,128)(2,1)S(1)} %reshape.58.head_ref, bf16[2,256,216]{2,1,0:T(8,128)(2,1)S(1)} %copy-done.2, f32[216,512]{1,0:T(8,128)S(1)} %copy-done.1, ...), custom_call_target="tpu_custom_call" | custom-call | flops 1500000000 | bytes 2000000 | tf_op jit(solution)/shard_map/pallas_call | solution.py:341
  48.1 3.3 %all-to-all-start.2 = ((f32[4,8,768]{2,1,0:T(8,128)}), f32[4,8,768]{2,1,0:T(8,128)S(1)}, u32[]{:S(2)}, u32[]{:S(2)}) async-start(f32[4,8,768]{2,1,0:T(8,128)} %bitcast.8), calls=%async_computation.2 | async-start | bytes 196608 | tf_op jit(solution)/shard_map/all_to_all | solution.py:323
  51.5 2.0 %shard_map.159 = bf16[8,16,512]{2,1,0:T(8,128)(2,1)} custom-call(bf16[80,128]{1,0:T(8,128)(2,1)} %copy-done.6, bf16[272,128]{1,0:T(8,128)(2,1)} %get-tuple-element.27.rows_ref, bf16[80,128]{1,0:T(8,128)(2,1)} %copy-done.7, bf16[432,512]{1,0:T(8,128)(2,1)} %constant.40.clone.choice_ref), custom_call_target="tpu_custom_call" | custom-call | tf_op jit(solution)/shard_map/pallas_call | solution.py:354
  53.5 0.8 fusion.4
  54.3 2.5 %collective-permute-start.3 = (bf16[2,16,512]{2,1,0:T(8,128)(2,1)S(1)}, bf16[2,16,512]{2,1,0:T(8,128)(2,1)S(1)}, u32[]{:S(2)}, u32[]{:S(2)}) collective-permute-start(bf16[2,16,512]{2,1,0:T(8,128)(2,1)S(1)} %get-tuple-element.53), channel_id=1, source_target_pairs={{128,0},{256,128},{384,256},{0,384},{129,1},{257,129},{385,257},{1... | collective-permute-start | bytes 98312 | tf_op jit(solution)/shard_map/ppermute | solution.py:47
  56.7 3.1 %collective-permute-start.2 = (bf16[2,16,512]{2,1,0:T(8,128)(2,1)S(1)}, bf16[2,16,512]{2,1,0:T(8,128)(2,1)S(1)}, u32[]{:S(2)}, u32[]{:S(2)}) collective-permute-start(bf16[2,16,512]{2,1,0:T(8,128)(2,1)S(1)} %get-tuple-element.52), channel_id=1, source_target_pairs={{0,128},{128,256},{256,384},{384,0},{1,129},{129,257},{257,385},{3... | collective-permute-start | bytes 98312 | tf_op jit(solution)/shard_map/ppermute | solution.py:47
  59.8 0.0 collective-permute-done.3
  59.9 1.0 collective-permute-done.2
  60.8 0.9 pad_maximum_fusion
  61.8 0.0 all-to-all-done.2
  61.8 0.6 broadcast_in_dim.12
  62.5 10.9 %all-to-all-start.3 = ((bf16[8,8,768]{2,1,0:T(8,128)(2,1)}), bf16[8,8,768]{2,1,0:T(8,128)(2,1)S(1)}, u32[]{:S(2)}, u32[]{:S(2)}) async-start(bf16[8,8,768]{2,1,0:T(8,128)(2,1)} %broadcast_in_dim.12), calls=%async_computation.3 | async-start | bytes 196608 | tf_op jit(solution)/shard_map/all_to_all | solution.py:323
  73.4 2.5 %collective-permute-start.5 = (bf16[12,2,512]{2,1,0:T(2,128)(2,1)S(1)}, bf16[12,2,512]{2,1,0:T(2,128)(2,1)S(1)}, u32[]{:S(2)}, u32[]{:S(2)}) collective-permute-start(bf16[12,2,512]{2,1,0:T(2,128)(2,1)S(1)} %get-tuple-element.51), channel_id=1, source_target_pairs={{32,0},{64,32},{96,64},{0,96},{33,1},{65,33},{97,65},{1,97},{34,2}... | collective-permute-start | bytes 73736 | tf_op jit(solution)/shard_map/ppermute | solution.py:47
  75.9 2.7 %collective-permute-start.4 = (bf16[12,2,512]{2,1,0:T(2,128)(2,1)S(1)}, bf16[12,2,512]{2,1,0:T(2,128)(2,1)S(1)}, u32[]{:S(2)}, u32[]{:S(2)}) collective-permute-start(bf16[12,2,512]{2,1,0:T(2,128)(2,1)S(1)} %get-tuple-element.50), channel_id=1, source_target_pairs={{0,32},{32,64},{64,96},{96,0},{1,33},{33,65},{65,97},{97,1},{2,34}... | collective-permute-start | bytes 73736 | tf_op jit(solution)/shard_map/ppermute | solution.py:47
  78.7 0.1 pad.45.clone
  78.8 7.6 %all-to-all-done.3 = bf16[8,8,768]{2,1,0:T(8,128)(2,1)S(1)} async-done(((bf16[8,8,768]{2,1,0:T(8,128)(2,1)}), bf16[8,8,768]{2,1,0:T(8,128)(2,1)S(1)}, u32[]{:S(2)}, u32[]{:S(2)}) %all-to-all-start.3) | async-done | bytes 98336 | tf_op jit(solution)/shard_map/all_to_all | solution.py:323
  86.4 0.6 broadcast_in_dim.13
  87.0 4.5 %all-to-all-start.4 = ((bf16[4,8,768]{2,1,0:T(8,128)(2,1)}), bf16[4,8,768]{2,1,0:T(8,128)(2,1)S(1)}, u32[]{:S(2)}, u32[]{:S(2)}) async-start(bf16[4,8,768]{2,1,0:T(8,128)(2,1)} %broadcast_in_dim.13), calls=%async_computation.4 | async-start | bytes 98304 | tf_op jit(solution)/shard_map/all_to_all | solution.py:323
  91.5 0.0 collective-permute-done.5
  91.5 0.0 collective-permute-done.4
  91.5 0.2 maximum_maximum_fusion.field_ref
  91.7 0.0 copy-start.5
  91.7 4.9 %all-to-all-done.4 = bf16[4,8,768]{2,1,0:T(8,128)(2,1)S(1)} async-done(((bf16[4,8,768]{2,1,0:T(8,128)(2,1)}), bf16[4,8,768]{2,1,0:T(8,128)(2,1)S(1)}, u32[]{:S(2)}, u32[]{:S(2)}) %all-to-all-start.4) | async-done | bytes 49184 | tf_op jit(solution)/shard_map/all_to_all | solution.py:323
  96.7 1.0 broadcast_in_dim.14
  97.6 8.1 %all-to-all-start.5 = ((bf16[16,32,768]{2,1,0:T(8,128)(2,1)}), bf16[16,32,768]{2,1,0:T(8,128)(2,1)S(1)}, u32[]{:S(2)}, u32[]{:S(2)}) async-start(bf16[16,32,768]{2,1,0:T(8,128)(2,1)} %broadcast_in_dim.14), calls=%async_computation.5 | async-start | bytes 1572864 | tf_op jit(solution)/shard_map/all_to_all | solution.py:323
  105.7 1.0 reshape.61
  106.8 0.1 rev.7
  106.9 0.1 slice.27
  106.9 0.3 fusion.2.weight_ref
  107.2 0.0 copy-start
  107.3 2.6 %shard_map.160 = (bf16[8,16,256]{2,1,0:T(8,128)(2,1)}, bf16[32,256]{1,0:T(8,128)(2,1)}) custom-call(bf16[12,32,512]{2,1,0:T(8,128)(2,1)S(1)} %maximum_maximum_fusion.field_ref, bf16[9,32,384]{2,1,0:T(8,128)(2,1)S(1)} %concatenate.16.head_ref, bf16[9,256,256]{2,1,0:T(8,128)(2,1)S(1)} %fusion.2.weight_ref), custom_call_target="tpu_custom_call" | custom-call | flops 700000000 | bytes 3000000 | tf_op jit(solution)/shard_map/pallas_call | solution.py:372
  109.8 8.7 %all-to-all-done.5.share_ref = bf16[16,32,768]{2,1,0:T(8,128)(2,1)S(1)} async-done(((bf16[16,32,768]{2,1,0:T(8,128)(2,1)}), bf16[16,32,768]{2,1,0:T(8,128)(2,1)S(1)}, u32[]{:S(2)}, u32[]{:S(2)}) %all-to-all-start.5) | async-done | bytes 786464 | tf_op jit(solution)/shard_map/all_to_all | solution.py:323
  118.5 1.4 %shard_map.161 = (f32[27,12288]{1,0:T(8,128)}, f32[27,3,64]{2,1,0:T(4,128)S(1)}) custom-call(bf16[16,32,768]{2,1,0:T(8,128)(2,1)S(1)} %all-to-all-done.5.share_ref, bf16[512,64]{1,0:T(8,128)(2,1)S(1)} %copy-done), custom_call_target="tpu_custom_call" | custom-call | tf_op jit(solution)/shard_map/pallas_call | solution.py:364
  120.0 0.6 copy.29
  (17 shorter events, 0.2 us)
Async XLA Ops:
  2.7 10.5 %copy-start.8 = (bf16[3,8,16,4]{2,3,1,0:T(4,128)(2,1)S(1)}, bf16[3,8,16,4]{2,3,1,0:T(4,128)(2,1)}, u32[]{:S(2)}) copy-start(bf16[3,8,16,4]{2,3,1,0:T(4,128)(2,1)} %param.16) | copy-start | bytes 9220
  2.7 24.7 %copy-start.9 = (bf16[27,3,64]{2,0,1:T(8,128)(2,1)S(1)}, bf16[27,3,64]{2,0,1:T(8,128)(2,1)}, u32[]{:S(2)}) copy-start(bf16[27,3,64]{2,0,1:T(8,128)(2,1)} %param.18) | copy-start | bytes 31108
  2.7 29.6 %all-to-all-start = ((bf16[16,160,256]{2,1,0:T(8,128)(2,1)}), bf16[16,160,256]{2,1,0:T(8,128)(2,1)S(1)}, u32[]{:S(2)}, u32[]{:S(2)}) async-start(bf16[16,160,256]{2,1,0:T(8,128)(2,1)} %broadcast_in_dim.10), calls=%async_computation | async-start | bytes 2621440 | tf_op jit(solution)/shard_map/all_to_all | solution.py:323
  15.5 11.9 %collective-permute-start = (bf16[80,128]{1,0:T(8,128)(2,1)}, bf16[80,128]{1,0:T(8,128)(2,1)S(1)}, u32[]{:S(2)}, u32[]{:S(2)}) collective-permute-start(bf16[80,128]{1,0:T(8,128)(2,1)} %get-tuple-element.21), channel_id=1, source_target_pairs={{0,1},{1,2},{2,3},{3,4},{4,5},{5,6},{6,7},{7,8},{8,9},{9,10},{10,1... | collective-permute-start | bytes 61448 | tf_op jit(solution)/shard_map/ppermute | solution.py:47
  17.4 11.0 %collective-permute-start.1 = (bf16[80,128]{1,0:T(8,128)(2,1)}, bf16[80,128]{1,0:T(8,128)(2,1)S(1)}, u32[]{:S(2)}, u32[]{:S(2)}) collective-permute-start(bf16[80,128]{1,0:T(8,128)(2,1)} %get-tuple-element.23), channel_id=1, source_target_pairs={{1,0},{2,1},{3,2},{4,3},{5,4},{6,5},{7,6},{8,7},{9,8},{10,9},{11,1... | collective-permute-start | bytes 61448 | tf_op jit(solution)/shard_map/ppermute | solution.py:47
  27.4 1.0 copy-start.6
  28.4 0.6 copy-start.7
  32.3 11.7 %all-to-all-start.1 = ((bf16[16,48,128]{2,1,0:T(8,128)(2,1)}), bf16[16,48,128]{2,1,0:T(8,128)(2,1)S(1)}, u32[]{:S(2)}, u32[]{:S(2)}) async-start(bf16[16,48,128]{2,1,0:T(8,128)(2,1)} %shard_map.157), calls=%async_computation.1 | async-start | bytes 393216 | tf_op jit(solution)/shard_map/all_to_all | solution.py:323
  37.3 6.6 %copy-start.1 = (f32[216,512]{1,0:T(8,128)S(1)}, f32[216,512]{1,0:T(8,128)}, u32[]{:S(2)}) copy-start(f32[216,512]{1,0:T(8,128)} %constant.42.clone.column_ref) | copy-start | bytes 1327108
  37.4 6.6 %copy-start.2 = (bf16[2,256,216]{2,1,0:T(8,128)(2,1)S(1)}, bf16[2,256,216]{2,1,0:T(8,128)(2,1)}, u32[]{:S(2)}) copy-start(bf16[2,256,216]{2,1,0:T(8,128)(2,1)} %constant.41.clone.tap_ref) | copy-start | bytes 663556
  37.4 6.6 %copy-start.3 = (bf16[128,32]{1,0:T(8,128)(2,1)S(1)}, bf16[128,32]{1,0:T(8,128)(2,1)}, u32[]{:S(2)}) copy-start(bf16[128,32]{1,0:T(8,128)(2,1)} %constant.44.clone.double_ref) | copy-start | bytes 24580
  37.4 6.6 %copy-start.4 = (f32[32,24]{1,0:T(8,128)S(1)}, f32[32,24]{1,0:T(8,128)}, u32[]{:S(2)}) copy-start(f32[32,24]{1,0:T(8,128)} %constant.43.clone.row_ref) | copy-start | bytes 9220
  48.1 13.6 %all-to-all-start.2 = ((f32[4,8,768]{2,1,0:T(8,128)}), f32[4,8,768]{2,1,0:T(8,128)S(1)}, u32[]{:S(2)}, u32[]{:S(2)}) async-start(f32[4,8,768]{2,1,0:T(8,128)} %bitcast.8), calls=%async_computation.2 | async-start | bytes 196608 | tf_op jit(solution)/shard_map/all_to_all | solution.py:323
  54.3 5.6 %collective-permute-start.3 = (bf16[2,16,512]{2,1,0:T(8,128)(2,1)S(1)}, bf16[2,16,512]{2,1,0:T(8,128)(2,1)S(1)}, u32[]{:S(2)}, u32[]{:S(2)}) collective-permute-start(bf16[2,16,512]{2,1,0:T(8,128)(2,1)S(1)} %get-tuple-element.53), channel_id=1, source_target_pairs={{128,0},{256,128},{384,256},{0,384},{129,1},{257,129},{385,257},{1... | collective-permute-start | bytes 98312 | tf_op jit(solution)/shard_map/ppermute | solution.py:47
  56.7 4.1 %collective-permute-start.2 = (bf16[2,16,512]{2,1,0:T(8,128)(2,1)S(1)}, bf16[2,16,512]{2,1,0:T(8,128)(2,1)S(1)}, u32[]{:S(2)}, u32[]{:S(2)}) collective-permute-start(bf16[2,16,512]{2,1,0:T(8,128)(2,1)S(1)} %get-tuple-element.52), channel_id=1, source_target_pairs={{0,128},{128,256},{256,384},{384,0},{1,129},{129,257},{257,385},{3... | collective-permute-start | bytes 98312 | tf_op jit(solution)/shard_map/ppermute | solution.py:47
  62.5 23.9 %all-to-all-start.3 = ((bf16[8,8,768]{2,1,0:T(8,128)(2,1)}), bf16[8,8,768]{2,1,0:T(8,128)(2,1)S(1)}, u32[]{:S(2)}, u32[]{:S(2)}) async-start(bf16[8,8,768]{2,1,0:T(8,128)(2,1)} %broadcast_in_dim.12), calls=%async_computation.3 | async-start | bytes 196608 | tf_op jit(solution)/shard_map/all_to_all | solution.py:323
  73.4 18.1 %collective-permute-start.5 = (bf16[12,2,512]{2,1,0:T(2,128)(2,1)S(1)}, bf16[12,2,512]{2,1,0:T(2,128)(2,1)S(1)}, u32[]{:S(2)}, u32[]{:S(2)}) collective-permute-start(bf16[12,2,512]{2,1,0:T(2,128)(2,1)S(1)} %get-tuple-element.51), channel_id=1, source_target_pairs={{32,0},{64,32},{96,64},{0,96},{33,1},{65,33},{97,65},{1,97},{34,2}... | collective-permute-start | bytes 73736 | tf_op jit(solution)/shard_map/ppermute | solution.py:47
  75.9 15.6 %collective-permute-start.4 = (bf16[12,2,512]{2,1,0:T(2,128)(2,1)S(1)}, bf16[12,2,512]{2,1,0:T(2,128)(2,1)S(1)}, u32[]{:S(2)}, u32[]{:S(2)}) collective-permute-start(bf16[12,2,512]{2,1,0:T(2,128)(2,1)S(1)} %get-tuple-element.50), channel_id=1, source_target_pairs={{0,32},{32,64},{64,96},{96,0},{1,33},{33,65},{65,97},{97,1},{2,34}... | collective-permute-start | bytes 73736 | tf_op jit(solution)/shard_map/ppermute | solution.py:47
  87.0 9.6 %all-to-all-start.4 = ((bf16[4,8,768]{2,1,0:T(8,128)(2,1)}), bf16[4,8,768]{2,1,0:T(8,128)(2,1)S(1)}, u32[]{:S(2)}, u32[]{:S(2)}) async-start(bf16[4,8,768]{2,1,0:T(8,128)(2,1)} %broadcast_in_dim.13), calls=%async_computation.4 | async-start | bytes 98304 | tf_op jit(solution)/shard_map/all_to_all | solution.py:323
  91.7 14.0 %copy-start.5 = (bf16[27,12288]{1,0:T(8,128)(2,1)S(1)}, bf16[27,12288]{1,0:T(8,128)(2,1)}, u32[]{:S(2)}) copy-start(bf16[27,12288]{1,0:T(8,128)(2,1)} %param.17) | copy-start | bytes 1990660
  97.6 20.9 %all-to-all-start.5 = ((bf16[16,32,768]{2,1,0:T(8,128)(2,1)}), bf16[16,32,768]{2,1,0:T(8,128)(2,1)S(1)}, u32[]{:S(2)}, u32[]{:S(2)}) async-start(bf16[16,32,768]{2,1,0:T(8,128)(2,1)} %broadcast_in_dim.14), calls=%async_computation.5 | async-start | bytes 1572864 | tf_op jit(solution)/shard_map/all_to_all | solution.py:323
  107.2 11.3 %copy-start = (bf16[512,64]{1,0:T(8,128)(2,1)S(1)}, bf16[512,64]{1,0:T(8,128)(2,1)}, u32[]{:S(2)}) copy-start(bf16[512,64]{1,0:T(8,128)(2,1)} %constant.45.clone.choice_ref) | copy-start | bytes 196612

commit v5 on v4

--- a/solution.py
+++ b/solution.py
@@ -63,8 +63,10 @@
 
 
 def plane_inputs(coarse, skip_features):
-    part = jnp.concatenate([coarse.reshape(32, 256), skip_features.reshape(128, 256)], axis=0)
-    return spread(part, PLANE)
+    parts = pl.pallas_call(
+        message_kernel, out_shape=jax.ShapeDtypeStruct((BLOCKS, 160, 256), BF16)
+    )(coarse.reshape(32, 256), skip_features.reshape(128, 256))
+    return traded(parts, PLANE)
 
 
 def with_x_rims(field):
@@ -126,11 +128,10 @@
         for y in range(SIZE_Y):
             double[x, y, x // 2, y // 2] = 1.0
     return (
-        jnp.asarray(tap_rows.reshape(2, 256, 216), BF16),
+        jnp.asarray(tap_rows.reshape(2, 256, 216)),
         jnp.asarray(head_columns.reshape(216, 512)),
         jnp.asarray(head_rows.reshape(32, ROWS)),
-        jnp.asarray(double.reshape(128, 32), BF16),
-    )
+    ), jnp.asarray(double.reshape(128, 32), BF16)
 
 
 def head_channels():
@@ -229,17 +230,23 @@
                 stack_ref[start : start + ROWS, 128 * at : 128 * at + 128] = block
 
 
-def share_kernel(
-    data_ref, input_ref, head_ref, tap_ref, column_ref, row_ref, double_ref, share_ref, stack_s, in_s
-):
+def message_kernel(coarse_ref, skip_ref, parts_ref):
+    for at in range(BLOCKS):
+        parts_ref[at, 0:32, :] = coarse_ref[...]
+        parts_ref[at, 32:160, :] = skip_ref[...]
+
+
+def fine_kernel(input_ref, double_ref, fine_ref):
     for at in range(BLOCKS):
         rows = slice(128 * at, 128 * at + 128)
         fine = jnp.dot(double_ref[...], input_ref[at, 0:32, :], preferred_element_type=F32)
         for pair in range(2):
             lanes = slice(128 * pair, 128 * pair + 128)
-            in_s[pair, rows, 0:128] = fine[:, lanes].astype(BF16)
-            in_s[pair, rows, 128:256] = input_ref[at, 32:160, lanes]
-
+            fine_ref[pair, rows, 0:128] = fine[:, lanes].astype(BF16)
+            fine_ref[pair, rows, 128:256] = input_ref[at, 32:160, lanes]
+
+
+def share_kernel(data_ref, fine_ref, head_ref, tap_ref, column_ref, row_ref, share_ref, stack_s):
     blocks = [data_ref[at].astype(F32) for at in range(BLOCKS)]
     stack_moved([block[ROWS:48] for block in blocks], stack_s)
     cot = stack_s[...].astype(BF16)
@@ -257,12 +264,15 @@
 
     stack_moved([d_pre[:, 128 * at : 128 * at + 128] for at in range(BLOCKS)], stack_s)
     back = stack_s[...].astype(BF16)
-    total = jnp.zeros((256, 256), F32)
+    up = jnp.zeros((128, 128), F32)
+    skip = jnp.zeros((128, 128), F32)
     for pair in range(2):
-        taps = jnp.dot(tap_ref[pair], back, preferred_element_type=F32).astype(BF16)
-        total = total + jnp.dot(taps, in_s[pair], preferred_element_type=F32)
-    up = total[0:128, 0:128] + total[128:256, 0:128]
-    skip = total[0:128, 128:256] + rolled(total[128:256, 128:256], 64)
+        result = jnp.dot(back, fine_ref[pair], preferred_element_type=F32)
+        taps = jnp.dot(
+            tap_ref[pair], result, precision=HIGHEST, preferred_element_type=F32
+        )
+        up = up + taps[0:128, 0:128] + taps[128:256, 0:128]
+        skip = skip + taps[0:128, 128:256] + rolled(taps[128:256, 128:256], 64)
     half = low_half((32, 128))
     for even in range(0, OWN, 2):
         first, second = slice(32 * even, 32 * even + 32), slice(32 * even + 32, 32 * even + 64)
@@ -338,27 +348,37 @@
     )(*deep, share_choice)
     parts, inputs = lax.optimization_barrier((parts, inputs))
     data = traded(parts, PLANE)
+    chosen, double = choices()
+    fine = pl.pallas_call(
+        fine_kernel,
+        out_shape=jax.ShapeDtypeStruct((2, 2048, 256), BF16),
+        cost_estimate=pl.CostEstimate(
+            flops=300_000_000, bytes_accessed=4_000_000, transcendentals=0
+        ),
+    )(inputs, double)
+    field = pl.pallas_call(
+        field_kernel,
+        out_shape=jax.ShapeDtypeStruct((SIZE_X, SIZE_Y, 512), BF16),
+        cost_estimate=pl.CostEstimate(
+            flops=60_000_000, bytes_accessed=4_000_000, transcendentals=0
+        ),
+    )(*deep, field_choice)
+    data, fine, field = lax.optimization_barrier((data, fine, field))
     share = pl.pallas_call(
         share_kernel,
         out_shape=jax.ShapeDtypeStruct(SHARE, F32),
-        scratch_shapes=[
-            pltpu.VMEM((216, 2048), F32),
-            pltpu.VMEM((2, 2048, 256), BF16),
-        ],
-        compiler_params=pltpu.CompilerParams(vmem_limit_bytes=40 * 2**20),
+        scratch_shapes=[pltpu.VMEM((216, 2048), F32)],
+        compiler_params=pltpu.CompilerParams(vmem_limit_bytes=32 * 2**20),
         cost_estimate=pl.CostEstimate(
             flops=1_500_000_000, bytes_accessed=2_000_000, transcendentals=200_000
         ),
-    )(data, inputs, own_head_matrix(head), *choices())
-    deep, share = lax.optimization_barrier((deep, share))
-    field = pl.pallas_call(
-        field_kernel, out_shape=jax.ShapeDtypeStruct((SIZE_X, SIZE_Y, 512), BF16)
-    )(*deep, field_choice)
-    field = with_x_rims(field)
+    )(data, fine, own_head_matrix(head), *chosen)
     near = jnp.sum(traded(share.reshape(4, 8, SHARE[1]), NEAR), axis=0)
     field, near = lax.optimization_barrier((field, near))
+    field = with_x_rims(field)
+    far = jnp.sum(spread(near.astype(BF16), FAR).astype(F32), axis=0)
+    field, far = lax.optimization_barrier((field, far))
     field = with_y_rims(field)
-    far = jnp.sum(spread(near.astype(BF16), FAR).astype(F32), axis=0)
     column = spread(far.astype(BF16), NEAR).reshape(SHARE)
     field, column = lax.optimization_barrier((field, column))
     body, head_grad = pl.pallas_call(

time: 122 us -> 123 us (level)
  blocking collectives: 0 us -> 7.92 us
  waiting for transfers between devices: 30 us -> 22.6 us
  Pallas kernels: 14 us -> 18.3 us
  other arithmetic: 2.3 us -> 0.54 us
  starting transfers between devices: 65 us -> 63.7 us
    all_to_all x0 -> x1, blocking collectives: none -> 7.92 us  [traded(): return lax.all_to_all(parts, axes, 0, 0)]
    all_to_all x6 -> x5, waiting for transfers between devices: 28 us -> 20.4 us  [traded(): return lax.all_to_all(parts, axes, 0, 0)]
    pallas_call x0 -> x2, Pallas kernels: none -> 5.28 us  [the longest x1 3.28 us: per_device(): pl.pallas_call(fine_kernel, out_shape=jax.ShapeDtypeStruct((2, 2048, 256)...]
    ppermute x3, starting transfers between devices: 14.9 us -> 18.2 us  [from_both(): lax.ppermute(to_previous, axis, down)]
    all_to_all x6 -> x5, starting transfers between devices: 42.3 us -> 39.8 us  [traded(): return lax.all_to_all(parts, axes, 0, 0)]
    ppermute x3, starting transfers between devices: 7.75 us -> 5.75 us  [from_both(): lax.ppermute(to_next, axis, up)]
    unnamed x21 -> x25, local copies, waits for them, and re-layouts: 1.28 us -> 2.86 us
    broadcast_in_dim x4 -> x3, local copies, waits for them, and re-layouts: 3.42 us -> 2.23 us  [spread(): return traded(jnp.broadcast_to(part[None], (peers, *part.shape)), axes)]
  transfers between devices with their start and end apart: 12 -> 11, of which waited for: 7 -> 7; matrix products, arithmetic and copies ran while one was open for 5% -> 3% of each run, Pallas kernels for 7% -> 10%
where the time goes in v5:
time: 123 us; the launch traced here: 122 us
  starting transfers between devices  63.7 us (52%)
  waiting for transfers between devices  22.6 us (18%)
  Pallas kernels  18.3 us (15%)
  local copies, waits for them, and re-layouts  8.02 us (7%)
  blocking collectives  7.92 us (6%)
    all_to_all x5, starting transfers between devices, traded(): return lax.all_to_all(parts, axes, 0, 0)  39.8 us
    all_to_all x5, waiting for transfers between devices, traded(): return lax.all_to_all(parts, axes, 0, 0)  20.4 us
    ppermute x3, starting transfers between devices, from_both(): lax.ppermute(to_previous, axis, down)  18.2 us
    all_to_all x1, blocking collectives, traded(): return lax.all_to_all(parts, axes, 0, 0)  7.92 us
    ppermute x3, starting transfers between devices, from_both(): lax.ppermute(to_next, axis, up)  5.75 us
    pallas_call x1, Pallas kernels, per_device(): pl.pallas_call(fine_kernel, out_shape=jax.ShapeDtypeStruct((2, 2048, 256)...  3.28 us
    pallas_call x1, Pallas kernels, per_device(): pl.pallas_call(share_kernel, out_shape=jax.ShapeDtypeStruct(SHARE, F32),...  3.14 us
    unnamed x25, local copies, waits for them, and re-layouts  2.86 us
  transfers between devices with their start and end apart: 11, of which 7 were waited for; matrix products, arithmetic and copies ran while one was open for 3% of the time, Pallas kernels for 10%

profile of v5, /device:TPU:1, one launch (start us, length us, event | category | flops | bytes accessed | tf_op | source)
XLA Modules:
  0.0 122.0 jit_solution(13133522386829678065)
XLA Ops:
  0.6 2.0 %shard_map.158 = bf16[16,160,256]{2,1,0:T(8,128)(2,1)} custom-call(bf16[32,256]{1,0:T(8,128)(2,1)} %bitcast.25, bf16[128,256]{1,0:T(8,128)(2,1)} %bitcast.22), custom_call_target="tpu_custom_call" | custom-call | tf_op jit(solution)/shard_map/pallas_call | solution.py:66
  2.6 0.0 copy-start.10
  2.6 10.5 %all-to-all-start = ((bf16[16,160,256]{2,1,0:T(8,128)(2,1)}), bf16[16,160,256]{2,1,0:T(8,128)(2,1)S(1)}, u32[]{:S(2)}, u32[]{:S(2)}) async-start(bf16[16,160,256]{2,1,0:T(8,128)(2,1)} %shard_map.158), calls=%async_computation | async-start | bytes 2621440 | tf_op jit(solution)/shard_map/all_to_all | solution.py:333
  13.2 0.0 copy-done.10
  13.2 0.1 reshape.51
  13.3 0.6 pad.32.cot_ref
  13.9 1.6 %shard_map.156 = (bf16[272,128]{1,0:T(8,128)(2,1)}, bf16[80,128]{1,0:T(8,128)(2,1)}, bf16[80,128]{1,0:T(8,128)(2,1)}) custom-call(bf16[128,256]{1,0:T(8,128)(2,1)} %bitcast.23, bf16[16,128]{1,0:T(8,128)(2,1)} %pad.32.cot_ref), custom_call_target="tpu_custom_call" | custom-call | tf_op jit(solution)/shard_map/pallas_call | solution.py:53
  15.5 1.9 %collective-permute-start = (bf16[80,128]{1,0:T(8,128)(2,1)}, bf16[80,128]{1,0:T(8,128)(2,1)S(1)}, u32[]{:S(2)}, u32[]{:S(2)}) collective-permute-start(bf16[80,128]{1,0:T(8,128)(2,1)} %get-tuple-element.22), channel_id=1, source_target_pairs={{0,1},{1,2},{2,3},{3,4},{4,5},{5,6},{6,7},{7,8},{8,9},{9,10},{10,1... | collective-permute-start | bytes 61448 | tf_op jit(solution)/shard_map/ppermute | solution.py:47
  17.4 9.9 %collective-permute-start.1 = (bf16[80,128]{1,0:T(8,128)(2,1)}, bf16[80,128]{1,0:T(8,128)(2,1)S(1)}, u32[]{:S(2)}, u32[]{:S(2)}) collective-permute-start(bf16[80,128]{1,0:T(8,128)(2,1)} %get-tuple-element.24), channel_id=1, source_target_pairs={{1,0},{2,1},{3,2},{4,3},{5,4},{6,5},{7,6},{8,7},{9,8},{10,9},{11,1... | collective-permute-start | bytes 61448 | tf_op jit(solution)/shard_map/ppermute | solution.py:47
  27.3 0.0 copy-done.11
  27.4 0.0 collective-permute-done.before_ref
  27.4 0.0 copy-start.8
  27.4 1.0 collective-permute-done.1.after_ref
  28.4 0.0 copy-done.8
  28.4 0.6 copy-done.9
  29.0 2.2 %shard_map.157 = bf16[16,48,128]{2,1,0:T(8,128)(2,1)} custom-call(bf16[80,128]{1,0:T(8,128)(2,1)} %copy-done.8, bf16[272,128]{1,0:T(8,128)(2,1)} %get-tuple-element.23.rows_ref, bf16[80,128]{1,0:T(8,128)(2,1)} %copy-done.9, bf16[768,432]{1,0:T(8,128)(2,1)} %constant.38.clone.choice_ref), custom_call_target="tpu_custom_call" | custom-call | tf_op jit(solution)/shard_map/pallas_call | solution.py:346
  31.2 1.0 all-to-all-done.input_ref
  32.2 5.0 %all-to-all-start.1 = ((bf16[16,48,128]{2,1,0:T(8,128)(2,1)}), bf16[16,48,128]{2,1,0:T(8,128)(2,1)S(1)}, u32[]{:S(2)}, u32[]{:S(2)}) async-start(bf16[16,48,128]{2,1,0:T(8,128)(2,1)} %shard_map.157), calls=%async_computation.1 | async-start | bytes 393216 | tf_op jit(solution)/shard_map/all_to_all | solution.py:333
  37.2 0.1 fusion.5
  37.3 0.2 concatenate.12.head_ref
  37.5 0.4 copy.27
  37.9 0.0 copy-done.5
  38.0 0.1 reshape.57.head_ref
  38.1 2.0 %shard_map.160 = bf16[8,16,512]{2,1,0:T(8,128)(2,1)} custom-call(bf16[80,128]{1,0:T(8,128)(2,1)} %copy-done.8, bf16[272,128]{1,0:T(8,128)(2,1)} %get-tuple-element.23.rows_ref, bf16[80,128]{1,0:T(8,128)(2,1)} %copy-done.9, bf16[432,512]{1,0:T(8,128)(2,1)} %constant.39.clone.choice_ref), custom_call_target="tpu_custom_call" | custom-call | flops 60000000 | bytes 4000000 | tf_op jit(solution)/shard_map/pallas_call | solution.py:359
  40.1 3.3 %shard_map.159.fine_ref = bf16[2,2048,256]{2,1,0:T(8,128)(2,1)} custom-call(bf16[16,160,256]{2,1,0:T(8,128)(2,1)} %copy-done.5, bf16[128,32]{1,0:T(8,128)(2,1)} %constant.43.clone.double_ref), custom_call_target="tpu_custom_call" | custom-call | flops 300000000 | bytes 4000000 | tf_op jit(solution)/shard_map/pallas_call | solution.py:352
  43.4 0.5 all-to-all-done.1.data_ref
  43.9 0.0 copy-done.2
  43.9 0.0 copy-done.3
  43.9 0.0 copy-done.4
  43.9 0.0 copy-start
  43.9 1.6 %copy-done = bf16[2,2048,256]{2,1,0:T(8,128)(2,1)S(1)} copy-done((bf16[2,2048,256]{2,1,0:T(8,128)(2,1)S(1)}, bf16[2,2048,256]{2,1,0:T(8,128)(2,1)}, u32[]{:S(2)}) %copy-start) | copy-done | bytes 2097176
  45.5 3.1 %shard_map.161 = f32[32,768]{1,0:T(8,128)S(1)} custom-call(bf16[16,48,128]{2,1,0:T(8,128)(2,1)S(1)} %all-to-all-done.1.data_ref, bf16[2,2048,256]{2,1,0:T(8,128)(2,1)S(1)} %copy-done, bf16[24,216]{1,0:T(8,128)(2,1)S(1)} %reshape.57.head_ref, f32[2,256,216]{2,1,0:T(8,128)S(1)} %copy-done.2, f32[216,512]{1,0:T(8,128)S(1)} %copy-done.3, f32[32,24]{1,0:T(8,128)S(1)} %copy-done.4), custom_call_target="tpu_custom_call" | custom-call | flops 1500000000 | bytes 2000000 | tf_op jit(solution)/shard_map/pallas_call | solution.py:367
  48.7 7.9 %all_to_all.30 = f32[4,8,768]{2,1,0:T(8,128)S(1)} all-to-all(f32[4,8,768]{2,1,0:T(8,128)S(1)} %bitcast.16), channel_id=1, replica_groups=mesh['gx'=4,'gy'=4,'gzh'=2,'gzm'=8,'gzl'=2] {'gzh','gzl'}, dimensions={0} | all-to-all | bytes 196608 | tf_op jit(solution)/shard_map/all_to_all | solution.py:333
  56.6 0.6 broadcast_in_dim.8
  57.2 11.4 %all-to-all-start.3 = ((bf16[8,8,768]{2,1,0:T(8,128)(2,1)}), bf16[8,8,768]{2,1,0:T(8,128)(2,1)S(1)}, u32[]{:S(2)}, u32[]{:S(2)}) async-start(bf16[8,8,768]{2,1,0:T(8,128)(2,1)} %broadcast_in_dim.8), calls=%async_computation.3 | async-start | bytes 196608 | tf_op jit(solution)/shard_map/all_to_all | solution.py:333
  68.6 0.0 copy-done.6
  68.6 4.2 %collective-permute-start.3 = (bf16[2,16,512]{2,1,0:T(8,128)(2,1)S(1)}, bf16[2,16,512]{2,1,0:T(8,128)(2,1)S(1)}, u32[]{:S(2)}, u32[]{:S(2)}) collective-permute-start(bf16[2,16,512]{2,1,0:T(8,128)(2,1)S(1)} %get-tuple-element.55), channel_id=1, source_target_pairs={{128,0},{256,128},{384,256},{0,384},{129,1},{257,129},{385,257},{1... | collective-permute-start | bytes 98312 | tf_op jit(solution)/shard_map/ppermute | solution.py:47
  72.8 1.9 %collective-permute-start.2 = (bf16[2,16,512]{2,1,0:T(8,128)(2,1)S(1)}, bf16[2,16,512]{2,1,0:T(8,128)(2,1)S(1)}, u32[]{:S(2)}, u32[]{:S(2)}) collective-permute-start(bf16[2,16,512]{2,1,0:T(8,128)(2,1)S(1)} %get-tuple-element.54), channel_id=1, source_target_pairs={{0,128},{128,256},{256,384},{384,0},{1,129},{129,257},{257,385},{3... | collective-permute-start | bytes 98312 | tf_op jit(solution)/shard_map/ppermute | solution.py:47
  74.7 0.0 collective-permute-done.3
  74.7 1.2 collective-permute-done.2
  75.9 5.4 %all-to-all-done.3 = bf16[8,8,768]{2,1,0:T(8,128)(2,1)S(1)} async-done(((bf16[8,8,768]{2,1,0:T(8,128)(2,1)}), bf16[8,8,768]{2,1,0:T(8,128)(2,1)S(1)}, u32[]{:S(2)}, u32[]{:S(2)}) %all-to-all-start.3) | async-done | bytes 98336 | tf_op jit(solution)/shard_map/all_to_all | solution.py:333
  81.4 4.1 %collective-permute-start.5 = (bf16[12,2,512]{2,1,0:T(2,128)(2,1)S(1)}, bf16[12,2,512]{2,1,0:T(2,128)(2,1)S(1)}, u32[]{:S(2)}, u32[]{:S(2)}) collective-permute-start(bf16[12,2,512]{2,1,0:T(2,128)(2,1)S(1)} %get-tuple-element.53), channel_id=1, source_target_pairs={{32,0},{64,32},{96,64},{0,96},{33,1},{65,33},{97,65},{1,97},{34,2}... | collective-permute-start | bytes 73736 | tf_op jit(solution)/shard_map/ppermute | solution.py:47
  85.5 1.9 %collective-permute-start.4 = (bf16[12,2,512]{2,1,0:T(2,128)(2,1)S(1)}, bf16[12,2,512]{2,1,0:T(2,128)(2,1)S(1)}, u32[]{:S(2)}, u32[]{:S(2)}) collective-permute-start(bf16[12,2,512]{2,1,0:T(2,128)(2,1)S(1)} %get-tuple-element.52), channel_id=1, source_target_pairs={{0,32},{32,64},{64,96},{96,0},{1,33},{33,65},{65,97},{97,1},{2,34}... | collective-permute-start | bytes 73736 | tf_op jit(solution)/shard_map/ppermute | solution.py:47
  87.4 0.1 pad.45.clone
  87.5 0.6 broadcast_in_dim.10
  88.1 3.3 %all-to-all-start.4 = ((bf16[4,8,768]{2,1,0:T(8,128)(2,1)}), bf16[4,8,768]{2,1,0:T(8,128)(2,1)S(1)}, u32[]{:S(2)}, u32[]{:S(2)}) async-start(bf16[4,8,768]{2,1,0:T(8,128)(2,1)} %broadcast_in_dim.10), calls=%async_computation.4 | async-start | bytes 98304 | tf_op jit(solution)/shard_map/all_to_all | solution.py:333
  91.4 0.0 collective-permute-done.5
  91.4 0.0 collective-permute-done.4
  91.4 0.2 maximum_maximum_fusion.field_ref
  91.6 0.0 copy-start.7
  91.6 4.9 %all-to-all-done.4 = bf16[4,8,768]{2,1,0:T(8,128)(2,1)S(1)} async-done(((bf16[4,8,768]{2,1,0:T(8,128)(2,1)}), bf16[4,8,768]{2,1,0:T(8,128)(2,1)S(1)}, u32[]{:S(2)}, u32[]{:S(2)}) %all-to-all-start.4) | async-done | bytes 49184 | tf_op jit(solution)/shard_map/all_to_all | solution.py:333
  96.5 1.0 broadcast_in_dim.11
  97.5 9.7 %all-to-all-start.5 = ((bf16[16,32,768]{2,1,0:T(8,128)(2,1)}), bf16[16,32,768]{2,1,0:T(8,128)(2,1)S(1)}, u32[]{:S(2)}, u32[]{:S(2)}) async-start(bf16[16,32,768]{2,1,0:T(8,128)(2,1)} %broadcast_in_dim.11), calls=%async_computation.5 | async-start | bytes 1572864 | tf_op jit(solution)/shard_map/all_to_all | solution.py:333
  107.1 0.0 copy-done.7
  107.1 1.0 reshape.60
  108.1 0.1 rev.7
  108.2 0.1 slice.25
  108.3 0.3 fusion.2.weight_ref
  108.6 0.0 copy-start.1
  108.6 2.6 %shard_map.162 = (bf16[8,16,256]{2,1,0:T(8,128)(2,1)}, bf16[32,256]{1,0:T(8,128)(2,1)}) custom-call(bf16[12,32,512]{2,1,0:T(8,128)(2,1)S(1)} %maximum_maximum_fusion.field_ref, bf16[9,32,384]{2,1,0:T(8,128)(2,1)S(1)} %concatenate.12.head_ref, bf16[9,256,256]{2,1,0:T(8,128)(2,1)S(1)} %fusion.2.weight_ref), custom_call_target="tpu_custom_call" | custom-call | flops 700000000 | bytes 3000000 | tf_op jit(solution)/shard_map/pallas_call | solution.py:392
  111.2 8.7 %all-to-all-done.5.share_ref = bf16[16,32,768]{2,1,0:T(8,128)(2,1)S(1)} async-done(((bf16[16,32,768]{2,1,0:T(8,128)(2,1)}), bf16[16,32,768]{2,1,0:T(8,128)(2,1)S(1)}, u32[]{:S(2)}, u32[]{:S(2)}) %all-to-all-start.5) | async-done | bytes 786464 | tf_op jit(solution)/shard_map/all_to_all | solution.py:333
  119.9 0.0 copy-done.1
  119.9 1.4 %shard_map.163 = (f32[27,12288]{1,0:T(8,128)}, f32[27,3,64]{2,1,0:T(4,128)S(1)}) custom-call(bf16[16,32,768]{2,1,0:T(8,128)(2,1)S(1)} %all-to-all-done.5.share_ref, bf16[512,64]{1,0:T(8,128)(2,1)S(1)} %copy-done.1), custom_call_target="tpu_custom_call" | custom-call | tf_op jit(solution)/shard_map/pallas_call | solution.py:384
  121.4 0.6 copy.29
  (20 shorter events, 0.3 us)
Async XLA Ops:
  2.6 10.5 %copy-start.10 = (bf16[3,8,16,4]{2,3,1,0:T(4,128)(2,1)S(1)}, bf16[3,8,16,4]{2,3,1,0:T(4,128)(2,1)}, u32[]{:S(2)}) copy-start(bf16[3,8,16,4]{2,3,1,0:T(4,128)(2,1)} %param.16) | copy-start | bytes 9220
  2.6 24.7 %copy-start.11 = (bf16[27,3,64]{2,0,1:T(8,128)(2,1)S(1)}, bf16[27,3,64]{2,0,1:T(8,128)(2,1)}, u32[]{:S(2)}) copy-start(bf16[27,3,64]{2,0,1:T(8,128)(2,1)} %param.18) | copy-start | bytes 31108
  2.6 29.6 %all-to-all-start = ((bf16[16,160,256]{2,1,0:T(8,128)(2,1)}), bf16[16,160,256]{2,1,0:T(8,128)(2,1)S(1)}, u32[]{:S(2)}, u32[]{:S(2)}) async-start(bf16[16,160,256]{2,1,0:T(8,128)(2,1)} %shard_map.158), calls=%async_computation | async-start | bytes 2621440 | tf_op jit(solution)/shard_map/all_to_all | solution.py:333
  15.5 11.9 %collective-permute-start = (bf16[80,128]{1,0:T(8,128)(2,1)}, bf16[80,128]{1,0:T(8,128)(2,1)S(1)}, u32[]{:S(2)}, u32[]{:S(2)}) collective-permute-start(bf16[80,128]{1,0:T(8,128)(2,1)} %get-tuple-element.22), channel_id=1, source_target_pairs={{0,1},{1,2},{2,3},{3,4},{4,5},{5,6},{6,7},{7,8},{8,9},{9,10},{10,1... | collective-permute-start | bytes 61448 | tf_op jit(solution)/shard_map/ppermute | solution.py:47
  17.4 11.0 %collective-permute-start.1 = (bf16[80,128]{1,0:T(8,128)(2,1)}, bf16[80,128]{1,0:T(8,128)(2,1)S(1)}, u32[]{:S(2)}, u32[]{:S(2)}) collective-permute-start(bf16[80,128]{1,0:T(8,128)(2,1)} %get-tuple-element.24), channel_id=1, source_target_pairs={{1,0},{2,1},{3,2},{4,3},{5,4},{6,5},{7,6},{8,7},{9,8},{10,9},{11,1... | collective-permute-start | bytes 61448 | tf_op jit(solution)/shard_map/ppermute | solution.py:47
  27.4 1.0 copy-start.8
  28.4 0.6 copy-start.9
  32.2 5.7 %copy-start.5 = (bf16[16,160,256]{2,1,0:T(8,128)(2,1)}, bf16[16,160,256]{2,1,0:T(8,128)(2,1)S(1)}, u32[]{:S(2)}) copy-start(bf16[16,160,256]{2,1,0:T(8,128)(2,1)S(1)} %all-to-all-done.input_ref) | copy-start | bytes 3932164
  32.2 11.7 %all-to-all-start.1 = ((bf16[16,48,128]{2,1,0:T(8,128)(2,1)}), bf16[16,48,128]{2,1,0:T(8,128)(2,1)S(1)}, u32[]{:S(2)}, u32[]{:S(2)}) async-start(bf16[16,48,128]{2,1,0:T(8,128)(2,1)} %shard_map.157), calls=%async_computation.1 | async-start | bytes 393216 | tf_op jit(solution)/shard_map/all_to_all | solution.py:333
  40.1 3.8 %copy-start.2 = (f32[2,256,216]{2,1,0:T(8,128)S(1)}, f32[2,256,216]{2,1,0:T(8,128)}, u32[]{:S(2)}) copy-start(f32[2,256,216]{2,1,0:T(8,128)} %constant.40.clone.tap_ref) | copy-start | bytes 1327108
  40.1 3.8 %copy-start.3 = (f32[216,512]{1,0:T(8,128)S(1)}, f32[216,512]{1,0:T(8,128)}, u32[]{:S(2)}) copy-start(f32[216,512]{1,0:T(8,128)} %constant.41.clone.column_ref) | copy-start | bytes 1327108
  40.1 3.8 %copy-start.4 = (f32[32,24]{1,0:T(8,128)S(1)}, f32[32,24]{1,0:T(8,128)}, u32[]{:S(2)}) copy-start(f32[32,24]{1,0:T(8,128)} %constant.42.clone.row_ref) | copy-start | bytes 9220
  43.9 1.6 %copy-start = (bf16[2,2048,256]{2,1,0:T(8,128)(2,1)S(1)}, bf16[2,2048,256]{2,1,0:T(8,128)(2,1)}, u32[]{:S(2)}) copy-start(bf16[2,2048,256]{2,1,0:T(8,128)(2,1)} %shard_map.159.fine_ref) | copy-start | bytes 6291460
  45.5 23.1 %copy-start.6 = (bf16[8,16,512]{2,1,0:T(8,128)(2,1)S(1)}, bf16[8,16,512]{2,1,0:T(8,128)(2,1)}, u32[]{:S(2)}) copy-start(bf16[8,16,512]{2,1,0:T(8,128)(2,1)} %shard_map.160) | copy-start | bytes 393220
  57.2 24.1 %all-to-all-start.3 = ((bf16[8,8,768]{2,1,0:T(8,128)(2,1)}), bf16[8,8,768]{2,1,0:T(8,128)(2,1)S(1)}, u32[]{:S(2)}, u32[]{:S(2)}) async-start(bf16[8,8,768]{2,1,0:T(8,128)(2,1)} %broadcast_in_dim.8), calls=%async_computation.3 | async-start | bytes 196608 | tf_op jit(solution)/shard_map/all_to_all | solution.py:333
  68.6 6.1 %collective-permute-start.3 = (bf16[2,16,512]{2,1,0:T(8,128)(2,1)S(1)}, bf16[2,16,512]{2,1,0:T(8,128)(2,1)S(1)}, u32[]{:S(2)}, u32[]{:S(2)}) collective-permute-start(bf16[2,16,512]{2,1,0:T(8,128)(2,1)S(1)} %get-tuple-element.55), channel_id=1, source_target_pairs={{128,0},{256,128},{384,256},{0,384},{129,1},{257,129},{385,257},{1... | collective-permute-start | bytes 98312 | tf_op jit(solution)/shard_map/ppermute | solution.py:47
  72.8 3.1 %collective-permute-start.2 = (bf16[2,16,512]{2,1,0:T(8,128)(2,1)S(1)}, bf16[2,16,512]{2,1,0:T(8,128)(2,1)S(1)}, u32[]{:S(2)}, u32[]{:S(2)}) collective-permute-start(bf16[2,16,512]{2,1,0:T(8,128)(2,1)S(1)} %get-tuple-element.54), channel_id=1, source_target_pairs={{0,128},{128,256},{256,384},{384,0},{1,129},{129,257},{257,385},{3... | collective-permute-start | bytes 98312 | tf_op jit(solution)/shard_map/ppermute | solution.py:47
  81.4 10.0 %collective-permute-start.5 = (bf16[12,2,512]{2,1,0:T(2,128)(2,1)S(1)}, bf16[12,2,512]{2,1,0:T(2,128)(2,1)S(1)}, u32[]{:S(2)}, u32[]{:S(2)}) collective-permute-start(bf16[12,2,512]{2,1,0:T(2,128)(2,1)S(1)} %get-tuple-element.53), channel_id=1, source_target_pairs={{32,0},{64,32},{96,64},{0,96},{33,1},{65,33},{97,65},{1,97},{34,2}... | collective-permute-start | bytes 73736 | tf_op jit(solution)/shard_map/ppermute | solution.py:47
  85.5 5.9 %collective-permute-start.4 = (bf16[12,2,512]{2,1,0:T(2,128)(2,1)S(1)}, bf16[12,2,512]{2,1,0:T(2,128)(2,1)S(1)}, u32[]{:S(2)}, u32[]{:S(2)}) collective-permute-start(bf16[12,2,512]{2,1,0:T(2,128)(2,1)S(1)} %get-tuple-element.52), channel_id=1, source_target_pairs={{0,32},{32,64},{64,96},{96,0},{1,33},{33,65},{65,97},{97,1},{2,34}... | collective-permute-start | bytes 73736 | tf_op jit(solution)/shard_map/ppermute | solution.py:47
  88.1 8.4 %all-to-all-start.4 = ((bf16[4,8,768]{2,1,0:T(8,128)(2,1)}), bf16[4,8,768]{2,1,0:T(8,128)(2,1)S(1)}, u32[]{:S(2)}, u32[]{:S(2)}) async-start(bf16[4,8,768]{2,1,0:T(8,128)(2,1)} %broadcast_in_dim.10), calls=%async_computation.4 | async-start | bytes 98304 | tf_op jit(solution)/shard_map/all_to_all | solution.py:333
  91.6 15.5 %copy-start.7 = (bf16[27,12288]{1,0:T(8,128)(2,1)S(1)}, bf16[27,12288]{1,0:T(8,128)(2,1)}, u32[]{:S(2)}) copy-start(bf16[27,12288]{1,0:T(8,128)(2,1)} %param.17) | copy-start | bytes 1990660
  97.5 22.5 %all-to-all-start.5 = ((bf16[16,32,768]{2,1,0:T(8,128)(2,1)}), bf16[16,32,768]{2,1,0:T(8,128)(2,1)S(1)}, u32[]{:S(2)}, u32[]{:S(2)}) async-start(bf16[16,32,768]{2,1,0:T(8,128)(2,1)} %broadcast_in_dim.11), calls=%async_computation.5 | async-start | bytes 1572864 | tf_op jit(solution)/shard_map/all_to_all | solution.py:333
  108.6 11.3 %copy-start.1 = (bf16[512,64]{1,0:T(8,128)(2,1)S(1)}, bf16[512,64]{1,0:T(8,128)(2,1)}, u32[]{:S(2)}) copy-start(bf16[512,64]{1,0:T(8,128)(2,1)} %constant.44.clone.choice_ref) | copy-start | bytes 196612

commit v6 on v5

--- a/solution.py
+++ b/solution.py
@@ -96,7 +96,8 @@
 def row_choices():
     pre_at = lambda z, c: c if z < 0 else 352 + c if z > 3 else 80 + 64 * z + c
     cot_at = lambda z, o: 76 + 3 * z + o if z < 0 else 404 + 3 * z + o if z > 3 else 336 + 3 * z + o
-    shares = np.zeros((BLOCKS, 48, 432), np.float32)
+    shares = np.zeros((BLOCKS, ROWS, 432), np.float32)
+    cots = np.zeros((24, 432), np.float32)
     lanes = np.zeros((432, 512), np.float32)
     for z in range(-1, 5):
         for c in range(C_HID):
@@ -104,9 +105,10 @@
             lanes[pre_at(z, c), C_HID * (z + 1) + c] = 1.0
     for z in range(-2, 6):
         for o in range(C_VEL):
-            shares[:, ROWS + C_VEL * (z + 2) + o, cot_at(z, o)] = 1.0
+            cots[C_VEL * (z + 2) + o, cot_at(z, o)] = 1.0
             lanes[cot_at(z, o), 384 + C_VEL * (z + 2) + o] = 1.0
-    return jnp.asarray(shares.reshape(768, 432), BF16), jnp.asarray(lanes, BF16)
+    rows = np.concatenate([shares.reshape(BLOCKS * ROWS, 432), cots], axis=0)
+    return jnp.asarray(rows, BF16), jnp.asarray(lanes, BF16)
 
 
 def choices():
@@ -128,7 +130,7 @@
         for y in range(SIZE_Y):
             double[x, y, x // 2, y // 2] = 1.0
     return (
-        jnp.asarray(tap_rows.reshape(2, 256, 216)),
+        jnp.asarray(tap_rows.reshape(2, 256, 216), BF16),
         jnp.asarray(head_columns.reshape(216, 512)),
         jnp.asarray(head_rows.reshape(32, ROWS)),
     ), jnp.asarray(double.reshape(128, 32), BF16)
@@ -159,7 +161,10 @@
 def parts_kernel(before_ref, rows_ref, after_ref, choice_ref, parts_ref):
     rows = joined(before_ref, rows_ref, after_ref)
     parts = jnp.dot(choice_ref[...], rows, preferred_element_type=F32)
-    parts_ref[...] = parts.astype(BF16).reshape(BLOCKS, 48, 128)
+    cot = parts[BLOCKS * ROWS :]
+    for at in range(BLOCKS):
+        both = jnp.concatenate([parts[ROWS * at : ROWS * at + ROWS], cot], axis=0)
+        parts_ref[at] = both.astype(BF16)
 
 
 def field_kernel(before_ref, rows_ref, after_ref, choice_ref, field_ref):
@@ -269,7 +274,7 @@
     for pair in range(2):
         result = jnp.dot(back, fine_ref[pair], preferred_element_type=F32)
         taps = jnp.dot(
-            tap_ref[pair], result, precision=HIGHEST, preferred_element_type=F32
+            tap_ref[pair].astype(F32), result, precision=HIGHEST, preferred_element_type=F32
         )
         up = up + taps[0:128, 0:128] + taps[128:256, 0:128]
         skip = skip + taps[0:128, 128:256] + rolled(taps[128:256, 128:256], 64)
@@ -377,10 +382,9 @@
     field, near = lax.optimization_barrier((field, near))
     field = with_x_rims(field)
     far = jnp.sum(spread(near.astype(BF16), FAR).astype(F32), axis=0)
-    field, far = lax.optimization_barrier((field, far))
-    field = with_y_rims(field)
     column = spread(far.astype(BF16), NEAR).reshape(SHARE)
     field, column = lax.optimization_barrier((field, column))
+    field = with_y_rims(field)
     body, head_grad = pl.pallas_call(
         unpack_kernel,
         out_shape=(

time: 123 us -> 118 us (0.959)
  waiting for transfers between devices: 22.6 us -> 18.1 us
    all_to_all x5, waiting for transfers between devices: 20.4 us -> 13.3 us  [traded(): return lax.all_to_all(parts, axes, 0, 0)]
    ppermute x3, waiting for transfers between devices: 1 us -> 4.25 us  [from_both(): lax.ppermute(to_previous, axis, down)]
  transfers between devices with their start and end apart: 11 -> 11, of which waited for: 7 -> 7; matrix products, arithmetic and copies ran while one was open for 3% -> 4% of each run, Pallas kernels for 10% -> 10%
where the time goes in v6:
time: 118 us; the launch traced here: 117 us
  starting transfers between devices  63.3 us (54%)
  waiting for transfers between devices  18.1 us (15%)
  Pallas kernels  18 us (15%)
  local copies, waits for them, and re-layouts  8.02 us (7%)
  blocking collectives  7.92 us (7%)
    all_to_all x5, starting transfers between devices, traded(): return lax.all_to_all(parts, axes, 0, 0)  39 us
    ppermute x3, starting transfers between devices, from_both(): lax.ppermute(to_previous, axis, down)  18.6 us
    all_to_all x5, waiting for transfers between devices, traded(): return lax.all_to_all(parts, axes, 0, 0)  13.3 us
    all_to_all x1, blocking collectives, traded(): return lax.all_to_all(parts, axes, 0, 0)  7.92 us
    ppermute x3, starting transfers between devices, from_both(): lax.ppermute(to_next, axis, up)  5.75 us
    ppermute x3, waiting for transfers between devices, from_both(): lax.ppermute(to_previous, axis, down)  4.25 us
    pallas_call x1, Pallas kernels, per_device(): pl.pallas_call(fine_kernel, out_shape=jax.ShapeDtypeStruct((2, 2048, 256)...  3.27 us
    pallas_call x1, Pallas kernels, per_device(): pl.pallas_call(share_kernel, out_shape=jax.ShapeDtypeStruct(SHARE, F32),...  3.14 us
  transfers between devices with their start and end apart: 11, of which 7 were waited for; matrix products, arithmetic and copies ran while one was open for 4% of the time, Pallas kernels for 10%

profile of v6, /device:TPU:1, one launch (start us, length us, event | category | flops | bytes accessed | tf_op | source)
XLA Modules:
  0.0 116.8 jit_solution(8439966857439851476)
XLA Ops:
  0.6 2.0 %shard_map.158 = bf16[16,160,256]{2,1,0:T(8,128)(2,1)} custom-call(bf16[32,256]{1,0:T(8,128)(2,1)} %bitcast.25, bf16[128,256]{1,0:T(8,128)(2,1)} %bitcast.22), custom_call_target="tpu_custom_call" | custom-call | tf_op jit(solution)/shard_map/pallas_call | solution.py:66
  2.6 0.0 copy-start.10
  2.6 10.5 %all-to-all-start = ((bf16[16,160,256]{2,1,0:T(8,128)(2,1)}), bf16[16,160,256]{2,1,0:T(8,128)(2,1)S(1)}, u32[]{:S(2)}, u32[]{:S(2)}) async-start(bf16[16,160,256]{2,1,0:T(8,128)(2,1)} %shard_map.158), calls=%async_computation | async-start | bytes 2621440 | tf_op jit(solution)/shard_map/all_to_all | solution.py:338
  13.2 0.0 copy-done.10
  13.2 0.1 reshape.51
  13.3 0.6 pad.32.cot_ref
  13.9 1.6 %shard_map.156 = (bf16[272,128]{1,0:T(8,128)(2,1)}, bf16[80,128]{1,0:T(8,128)(2,1)}, bf16[80,128]{1,0:T(8,128)(2,1)}) custom-call(bf16[128,256]{1,0:T(8,128)(2,1)} %bitcast.23, bf16[16,128]{1,0:T(8,128)(2,1)} %pad.32.cot_ref), custom_call_target="tpu_custom_call" | custom-call | tf_op jit(solution)/shard_map/pallas_call | solution.py:53
  15.5 1.9 %collective-permute-start = (bf16[80,128]{1,0:T(8,128)(2,1)}, bf16[80,128]{1,0:T(8,128)(2,1)S(1)}, u32[]{:S(2)}, u32[]{:S(2)}) collective-permute-start(bf16[80,128]{1,0:T(8,128)(2,1)} %get-tuple-element.20), channel_id=1, source_target_pairs={{0,1},{1,2},{2,3},{3,4},{4,5},{5,6},{6,7},{7,8},{8,9},{9,10},{10,1... | collective-permute-start | bytes 61448 | tf_op jit(solution)/shard_map/ppermute | solution.py:47
  17.4 9.9 %collective-permute-start.1 = (bf16[80,128]{1,0:T(8,128)(2,1)}, bf16[80,128]{1,0:T(8,128)(2,1)S(1)}, u32[]{:S(2)}, u32[]{:S(2)}) collective-permute-start(bf16[80,128]{1,0:T(8,128)(2,1)} %get-tuple-element.22), channel_id=1, source_target_pairs={{1,0},{2,1},{3,2},{4,3},{5,4},{6,5},{7,6},{8,7},{9,8},{10,9},{11,1... | collective-permute-start | bytes 61448 | tf_op jit(solution)/shard_map/ppermute | solution.py:47
  27.3 0.0 copy-done.11
  27.4 0.0 collective-permute-done.before_ref
  27.4 0.0 copy-start.8
  27.4 1.0 collective-permute-done.1.after_ref
  28.4 0.0 copy-done.8
  28.4 0.6 copy-done.9
  29.0 2.0 %shard_map.157 = bf16[16,48,128]{2,1,0:T(8,128)(2,1)} custom-call(bf16[80,128]{1,0:T(8,128)(2,1)} %copy-done.8, bf16[272,128]{1,0:T(8,128)(2,1)} %get-tuple-element.21.rows_ref, bf16[80,128]{1,0:T(8,128)(2,1)} %copy-done.9, bf16[408,432]{1,0:T(8,128)(2,1)} %constant.39.clone.choice_ref), custom_call_target="tpu_custom_call" | custom-call | tf_op jit(solution)/shard_map/pallas_call | solution.py:351
  31.0 1.2 %all-to-all-done.input_ref = bf16[16,160,256]{2,1,0:T(8,128)(2,1)S(1)} async-done(((bf16[16,160,256]{2,1,0:T(8,128)(2,1)}), bf16[16,160,256]{2,1,0:T(8,128)(2,1)S(1)}, u32[]{:S(2)}, u32[]{:S(2)}) %all-to-all-start) | async-done | bytes 1310752 | tf_op jit(solution)/shard_map/all_to_all | solution.py:338
  32.2 4.8 %all-to-all-start.1 = ((bf16[16,48,128]{2,1,0:T(8,128)(2,1)}), bf16[16,48,128]{2,1,0:T(8,128)(2,1)S(1)}, u32[]{:S(2)}, u32[]{:S(2)}) async-start(bf16[16,48,128]{2,1,0:T(8,128)(2,1)} %shard_map.157), calls=%async_computation.1 | async-start | bytes 393216 | tf_op jit(solution)/shard_map/all_to_all | solution.py:338
  37.0 0.1 fusion.5
  37.1 0.2 concatenate.12.head_ref
  37.3 0.4 copy.27
  37.7 0.0 copy-done.5
  37.8 0.1 reshape.57.head_ref
  37.9 2.0 %shard_map.160 = bf16[8,16,512]{2,1,0:T(8,128)(2,1)} custom-call(bf16[80,128]{1,0:T(8,128)(2,1)} %copy-done.8, bf16[272,128]{1,0:T(8,128)(2,1)} %get-tuple-element.21.rows_ref, bf16[80,128]{1,0:T(8,128)(2,1)} %copy-done.9, bf16[432,512]{1,0:T(8,128)(2,1)} %constant.40.clone.choice_ref), custom_call_target="tpu_custom_call" | custom-call | flops 60000000 | bytes 4000000 | tf_op jit(solution)/shard_map/pallas_call | solution.py:364
  39.9 3.3 %shard_map.159.fine_ref = bf16[2,2048,256]{2,1,0:T(8,128)(2,1)} custom-call(bf16[16,160,256]{2,1,0:T(8,128)(2,1)} %copy-done.5, bf16[128,32]{1,0:T(8,128)(2,1)} %constant.44.clone.double_ref), custom_call_target="tpu_custom_call" | custom-call | flops 300000000 | bytes 4000000 | tf_op jit(solution)/shard_map/pallas_call | solution.py:357
  43.2 0.5 all-to-all-done.1.data_ref
  43.7 0.0 copy-done.2
  43.7 0.0 copy-done.3
  43.7 0.0 copy-done.4
  43.7 0.0 copy-start
  43.7 1.6 %copy-done = bf16[2,2048,256]{2,1,0:T(8,128)(2,1)S(1)} copy-done((bf16[2,2048,256]{2,1,0:T(8,128)(2,1)S(1)}, bf16[2,2048,256]{2,1,0:T(8,128)(2,1)}, u32[]{:S(2)}) %copy-start) | copy-done | bytes 2097176
  45.3 3.1 %shard_map.161 = f32[32,768]{1,0:T(8,128)S(1)} custom-call(bf16[16,48,128]{2,1,0:T(8,128)(2,1)S(1)} %all-to-all-done.1.data_ref, bf16[2,2048,256]{2,1,0:T(8,128)(2,1)S(1)} %copy-done, bf16[24,216]{1,0:T(8,128)(2,1)S(1)} %reshape.57.head_ref, bf16[2,256,216]{2,1,0:T(8,128)(2,1)S(1)} %copy-done.3, f32[216,512]{1,0:T(8,128)S(1)} %copy-done.2, ...), custom_call_target="tpu_custom_call" | custom-call | flops 1500000000 | bytes 2000000 | tf_op jit(solution)/shard_map/pallas_call | solution.py:372
  48.4 7.9 %all_to_all.30 = f32[4,8,768]{2,1,0:T(8,128)S(1)} all-to-all(f32[4,8,768]{2,1,0:T(8,128)S(1)} %bitcast.16), channel_id=1, replica_groups=mesh['gx'=4,'gy'=4,'gzh'=2,'gzm'=8,'gzl'=2] {'gzh','gzl'}, dimensions={0} | all-to-all | bytes 196608 | tf_op jit(solution)/shard_map/all_to_all | solution.py:338
  56.4 0.6 broadcast_in_dim.8
  57.0 11.6 %all-to-all-start.3 = ((bf16[8,8,768]{2,1,0:T(8,128)(2,1)}), bf16[8,8,768]{2,1,0:T(8,128)(2,1)S(1)}, u32[]{:S(2)}, u32[]{:S(2)}) async-start(bf16[8,8,768]{2,1,0:T(8,128)(2,1)} %broadcast_in_dim.8), calls=%async_computation.3 | async-start | bytes 196608 | tf_op jit(solution)/shard_map/all_to_all | solution.py:338
  68.6 0.0 copy-done.6
  68.6 4.2 %collective-permute-start.3 = (bf16[2,16,512]{2,1,0:T(8,128)(2,1)S(1)}, bf16[2,16,512]{2,1,0:T(8,128)(2,1)S(1)}, u32[]{:S(2)}, u32[]{:S(2)}) collective-permute-start(bf16[2,16,512]{2,1,0:T(8,128)(2,1)S(1)} %get-tuple-element.51), channel_id=1, source_target_pairs={{128,0},{256,128},{384,256},{0,384},{129,1},{257,129},{385,257},{1... | collective-permute-start | bytes 98312 | tf_op jit(solution)/shard_map/ppermute | solution.py:47
  72.8 1.9 %collective-permute-start.2 = (bf16[2,16,512]{2,1,0:T(8,128)(2,1)S(1)}, bf16[2,16,512]{2,1,0:T(8,128)(2,1)S(1)}, u32[]{:S(2)}, u32[]{:S(2)}) collective-permute-start(bf16[2,16,512]{2,1,0:T(8,128)(2,1)S(1)} %get-tuple-element.50), channel_id=1, source_target_pairs={{0,128},{128,256},{256,384},{384,0},{1,129},{129,257},{257,385},{3... | collective-permute-start | bytes 98312 | tf_op jit(solution)/shard_map/ppermute | solution.py:47
  74.7 6.6 %all-to-all-done.3 = bf16[8,8,768]{2,1,0:T(8,128)(2,1)S(1)} async-done(((bf16[8,8,768]{2,1,0:T(8,128)(2,1)}), bf16[8,8,768]{2,1,0:T(8,128)(2,1)S(1)}, u32[]{:S(2)}, u32[]{:S(2)}) %all-to-all-start.3) | async-done | bytes 98336 | tf_op jit(solution)/shard_map/all_to_all | solution.py:338
  81.3 0.6 broadcast_in_dim.9
  82.0 3.3 %all-to-all-start.4 = ((bf16[4,8,768]{2,1,0:T(8,128)(2,1)}), bf16[4,8,768]{2,1,0:T(8,128)(2,1)S(1)}, u32[]{:S(2)}, u32[]{:S(2)}) async-start(bf16[4,8,768]{2,1,0:T(8,128)(2,1)} %broadcast_in_dim.9), calls=%async_computation.4 | async-start | bytes 98304 | tf_op jit(solution)/shard_map/all_to_all | solution.py:338
  85.2 0.0 copy-start.7
  85.3 0.0 collective-permute-done.3
  85.3 0.0 collective-permute-done.2
  85.3 5.1 %all-to-all-done.4 = bf16[4,8,768]{2,1,0:T(8,128)(2,1)S(1)} async-done(((bf16[4,8,768]{2,1,0:T(8,128)(2,1)}), bf16[4,8,768]{2,1,0:T(8,128)(2,1)S(1)}, u32[]{:S(2)}, u32[]{:S(2)}) %all-to-all-start.4) | async-done | bytes 49184 | tf_op jit(solution)/shard_map/all_to_all | solution.py:338
  90.4 1.0 broadcast_in_dim.11
  91.3 8.8 %all-to-all-start.5 = ((bf16[16,32,768]{2,1,0:T(8,128)(2,1)}), bf16[16,32,768]{2,1,0:T(8,128)(2,1)S(1)}, u32[]{:S(2)}, u32[]{:S(2)}) async-start(bf16[16,32,768]{2,1,0:T(8,128)(2,1)} %broadcast_in_dim.11), calls=%async_computation.5 | async-start | bytes 1572864 | tf_op jit(solution)/shard_map/all_to_all | solution.py:338
  100.2 0.0 copy-done.7
  100.2 1.0 reshape.60
  101.2 0.1 rev.7
  101.3 0.1 slice.25
  101.4 4.5 %collective-permute-start.5 = (bf16[12,2,512]{2,1,0:T(2,128)(2,1)S(1)}, bf16[12,2,512]{2,1,0:T(2,128)(2,1)S(1)}, u32[]{:S(2)}, u32[]{:S(2)}) collective-permute-start(bf16[12,2,512]{2,1,0:T(2,128)(2,1)S(1)} %get-tuple-element.49), channel_id=1, source_target_pairs={{32,0},{64,32},{96,64},{0,96},{33,1},{65,33},{97,65},{1,97},{34,2}... | collective-permute-start | bytes 73736 | tf_op jit(solution)/shard_map/ppermute | solution.py:47
  106.0 1.9 %collective-permute-start.4 = (bf16[12,2,512]{2,1,0:T(2,128)(2,1)S(1)}, bf16[12,2,512]{2,1,0:T(2,128)(2,1)S(1)}, u32[]{:S(2)}, u32[]{:S(2)}) collective-permute-start(bf16[12,2,512]{2,1,0:T(2,128)(2,1)S(1)} %get-tuple-element.48), channel_id=1, source_target_pairs={{0,32},{32,64},{64,96},{96,0},{1,33},{33,65},{65,97},{97,1},{2,34}... | collective-permute-start | bytes 73736 | tf_op jit(solution)/shard_map/ppermute | solution.py:47
  107.9 0.3 fusion.2.weight_ref
  108.2 0.1 pad.45.clone
  108.3 3.3 %collective-permute-done.5 = bf16[12,2,512]{2,1,0:T(2,128)(2,1)S(1)} collective-permute-done((bf16[12,2,512]{2,1,0:T(2,128)(2,1)S(1)}, bf16[12,2,512]{2,1,0:T(2,128)(2,1)S(1)}, u32[]{:S(2)}, u32[]{:S(2)}) %collective-permute-start.5) | collective-permute-done | bytes 24608 | tf_op jit(solution)/shard_map/ppermute | solution.py:47
  111.5 0.5 collective-permute-done.4
  112.0 0.2 maximum_maximum_fusion.field_ref
  112.2 0.0 copy-start.1
  112.2 2.6 %shard_map.162 = (bf16[8,16,256]{2,1,0:T(8,128)(2,1)}, bf16[32,256]{1,0:T(8,128)(2,1)}) custom-call(bf16[12,32,512]{2,1,0:T(8,128)(2,1)S(1)} %maximum_maximum_fusion.field_ref, bf16[9,32,384]{2,1,0:T(8,128)(2,1)S(1)} %concatenate.12.head_ref, bf16[9,256,256]{2,1,0:T(8,128)(2,1)S(1)} %fusion.2.weight_ref), custom_call_target="tpu_custom_call" | custom-call | flops 700000000 | bytes 3000000 | tf_op jit(solution)/shard_map/pallas_call | solution.py:396
  114.8 0.0 all-to-all-done.5.share_ref
  114.8 0.0 copy-done.1
  114.8 1.4 %shard_map.163 = (f32[27,12288]{1,0:T(8,128)}, f32[27,3,64]{2,1,0:T(4,128)S(1)}) custom-call(bf16[16,32,768]{2,1,0:T(8,128)(2,1)S(1)} %all-to-all-done.5.share_ref, bf16[512,64]{1,0:T(8,128)(2,1)S(1)} %copy-done.1), custom_call_target="tpu_custom_call" | custom-call | tf_op jit(solution)/shard_map/pallas_call | solution.py:388
  116.2 0.6 copy.29
  (20 shorter events, 0.3 us)
Async XLA Ops:
  2.6 10.5 %copy-start.10 = (bf16[3,8,16,4]{2,3,1,0:T(4,128)(2,1)S(1)}, bf16[3,8,16,4]{2,3,1,0:T(4,128)(2,1)}, u32[]{:S(2)}) copy-start(bf16[3,8,16,4]{2,3,1,0:T(4,128)(2,1)} %param.16) | copy-start | bytes 9220
  2.6 24.7 %copy-start.11 = (bf16[27,3,64]{2,0,1:T(8,128)(2,1)S(1)}, bf16[27,3,64]{2,0,1:T(8,128)(2,1)}, u32[]{:S(2)}) copy-start(bf16[27,3,64]{2,0,1:T(8,128)(2,1)} %param.18) | copy-start | bytes 31108
  2.6 29.6 %all-to-all-start = ((bf16[16,160,256]{2,1,0:T(8,128)(2,1)}), bf16[16,160,256]{2,1,0:T(8,128)(2,1)S(1)}, u32[]{:S(2)}, u32[]{:S(2)}) async-start(bf16[16,160,256]{2,1,0:T(8,128)(2,1)} %shard_map.158), calls=%async_computation | async-start | bytes 2621440 | tf_op jit(solution)/shard_map/all_to_all | solution.py:338
  15.5 11.9 %collective-permute-start = (bf16[80,128]{1,0:T(8,128)(2,1)}, bf16[80,128]{1,0:T(8,128)(2,1)S(1)}, u32[]{:S(2)}, u32[]{:S(2)}) collective-permute-start(bf16[80,128]{1,0:T(8,128)(2,1)} %get-tuple-element.20), channel_id=1, source_target_pairs={{0,1},{1,2},{2,3},{3,4},{4,5},{5,6},{6,7},{7,8},{8,9},{9,10},{10,1... | collective-permute-start | bytes 61448 | tf_op jit(solution)/shard_map/ppermute | solution.py:47
  17.4 11.0 %collective-permute-start.1 = (bf16[80,128]{1,0:T(8,128)(2,1)}, bf16[80,128]{1,0:T(8,128)(2,1)S(1)}, u32[]{:S(2)}, u32[]{:S(2)}) collective-permute-start(bf16[80,128]{1,0:T(8,128)(2,1)} %get-tuple-element.22), channel_id=1, source_target_pairs={{1,0},{2,1},{3,2},{4,3},{5,4},{6,5},{7,6},{8,7},{9,8},{10,9},{11,1... | collective-permute-start | bytes 61448 | tf_op jit(solution)/shard_map/ppermute | solution.py:47
  27.4 1.0 copy-start.8
  28.4 0.6 copy-start.9
  32.2 5.5 %copy-start.5 = (bf16[16,160,256]{2,1,0:T(8,128)(2,1)}, bf16[16,160,256]{2,1,0:T(8,128)(2,1)S(1)}, u32[]{:S(2)}) copy-start(bf16[16,160,256]{2,1,0:T(8,128)(2,1)S(1)} %all-to-all-done.input_ref) | copy-start | bytes 3932164
  32.2 11.5 %all-to-all-start.1 = ((bf16[16,48,128]{2,1,0:T(8,128)(2,1)}), bf16[16,48,128]{2,1,0:T(8,128)(2,1)S(1)}, u32[]{:S(2)}, u32[]{:S(2)}) async-start(bf16[16,48,128]{2,1,0:T(8,128)(2,1)} %shard_map.157), calls=%async_computation.1 | async-start | bytes 393216 | tf_op jit(solution)/shard_map/all_to_all | solution.py:338
  39.9 3.8 %copy-start.2 = (f32[216,512]{1,0:T(8,128)S(1)}, f32[216,512]{1,0:T(8,128)}, u32[]{:S(2)}) copy-start(f32[216,512]{1,0:T(8,128)} %constant.42.clone.column_ref) | copy-start | bytes 1327108
  39.9 3.8 %copy-start.3 = (bf16[2,256,216]{2,1,0:T(8,128)(2,1)S(1)}, bf16[2,256,216]{2,1,0:T(8,128)(2,1)}, u32[]{:S(2)}) copy-start(bf16[2,256,216]{2,1,0:T(8,128)(2,1)} %constant.41.clone.tap_ref) | copy-start | bytes 663556
  39.9 3.8 %copy-start.4 = (f32[32,24]{1,0:T(8,128)S(1)}, f32[32,24]{1,0:T(8,128)}, u32[]{:S(2)}) copy-start(f32[32,24]{1,0:T(8,128)} %constant.43.clone.row_ref) | copy-start | bytes 9220
  43.7 1.6 %copy-start = (bf16[2,2048,256]{2,1,0:T(8,128)(2,1)S(1)}, bf16[2,2048,256]{2,1,0:T(8,128)(2,1)}, u32[]{:S(2)}) copy-start(bf16[2,2048,256]{2,1,0:T(8,128)(2,1)} %shard_map.159.fine_ref) | copy-start | bytes 6291460
  45.3 23.3 %copy-start.6 = (bf16[8,16,512]{2,1,0:T(8,128)(2,1)S(1)}, bf16[8,16,512]{2,1,0:T(8,128)(2,1)}, u32[]{:S(2)}) copy-start(bf16[8,16,512]{2,1,0:T(8,128)(2,1)} %shard_map.160) | copy-start | bytes 393220
  57.0 24.3 %all-to-all-start.3 = ((bf16[8,8,768]{2,1,0:T(8,128)(2,1)}), bf16[8,8,768]{2,1,0:T(8,128)(2,1)S(1)}, u32[]{:S(2)}, u32[]{:S(2)}) async-start(bf16[8,8,768]{2,1,0:T(8,128)(2,1)} %broadcast_in_dim.8), calls=%async_computation.3 | async-start | bytes 196608 | tf_op jit(solution)/shard_map/all_to_all | solution.py:338
  68.6 16.6 %collective-permute-start.3 = (bf16[2,16,512]{2,1,0:T(8,128)(2,1)S(1)}, bf16[2,16,512]{2,1,0:T(8,128)(2,1)S(1)}, u32[]{:S(2)}, u32[]{:S(2)}) collective-permute-start(bf16[2,16,512]{2,1,0:T(8,128)(2,1)S(1)} %get-tuple-element.51), channel_id=1, source_target_pairs={{128,0},{256,128},{384,256},{0,384},{129,1},{257,129},{385,257},{1... | collective-permute-start | bytes 98312 | tf_op jit(solution)/shard_map/ppermute | solution.py:47
  72.8 12.5 %collective-permute-start.2 = (bf16[2,16,512]{2,1,0:T(8,128)(2,1)S(1)}, bf16[2,16,512]{2,1,0:T(8,128)(2,1)S(1)}, u32[]{:S(2)}, u32[]{:S(2)}) collective-permute-start(bf16[2,16,512]{2,1,0:T(8,128)(2,1)S(1)} %get-tuple-element.50), channel_id=1, source_target_pairs={{0,128},{128,256},{256,384},{384,0},{1,129},{129,257},{257,385},{3... | collective-permute-start | bytes 98312 | tf_op jit(solution)/shard_map/ppermute | solution.py:47
  82.0 8.4 %all-to-all-start.4 = ((bf16[4,8,768]{2,1,0:T(8,128)(2,1)}), bf16[4,8,768]{2,1,0:T(8,128)(2,1)S(1)}, u32[]{:S(2)}, u32[]{:S(2)}) async-start(bf16[4,8,768]{2,1,0:T(8,128)(2,1)} %broadcast_in_dim.9), calls=%async_computation.4 | async-start | bytes 98304 | tf_op jit(solution)/shard_map/all_to_all | solution.py:338
  85.2 14.9 %copy-start.7 = (bf16[27,12288]{1,0:T(8,128)(2,1)S(1)}, bf16[27,12288]{1,0:T(8,128)(2,1)}, u32[]{:S(2)}) copy-start(bf16[27,12288]{1,0:T(8,128)(2,1)} %param.17) | copy-start | bytes 1990660
  91.3 23.4 %all-to-all-start.5 = ((bf16[16,32,768]{2,1,0:T(8,128)(2,1)}), bf16[16,32,768]{2,1,0:T(8,128)(2,1)S(1)}, u32[]{:S(2)}, u32[]{:S(2)}) async-start(bf16[16,32,768]{2,1,0:T(8,128)(2,1)} %broadcast_in_dim.11), calls=%async_computation.5 | async-start | bytes 1572864 | tf_op jit(solution)/shard_map/all_to_all | solution.py:338
  101.4 10.1 %collective-permute-start.5 = (bf16[12,2,512]{2,1,0:T(2,128)(2,1)S(1)}, bf16[12,2,512]{2,1,0:T(2,128)(2,1)S(1)}, u32[]{:S(2)}, u32[]{:S(2)}) collective-permute-start(bf16[12,2,512]{2,1,0:T(2,128)(2,1)S(1)} %get-tuple-element.49), channel_id=1, source_target_pairs={{32,0},{64,32},{96,64},{0,96},{33,1},{65,33},{97,65},{1,97},{34,2}... | collective-permute-start | bytes 73736 | tf_op jit(solution)/shard_map/ppermute | solution.py:47
  106.0 6.0 %collective-permute-start.4 = (bf16[12,2,512]{2,1,0:T(2,128)(2,1)S(1)}, bf16[12,2,512]{2,1,0:T(2,128)(2,1)S(1)}, u32[]{:S(2)}, u32[]{:S(2)}) collective-permute-start(bf16[12,2,512]{2,1,0:T(2,128)(2,1)S(1)} %get-tuple-element.48), channel_id=1, source_target_pairs={{0,32},{32,64},{64,96},{96,0},{1,33},{33,65},{65,97},{97,1},{2,34}... | collective-permute-start | bytes 73736 | tf_op jit(solution)/shard_map/ppermute | solution.py:47
  112.2 2.6 %copy-start.1 = (bf16[512,64]{1,0:T(8,128)(2,1)S(1)}, bf16[512,64]{1,0:T(8,128)(2,1)}, u32[]{:S(2)}) copy-start(bf16[512,64]{1,0:T(8,128)(2,1)} %constant.45.clone.choice_ref) | copy-start | bytes 196612

commit v7 on v6

--- a/solution.py
+++ b/solution.py
@@ -64,7 +64,10 @@
 
 def plane_inputs(coarse, skip_features):
     parts = pl.pallas_call(
-        message_kernel, out_shape=jax.ShapeDtypeStruct((BLOCKS, 160, 256), BF16)
+        message_kernel,
+        out_shape=jax.ShapeDtypeStruct((BLOCKS, 160, 256), BF16),
+        out_specs=pl.BlockSpec(memory_space=pl.ANY),
+        scratch_shapes=[pltpu.SemaphoreType.DMA((2, BLOCKS))],
     )(coarse.reshape(32, 256), skip_features.reshape(128, 256))
     return traded(parts, PLANE)
 
@@ -94,21 +97,16 @@
 
 
 def row_choices():
-    pre_at = lambda z, c: c if z < 0 else 352 + c if z > 3 else 80 + 64 * z + c
-    cot_at = lambda z, o: 76 + 3 * z + o if z < 0 else 404 + 3 * z + o if z > 3 else 336 + 3 * z + o
-    shares = np.zeros((BLOCKS, ROWS, 432), np.float32)
-    cots = np.zeros((24, 432), np.float32)
-    lanes = np.zeros((432, 512), np.float32)
-    for z in range(-1, 5):
+    shares = np.zeros((BLOCKS, 6, OWN, 384), np.float32)
+    cots = np.zeros((128, 48), np.float32)
+    for z in range(6):
         for c in range(C_HID):
-            shares[c // OWN, OWN * (z + 1) + c % OWN, pre_at(z, c)] = 1.0
-            lanes[pre_at(z, c), C_HID * (z + 1) + c] = 1.0
+            shares[c // OWN, z, c % OWN, C_HID * z + c] = 1.0
     for z in range(-2, 6):
+        start = 12 + 3 * z if z < 0 else 20 + 3 * z if z > 3 else 16 + 3 * z
         for o in range(C_VEL):
-            cots[C_VEL * (z + 2) + o, cot_at(z, o)] = 1.0
-            lanes[cot_at(z, o), 384 + C_VEL * (z + 2) + o] = 1.0
-    rows = np.concatenate([shares.reshape(BLOCKS * ROWS, 432), cots], axis=0)
-    return jnp.asarray(rows, BF16), jnp.asarray(lanes, BF16)
+            cots[C_VEL * (z + 2) + o, start + o] = 1.0
+    return jnp.asarray(shares.reshape(384, 384), BF16), jnp.asarray(cots, BF16)
 
 
 def choices():
@@ -131,7 +129,7 @@
             double[x, y, x // 2, y // 2] = 1.0
     return (
         jnp.asarray(tap_rows.reshape(2, 256, 216), BF16),
-        jnp.asarray(head_columns.reshape(216, 512)),
+        jnp.asarray(head_columns.reshape(216, 512), BF16),
         jnp.asarray(head_rows.reshape(32, ROWS)),
     ), jnp.asarray(double.reshape(128, 32), BF16)
 
@@ -154,22 +152,25 @@
     low_ref[64:80, :] = cot_ref[...]
 
 
-def joined(before_ref, rows_ref, after_ref):
-    return jnp.concatenate([before_ref[...], rows_ref[...], after_ref[...]], axis=0)
-
-
-def parts_kernel(before_ref, rows_ref, after_ref, choice_ref, parts_ref):
-    rows = joined(before_ref, rows_ref, after_ref)
-    parts = jnp.dot(choice_ref[...], rows, preferred_element_type=F32)
-    cot = parts[BLOCKS * ROWS :]
-    for at in range(BLOCKS):
-        both = jnp.concatenate([parts[ROWS * at : ROWS * at + ROWS], cot], axis=0)
+def joined(before_ref, rows_ref, after_ref, cot_choice_ref):
+    pre = jnp.concatenate([before_ref[0:64, :], rows_ref[0:256, :], after_ref[0:64, :]], axis=0)
+    cot = jnp.concatenate(
+        [before_ref[64:80, :], rows_ref[256:272, :], after_ref[64:80, :]], axis=0
+    )
+    return pre, jnp.dot(cot_choice_ref[...], cot, preferred_element_type=F32)
+
+
+def parts_kernel(before_ref, rows_ref, after_ref, choice_ref, cot_choice_ref, parts_ref):
+    pre, cot = joined(before_ref, rows_ref, after_ref, cot_choice_ref)
+    parts = jnp.dot(choice_ref[...], pre, preferred_element_type=F32)
+    for at in range(BLOCKS):
+        both = jnp.concatenate([parts[ROWS * at : ROWS * at + ROWS], cot[0:24]], axis=0)
         parts_ref[at] = both.astype(BF16)
 
 
-def field_kernel(before_ref, rows_ref, after_ref, choice_ref, field_ref):
-    turned = joined(before_ref, rows_ref, after_ref).astype(F32).T.astype(BF16)
-    field = jnp.dot(turned, choice_ref[...], preferred_element_type=F32)
+def field_kernel(before_ref, rows_ref, after_ref, cot_choice_ref, field_ref):
+    pre, cot = joined(before_ref, rows_ref, after_ref, cot_choice_ref)
+    field = jnp.concatenate([pre.astype(F32), cot], axis=0).T
     field_ref[...] = field.astype(BF16).reshape(SIZE_X, SIZE_Y, 512)
 
 
@@ -182,7 +183,7 @@
         rows, choice_ref[...], (((0,), (0,)), ((), ())), preferred_element_type=F32
     )
     for o in range(C_VEL):
-        head_ref[:, o, :] = head[32 * o : 32 * o + 27] * NORM
+        head_ref[o] = head[32 * o : 32 * o + 27] * NORM
 
 
 def input_matrix(weight_one):
@@ -235,10 +236,19 @@
                 stack_ref[start : start + ROWS, 128 * at : 128 * at + 128] = block
 
 
-def message_kernel(coarse_ref, skip_ref, parts_ref):
-    for at in range(BLOCKS):
-        parts_ref[at, 0:32, :] = coarse_ref[...]
-        parts_ref[at, 32:160, :] = skip_ref[...]
+def message_kernel(coarse_ref, skip_ref, parts_ref, sems):
+    copies = []
+    for at in range(BLOCKS):
+        copies.append(
+            pltpu.make_async_copy(coarse_ref, parts_ref.at[at, 0:32, :], sems.at[0, at])
+        )
+        copies.append(
+            pltpu.make_async_copy(skip_ref, parts_ref.at[at, 32:160, :], sems.at[1, at])
+        )
+    for copy in copies:
+        copy.start()
+    for copy in copies:
+        copy.wait()
 
 
 def fine_kernel(input_ref, double_ref, fine_ref):
@@ -260,7 +270,9 @@
     d_pre = (d_hidden * gelu_slope(pre)).astype(BF16).astype(F32)
     hidden = gelu_value(pre).astype(BF16)
     pairs = lax.dot_general(hidden, cot, (((1,), (1,)), ((), ())), preferred_element_type=F32)
-    spans = jnp.dot(pairs, column_ref[...], precision=HIGHEST, preferred_element_type=F32)
+    spans = jnp.dot(
+        pairs, column_ref[...].astype(F32), precision=HIGHEST, preferred_element_type=F32
+    )
     depth = lax.broadcasted_iota(jnp.int32, (ROWS, 128), 0) // OWN
     kept = jnp.zeros((ROWS, 128), F32)
     for z in range(SIZE_Z):
@@ -347,10 +359,10 @@
     inputs = plane_inputs(coarse, skip_features)
     head = head_matrix(weight_out)
     deep = depth_rims(pre_act, cotangent)
-    share_choice, field_choice = row_choices()
+    share_choice, cot_choice = row_choices()
     parts = pl.pallas_call(
         parts_kernel, out_shape=jax.ShapeDtypeStruct((BLOCKS, 48, 128), BF16)
-    )(*deep, share_choice)
+    )(*deep, share_choice, cot_choice)
     parts, inputs = lax.optimization_barrier((parts, inputs))
     data = traded(parts, PLANE)
     chosen, double = choices()
@@ -367,7 +379,7 @@
         cost_estimate=pl.CostEstimate(
             flops=60_000_000, bytes_accessed=4_000_000, transcendentals=0
         ),
-    )(*deep, field_choice)
+    )(*deep, cot_choice)
     data, fine, field = lax.optimization_barrier((data, fine, field))
     share = pl.pallas_call(
         share_kernel,
@@ -380,16 +392,16 @@
     )(data, fine, own_head_matrix(head), *chosen)
     near = jnp.sum(traded(share.reshape(4, 8, SHARE[1]), NEAR), axis=0)
     field, near = lax.optimization_barrier((field, near))
-    field = with_x_rims(field)
+    field = with_y_rims(with_x_rims(field))
     far = jnp.sum(spread(near.astype(BF16), FAR).astype(F32), axis=0)
+    field, far = lax.optimization_barrier((field, far))
     column = spread(far.astype(BF16), NEAR).reshape(SHARE)
     field, column = lax.optimization_barrier((field, column))
-    field = with_y_rims(field)
     body, head_grad = pl.pallas_call(
         unpack_kernel,
         out_shape=(
             jax.ShapeDtypeStruct((27, C_HID * 192), F32),
-            jax.ShapeDtypeStruct((27, C_VEL, C_HID), F32),
+            jax.ShapeDtypeStruct((C_VEL, 27, C_HID), F32),
         ),
         compiler_params=pltpu.CompilerParams(vmem_limit_bytes=16 * 2**20),
     )(spread(column, PLANE), head_channels())
@@ -410,7 +422,7 @@
             flops=700_000_000, bytes_accessed=3_000_000, transcendentals=100_000
         ),
     )(field, head, input_matrix(weight_one))
-    return coarse_grad.reshape(4, 8, 256), skip_grad, body, head_grad
+    return coarse_grad.reshape(4, 8, 256), skip_grad, body, jnp.transpose(head_grad, (1, 0, 2))
 
 
 def solution(mesh):

time: 118 us -> 120 us (1.017)
  blocking collectives: 7.92 us -> 15.6 us
  starting transfers between devices: 63.3 us -> 59.1 us
  local copies, waits for them, and re-layouts: 8.02 us -> 6.8 us
    all_to_all x1 -> x2, blocking collectives: 7.92 us -> 15.6 us  [traded(): return lax.all_to_all(parts, axes, 0, 0)]
    ppermute x3, waiting for transfers between devices: 0.47 us -> 4.06 us  [from_both(): lax.ppermute(to_next, axis, up)]
    all_to_all x5 -> x4, starting transfers between devices: 39 us -> 35.5 us  [traded(): return lax.all_to_all(parts, axes, 0, 0)]
    ppermute x3, waiting for transfers between devices: 4.25 us -> 1 us  [from_both(): lax.ppermute(to_previous, axis, down)]
    ppermute x3, starting transfers between devices: 18.6 us -> 16.1 us  [from_both(): lax.ppermute(to_previous, axis, down)]
    ppermute x3, starting transfers between devices: 5.75 us -> 7.51 us  [from_both(): lax.ppermute(to_next, axis, up)]
    unnamed x25 -> x26, local copies, waits for them, and re-layouts: 2.86 us -> 2.25 us
    all_to_all x5 -> x4, waiting for transfers between devices: 13.3 us -> 13.1 us  [traded(): return lax.all_to_all(parts, axes, 0, 0)]
  transfers between devices with their start and end apart: 11 -> 10, of which waited for: 7 -> 6; matrix products, arithmetic and copies ran while one was open for 4% -> 3% of each run, Pallas kernels for 10% -> 9%
where the time goes in v7:
time: 120 us; the launch traced here: 119 us
  starting transfers between devices  59.1 us (49%)
  waiting for transfers between devices  18.2 us (15%)
  Pallas kernels  17.8 us (15%)
  blocking collectives  15.6 us (13%)
  local copies, waits for them, and re-layouts  6.8 us (6%)
    all_to_all x4, starting transfers between devices, traded(): return lax.all_to_all(parts, axes, 0, 0)  35.5 us
    ppermute x3, starting transfers between devices, from_both(): lax.ppermute(to_previous, axis, down)  16.1 us
    all_to_all x2, blocking collectives, traded(): return lax.all_to_all(parts, axes, 0, 0)  15.6 us
    all_to_all x4, waiting for transfers between devices, traded(): return lax.all_to_all(parts, axes, 0, 0)  13.1 us
    ppermute x3, starting transfers between devices, from_both(): lax.ppermute(to_next, axis, up)  7.51 us
    ppermute x3, waiting for transfers between devices, from_both(): lax.ppermute(to_next, axis, up)  4.06 us
    pallas_call x1, Pallas kernels, per_device(): pl.pallas_call(fine_kernel, out_shape=jax.ShapeDtypeStruct((2, 2048, 256)...  3.24 us
    pallas_call x1, Pallas kernels, per_device(): pl.pallas_call(share_kernel, out_shape=jax.ShapeDtypeStruct(SHARE, F32),...  3.14 us
  transfers between devices with their start and end apart: 10, of which 6 were waited for; matrix products, arithmetic and copies ran while one was open for 3% of the time, Pallas kernels for 9%

profile of v7, /device:TPU:1, one launch (start us, length us, event | category | flops | bytes accessed | tf_op | source)
XLA Modules:
  0.0 118.9 jit_solution(13729277383539927418)
XLA Ops:
  0.6 2.2 %shard_map.158 = bf16[16,160,256]{2,1,0:T(8,128)(2,1)} custom-call(bf16[32,256]{1,0:T(8,128)(2,1)} %bitcast.26, bf16[128,256]{1,0:T(8,128)(2,1)} %bitcast.23), custom_call_target="tpu_custom_call" | custom-call | tf_op jit(solution)/shard_map/pallas_call | solution.py:66
  2.8 0.0 copy-start.10
  2.8 0.0 copy-start.11
  2.8 10.4 %all-to-all-start = ((bf16[16,160,256]{2,1,0:T(8,128)(2,1)}), bf16[16,160,256]{2,1,0:T(8,128)(2,1)S(1)}, u32[]{:S(2)}, u32[]{:S(2)}) async-start(bf16[16,160,256]{2,1,0:T(8,128)(2,1)} %shard_map.158), calls=%async_computation | async-start | bytes 2621440 | tf_op jit(solution)/shard_map/all_to_all | solution.py:350
  13.2 0.0 copy-done.10
  13.3 0.1 reshape.51
  13.3 0.6 pad.32.cot_ref
  14.0 1.6 %shard_map.156 = (bf16[272,128]{1,0:T(8,128)(2,1)}, bf16[80,128]{1,0:T(8,128)(2,1)}, bf16[80,128]{1,0:T(8,128)(2,1)}) custom-call(bf16[128,256]{1,0:T(8,128)(2,1)} %bitcast.24, bf16[16,128]{1,0:T(8,128)(2,1)} %pad.32.cot_ref), custom_call_target="tpu_custom_call" | custom-call | tf_op jit(solution)/shard_map/pallas_call | solution.py:53
  15.5 1.9 %collective-permute-start = (bf16[80,128]{1,0:T(8,128)(2,1)}, bf16[80,128]{1,0:T(8,128)(2,1)S(1)}, u32[]{:S(2)}, u32[]{:S(2)}) collective-permute-start(bf16[80,128]{1,0:T(8,128)(2,1)} %get-tuple-element.22), channel_id=1, source_target_pairs={{0,1},{1,2},{2,3},{3,4},{4,5},{5,6},{6,7},{7,8},{8,9},{9,10},{10,1... | collective-permute-start | bytes 61448 | tf_op jit(solution)/shard_map/ppermute | solution.py:47
  17.5 9.9 %collective-permute-start.1 = (bf16[80,128]{1,0:T(8,128)(2,1)}, bf16[80,128]{1,0:T(8,128)(2,1)S(1)}, u32[]{:S(2)}, u32[]{:S(2)}) collective-permute-start(bf16[80,128]{1,0:T(8,128)(2,1)} %get-tuple-element.24), channel_id=1, source_target_pairs={{1,0},{2,1},{3,2},{4,3},{5,4},{6,5},{7,6},{8,7},{9,8},{10,9},{11,1... | collective-permute-start | bytes 61448 | tf_op jit(solution)/shard_map/ppermute | solution.py:47
  27.4 0.0 copy-done.11
  27.5 0.0 collective-permute-done.before_ref
  27.5 0.0 copy-start.8
  27.5 1.0 collective-permute-done.1.after_ref
  28.5 0.0 copy-start.9
  28.5 0.0 copy-done.8
  28.5 0.6 copy-done.9
  29.1 1.9 %shard_map.157 = bf16[16,48,128]{2,1,0:T(8,128)(2,1)} custom-call(bf16[80,128]{1,0:T(8,128)(2,1)} %copy-done.8, bf16[272,128]{1,0:T(8,128)(2,1)} %get-tuple-element.23.rows_ref, bf16[80,128]{1,0:T(8,128)(2,1)} %copy-done.9, bf16[384,384]{1,0:T(8,128)(2,1)} %constant.38.clone.choice_ref, bf16[128,48]{1,0:T(8,128)(2,1)} %constant.39.clone.cot_choice_ref), custom_call_target="tpu_custom_call" | custom-call | tf_op jit(solution)/shard_map/pallas_call | solution.py:363
  31.0 1.3 %all-to-all-done.input_ref = bf16[16,160,256]{2,1,0:T(8,128)(2,1)S(1)} async-done(((bf16[16,160,256]{2,1,0:T(8,128)(2,1)}), bf16[16,160,256]{2,1,0:T(8,128)(2,1)S(1)}, u32[]{:S(2)}, u32[]{:S(2)}) %all-to-all-start) | async-done | bytes 1310752 | tf_op jit(solution)/shard_map/all_to_all | solution.py:350
  32.3 0.0 copy-start.5
  32.3 4.7 %all-to-all-start.1 = ((bf16[16,48,128]{2,1,0:T(8,128)(2,1)}), bf16[16,48,128]{2,1,0:T(8,128)(2,1)S(1)}, u32[]{:S(2)}, u32[]{:S(2)}) async-start(bf16[16,48,128]{2,1,0:T(8,128)(2,1)} %shard_map.157), calls=%async_computation.1 | async-start | bytes 393216 | tf_op jit(solution)/shard_map/all_to_all | solution.py:350
  37.0 0.1 fusion.5
  37.1 0.2 concatenate.12.head_ref
  37.3 0.4 copy.25
  37.7 0.0 copy-done.5
  37.8 0.1 reshape.57.head_ref
  37.9 1.8 %shard_map.160 = bf16[8,16,512]{2,1,0:T(8,128)(2,1)} custom-call(bf16[80,128]{1,0:T(8,128)(2,1)} %copy-done.8, bf16[272,128]{1,0:T(8,128)(2,1)} %get-tuple-element.23.rows_ref, bf16[80,128]{1,0:T(8,128)(2,1)} %copy-done.9, bf16[128,48]{1,0:T(8,128)(2,1)} %constant.39.clone.cot_choice_ref), custom_call_target="tpu_custom_call" | custom-call | flops 60000000 | bytes 4000000 | tf_op jit(solution)/shard_map/pallas_call | solution.py:376
  39.7 3.2 %shard_map.159.fine_ref = bf16[2,2048,256]{2,1,0:T(8,128)(2,1)} custom-call(bf16[16,160,256]{2,1,0:T(8,128)(2,1)} %copy-done.5, bf16[128,32]{1,0:T(8,128)(2,1)} %constant.43.clone.double_ref), custom_call_target="tpu_custom_call" | custom-call | flops 300000000 | bytes 4000000 | tf_op jit(solution)/shard_map/pallas_call | solution.py:369
  42.9 0.8 all-to-all-done.1.data_ref
  43.7 0.0 copy-done.2
  43.7 0.0 copy-done.3
  43.7 0.0 copy-done.4
  43.7 0.0 copy-start
  43.7 1.6 %copy-done = bf16[2,2048,256]{2,1,0:T(8,128)(2,1)S(1)} copy-done((bf16[2,2048,256]{2,1,0:T(8,128)(2,1)S(1)}, bf16[2,2048,256]{2,1,0:T(8,128)(2,1)}, u32[]{:S(2)}) %copy-start) | copy-done | bytes 2097176
  45.3 3.1 %shard_map.161 = f32[32,768]{1,0:T(8,128)S(1)} custom-call(bf16[16,48,128]{2,1,0:T(8,128)(2,1)S(1)} %all-to-all-done.1.data_ref, bf16[2,2048,256]{2,1,0:T(8,128)(2,1)S(1)} %copy-done, bf16[24,216]{1,0:T(8,128)(2,1)S(1)} %reshape.57.head_ref, bf16[2,256,216]{2,1,0:T(8,128)(2,1)S(1)} %copy-done.2, bf16[216,512]{1,0:T(8,128)(2,1)S(1)} %copy-done.3, ...), custom_call_target="tpu_custom_call" | custom-call | flops 1500000000 | bytes 2000000 | tf_op jit(solution)/shard_map/pallas_call | solution.py:384
  48.4 7.9 %all_to_all.30 = f32[4,8,768]{2,1,0:T(8,128)S(1)} all-to-all(f32[4,8,768]{2,1,0:T(8,128)S(1)} %bitcast.17), channel_id=1, replica_groups=mesh['gx'=4,'gy'=4,'gzh'=2,'gzm'=8,'gzl'=2] {'gzh','gzl'}, dimensions={0} | all-to-all | bytes 196608 | tf_op jit(solution)/shard_map/all_to_all | solution.py:350
  56.4 0.0 copy-done.6
  56.4 3.7 %collective-permute-start.2 = (bf16[2,16,512]{2,1,0:T(8,128)(2,1)S(1)}, bf16[2,16,512]{2,1,0:T(8,128)(2,1)S(1)}, u32[]{:S(2)}, u32[]{:S(2)}) collective-permute-start(bf16[2,16,512]{2,1,0:T(8,128)(2,1)S(1)} %get-tuple-element.43), channel_id=1, source_target_pairs={{0,128},{128,256},{256,384},{384,0},{1,129},{129,257},{257,385},{3... | collective-permute-start | bytes 98312 | tf_op jit(solution)/shard_map/ppermute | solution.py:47
  60.1 2.1 %collective-permute-start.3 = (bf16[2,16,512]{2,1,0:T(8,128)(2,1)S(1)}, bf16[2,16,512]{2,1,0:T(8,128)(2,1)S(1)}, u32[]{:S(2)}, u32[]{:S(2)}) collective-permute-start(bf16[2,16,512]{2,1,0:T(8,128)(2,1)S(1)} %get-tuple-element.42), channel_id=1, source_target_pairs={{128,0},{256,128},{384,256},{0,384},{129,1},{257,129},{385,257},{1... | collective-permute-start | bytes 98312 | tf_op jit(solution)/shard_map/ppermute | solution.py:47
  62.2 0.6 broadcast_in_dim.9
  62.9 11.7 %all-to-all-start.3 = ((bf16[8,8,768]{2,1,0:T(8,128)(2,1)}), bf16[8,8,768]{2,1,0:T(8,128)(2,1)S(1)}, u32[]{:S(2)}, u32[]{:S(2)}) async-start(bf16[8,8,768]{2,1,0:T(8,128)(2,1)} %broadcast_in_dim.9), calls=%async_computation.3 | async-start | bytes 196608 | tf_op jit(solution)/shard_map/all_to_all | solution.py:350
  74.5 0.0 collective-permute-done.2
  74.6 0.0 collective-permute-done.3
  74.6 4.0 %collective-permute-start.5 = (bf16[12,2,512]{2,1,0:T(2,128)(2,1)S(1)}, bf16[12,2,512]{2,1,0:T(2,128)(2,1)S(1)}, u32[]{:S(2)}, u32[]{:S(2)}) collective-permute-start(bf16[12,2,512]{2,1,0:T(2,128)(2,1)S(1)} %get-tuple-element.41), channel_id=1, source_target_pairs={{32,0},{64,32},{96,64},{0,96},{33,1},{65,33},{97,65},{1,97},{34,2}... | collective-permute-start | bytes 73736 | tf_op jit(solution)/shard_map/ppermute | solution.py:47
  78.7 1.9 %collective-permute-start.4 = (bf16[12,2,512]{2,1,0:T(2,128)(2,1)S(1)}, bf16[12,2,512]{2,1,0:T(2,128)(2,1)S(1)}, u32[]{:S(2)}, u32[]{:S(2)}) collective-permute-start(bf16[12,2,512]{2,1,0:T(2,128)(2,1)S(1)} %get-tuple-element.40), channel_id=1, source_target_pairs={{0,32},{32,64},{64,96},{96,0},{1,33},{33,65},{65,97},{97,1},{2,34}... | collective-permute-start | bytes 73736 | tf_op jit(solution)/shard_map/ppermute | solution.py:47
  80.6 0.1 pad.45.clone
  80.7 0.0 collective-permute-done.5
  80.7 4.1 %collective-permute-done.4 = bf16[12,2,512]{2,1,0:T(2,128)(2,1)S(1)} collective-permute-done((bf16[12,2,512]{2,1,0:T(2,128)(2,1)S(1)}, bf16[12,2,512]{2,1,0:T(2,128)(2,1)S(1)}, u32[]{:S(2)}, u32[]{:S(2)}) %collective-permute-start.4) | collective-permute-done | bytes 24608 | tf_op jit(solution)/shard_map/ppermute | solution.py:47
  84.7 0.2 maximum_maximum_fusion.field_ref
  84.9 2.4 %all-to-all-done.3 = bf16[8,8,768]{2,1,0:T(8,128)(2,1)S(1)} async-done(((bf16[8,8,768]{2,1,0:T(8,128)(2,1)}), bf16[8,8,768]{2,1,0:T(8,128)(2,1)S(1)}, u32[]{:S(2)}, u32[]{:S(2)}) %all-to-all-start.3) | async-done | bytes 98336 | tf_op jit(solution)/shard_map/all_to_all | solution.py:350
  87.3 0.0 copy-start.7
  87.3 7.6 %all_to_all.31 = bf16[4,8,768]{2,1,0:T(8,128)(2,1)S(1)} all-to-all(bf16[4,8,768]{2,1,0:T(8,128)(2,1)S(1)} %broadcast_in_dim.10), channel_id=1, replica_groups=mesh['gx'=4,'gy'=4,'gzh'=2,'gzm'=8,'gzl'=2] {'gzh','gzl'}, dimensions={0} | all-to-all | bytes 98304 | tf_op jit(solution)/shard_map/all_to_all | solution.py:350
  95.0 1.0 broadcast_in_dim.11
  96.0 8.7 %all-to-all-start.5 = ((bf16[16,32,768]{2,1,0:T(8,128)(2,1)}), bf16[16,32,768]{2,1,0:T(8,128)(2,1)S(1)}, u32[]{:S(2)}, u32[]{:S(2)}) async-start(bf16[16,32,768]{2,1,0:T(8,128)(2,1)} %broadcast_in_dim.11), calls=%async_computation.5 | async-start | bytes 1572864 | tf_op jit(solution)/shard_map/all_to_all | solution.py:350
  104.7 0.0 copy-done.7
  104.7 1.0 reshape.60
  105.7 0.1 rev.7
  105.8 0.1 slice.27
  105.9 0.3 fusion.2.weight_ref
  106.2 0.0 copy-start.1
  106.2 2.6 %shard_map.162 = (bf16[8,16,256]{2,1,0:T(8,128)(2,1)}, bf16[32,256]{1,0:T(8,128)(2,1)}) custom-call(bf16[12,32,512]{2,1,0:T(8,128)(2,1)S(1)} %maximum_maximum_fusion.field_ref, bf16[9,32,384]{2,1,0:T(8,128)(2,1)S(1)} %concatenate.12.head_ref, bf16[9,256,256]{2,1,0:T(8,128)(2,1)S(1)} %fusion.2.weight_ref), custom_call_target="tpu_custom_call" | custom-call | flops 700000000 | bytes 3000000 | tf_op jit(solution)/shard_map/pallas_call | solution.py:408
  108.8 8.7 %all-to-all-done.5.share_ref = bf16[16,32,768]{2,1,0:T(8,128)(2,1)S(1)} async-done(((bf16[16,32,768]{2,1,0:T(8,128)(2,1)}), bf16[16,32,768]{2,1,0:T(8,128)(2,1)S(1)}, u32[]{:S(2)}, u32[]{:S(2)}) %all-to-all-start.5) | async-done | bytes 786464 | tf_op jit(solution)/shard_map/all_to_all | solution.py:350
  117.5 0.0 copy-done.1
  117.5 1.4 %shard_map.163 = (f32[27,12288]{1,0:T(8,128)}, f32[3,27,64]{2,1,0:T(8,128)}) custom-call(bf16[16,32,768]{2,1,0:T(8,128)(2,1)S(1)} %all-to-all-done.5.share_ref, bf16[512,64]{1,0:T(8,128)(2,1)S(1)} %copy-done.1), custom_call_target="tpu_custom_call" | custom-call | tf_op jit(solution)/shard_map/pallas_call | solution.py:400
  (20 shorter events, 0.2 us)
Async XLA Ops:
  2.8 10.4 %copy-start.10 = (bf16[3,8,16,4]{2,3,1,0:T(4,128)(2,1)S(1)}, bf16[3,8,16,4]{2,3,1,0:T(4,128)(2,1)}, u32[]{:S(2)}) copy-start(bf16[3,8,16,4]{2,3,1,0:T(4,128)(2,1)} %param.16) | copy-start | bytes 9220
  2.8 24.6 %copy-start.11 = (bf16[27,3,64]{2,0,1:T(8,128)(2,1)S(1)}, bf16[27,3,64]{2,0,1:T(8,128)(2,1)}, u32[]{:S(2)}) copy-start(bf16[27,3,64]{2,0,1:T(8,128)(2,1)} %param.18) | copy-start | bytes 31108
  2.8 29.5 %all-to-all-start = ((bf16[16,160,256]{2,1,0:T(8,128)(2,1)}), bf16[16,160,256]{2,1,0:T(8,128)(2,1)S(1)}, u32[]{:S(2)}, u32[]{:S(2)}) async-start(bf16[16,160,256]{2,1,0:T(8,128)(2,1)} %shard_map.158), calls=%async_computation | async-start | bytes 2621440 | tf_op jit(solution)/shard_map/all_to_all | solution.py:350
  15.5 11.9 %collective-permute-start = (bf16[80,128]{1,0:T(8,128)(2,1)}, bf16[80,128]{1,0:T(8,128)(2,1)S(1)}, u32[]{:S(2)}, u32[]{:S(2)}) collective-permute-start(bf16[80,128]{1,0:T(8,128)(2,1)} %get-tuple-element.22), channel_id=1, source_target_pairs={{0,1},{1,2},{2,3},{3,4},{4,5},{5,6},{6,7},{7,8},{8,9},{9,10},{10,1... | collective-permute-start | bytes 61448 | tf_op jit(solution)/shard_map/ppermute | solution.py:47
  17.5 11.0 %collective-permute-start.1 = (bf16[80,128]{1,0:T(8,128)(2,1)}, bf16[80,128]{1,0:T(8,128)(2,1)S(1)}, u32[]{:S(2)}, u32[]{:S(2)}) collective-permute-start(bf16[80,128]{1,0:T(8,128)(2,1)} %get-tuple-element.24), channel_id=1, source_target_pairs={{1,0},{2,1},{3,2},{4,3},{5,4},{6,5},{7,6},{8,7},{9,8},{10,9},{11,1... | collective-permute-start | bytes 61448 | tf_op jit(solution)/shard_map/ppermute | solution.py:47
  27.5 1.0 copy-start.8
  28.5 0.6 copy-start.9
  32.3 5.4 %copy-start.5 = (bf16[16,160,256]{2,1,0:T(8,128)(2,1)}, bf16[16,160,256]{2,1,0:T(8,128)(2,1)S(1)}, u32[]{:S(2)}) copy-start(bf16[16,160,256]{2,1,0:T(8,128)(2,1)S(1)} %all-to-all-done.input_ref) | copy-start | bytes 3932164
  32.3 11.4 %all-to-all-start.1 = ((bf16[16,48,128]{2,1,0:T(8,128)(2,1)}), bf16[16,48,128]{2,1,0:T(8,128)(2,1)S(1)}, u32[]{:S(2)}, u32[]{:S(2)}) async-start(bf16[16,48,128]{2,1,0:T(8,128)(2,1)} %shard_map.157), calls=%async_computation.1 | async-start | bytes 393216 | tf_op jit(solution)/shard_map/all_to_all | solution.py:350
  39.7 4.0 %copy-start.2 = (bf16[2,256,216]{2,1,0:T(8,128)(2,1)S(1)}, bf16[2,256,216]{2,1,0:T(8,128)(2,1)}, u32[]{:S(2)}) copy-start(bf16[2,256,216]{2,1,0:T(8,128)(2,1)} %constant.40.clone.tap_ref) | copy-start | bytes 663556
  39.7 4.0 %copy-start.3 = (bf16[216,512]{1,0:T(8,128)(2,1)S(1)}, bf16[216,512]{1,0:T(8,128)(2,1)}, u32[]{:S(2)}) copy-start(bf16[216,512]{1,0:T(8,128)(2,1)} %constant.41.clone.column_ref) | copy-start | bytes 663556
  39.7 4.0 %copy-start.4 = (f32[32,24]{1,0:T(8,128)S(1)}, f32[32,24]{1,0:T(8,128)}, u32[]{:S(2)}) copy-start(f32[32,24]{1,0:T(8,128)} %constant.42.clone.row_ref) | copy-start | bytes 9220
  43.7 1.6 %copy-start = (bf16[2,2048,256]{2,1,0:T(8,128)(2,1)S(1)}, bf16[2,2048,256]{2,1,0:T(8,128)(2,1)}, u32[]{:S(2)}) copy-start(bf16[2,2048,256]{2,1,0:T(8,128)(2,1)} %shard_map.159.fine_ref) | copy-start | bytes 6291460
  45.3 11.1 %copy-start.6 = (bf16[8,16,512]{2,1,0:T(8,128)(2,1)S(1)}, bf16[8,16,512]{2,1,0:T(8,128)(2,1)}, u32[]{:S(2)}) copy-start(bf16[8,16,512]{2,1,0:T(8,128)(2,1)} %shard_map.160) | copy-start | bytes 393220
  56.4 18.2 %collective-permute-start.2 = (bf16[2,16,512]{2,1,0:T(8,128)(2,1)S(1)}, bf16[2,16,512]{2,1,0:T(8,128)(2,1)S(1)}, u32[]{:S(2)}, u32[]{:S(2)}) collective-permute-start(bf16[2,16,512]{2,1,0:T(8,128)(2,1)S(1)} %get-tuple-element.43), channel_id=1, source_target_pairs={{0,128},{128,256},{256,384},{384,0},{1,129},{129,257},{257,385},{3... | collective-permute-start | bytes 98312 | tf_op jit(solution)/shard_map/ppermute | solution.py:47
  60.1 14.5 %collective-permute-start.3 = (bf16[2,16,512]{2,1,0:T(8,128)(2,1)S(1)}, bf16[2,16,512]{2,1,0:T(8,128)(2,1)S(1)}, u32[]{:S(2)}, u32[]{:S(2)}) collective-permute-start(bf16[2,16,512]{2,1,0:T(8,128)(2,1)S(1)} %get-tuple-element.42), channel_id=1, source_target_pairs={{128,0},{256,128},{384,256},{0,384},{129,1},{257,129},{385,257},{1... | collective-permute-start | bytes 98312 | tf_op jit(solution)/shard_map/ppermute | solution.py:47
  62.9 24.4 %all-to-all-start.3 = ((bf16[8,8,768]{2,1,0:T(8,128)(2,1)}), bf16[8,8,768]{2,1,0:T(8,128)(2,1)S(1)}, u32[]{:S(2)}, u32[]{:S(2)}) async-start(bf16[8,8,768]{2,1,0:T(8,128)(2,1)} %broadcast_in_dim.9), calls=%async_computation.3 | async-start | bytes 196608 | tf_op jit(solution)/shard_map/all_to_all | solution.py:350
  74.6 6.0 %collective-permute-start.5 = (bf16[12,2,512]{2,1,0:T(2,128)(2,1)S(1)}, bf16[12,2,512]{2,1,0:T(2,128)(2,1)S(1)}, u32[]{:S(2)}, u32[]{:S(2)}) collective-permute-start(bf16[12,2,512]{2,1,0:T(2,128)(2,1)S(1)} %get-tuple-element.41), channel_id=1, source_target_pairs={{32,0},{64,32},{96,64},{0,96},{33,1},{65,33},{97,65},{1,97},{34,2}... | collective-permute-start | bytes 73736 | tf_op jit(solution)/shard_map/ppermute | solution.py:47
  78.7 6.1 %collective-permute-start.4 = (bf16[12,2,512]{2,1,0:T(2,128)(2,1)S(1)}, bf16[12,2,512]{2,1,0:T(2,128)(2,1)S(1)}, u32[]{:S(2)}, u32[]{:S(2)}) collective-permute-start(bf16[12,2,512]{2,1,0:T(2,128)(2,1)S(1)} %get-tuple-element.40), channel_id=1, source_target_pairs={{0,32},{32,64},{64,96},{96,0},{1,33},{33,65},{65,97},{97,1},{2,34}... | collective-permute-start | bytes 73736 | tf_op jit(solution)/shard_map/ppermute | solution.py:47
  87.3 17.4 %copy-start.7 = (bf16[27,12288]{1,0:T(8,128)(2,1)S(1)}, bf16[27,12288]{1,0:T(8,128)(2,1)}, u32[]{:S(2)}) copy-start(bf16[27,12288]{1,0:T(8,128)(2,1)} %param.17) | copy-start | bytes 1990660
  96.0 21.5 %all-to-all-start.5 = ((bf16[16,32,768]{2,1,0:T(8,128)(2,1)}), bf16[16,32,768]{2,1,0:T(8,128)(2,1)S(1)}, u32[]{:S(2)}, u32[]{:S(2)}) async-start(bf16[16,32,768]{2,1,0:T(8,128)(2,1)} %broadcast_in_dim.11), calls=%async_computation.5 | async-start | bytes 1572864 | tf_op jit(solution)/shard_map/all_to_all | solution.py:350
  106.2 11.3 %copy-start.1 = (bf16[512,64]{1,0:T(8,128)(2,1)S(1)}, bf16[512,64]{1,0:T(8,128)(2,1)}, u32[]{:S(2)}) copy-start(bf16[512,64]{1,0:T(8,128)(2,1)} %constant.44.clone.choice_ref) | copy-start | bytes 196612

commit v8 on v7

--- a/solution.py
+++ b/solution.py
@@ -57,6 +57,7 @@
             jax.ShapeDtypeStruct((80, 128), BF16),
             jax.ShapeDtypeStruct((80, 128), BF16),
         ),
+        compiler_params=pltpu.CompilerParams(vmem_limit_bytes=8 * 2**20),
     )(pre_act.reshape(128, SIZE_Z * C_HID), cot)
     before, after = from_both(high, low, GZ)
     return before, rows, after
@@ -68,6 +69,7 @@
         out_shape=jax.ShapeDtypeStruct((BLOCKS, 160, 256), BF16),
         out_specs=pl.BlockSpec(memory_space=pl.ANY),
         scratch_shapes=[pltpu.SemaphoreType.DMA((2, BLOCKS))],
+        compiler_params=pltpu.CompilerParams(vmem_limit_bytes=8 * 2**20),
     )(coarse.reshape(32, 256), skip_features.reshape(128, 256))
     return traded(parts, PLANE)
 
@@ -361,7 +363,9 @@
     deep = depth_rims(pre_act, cotangent)
     share_choice, cot_choice = row_choices()
     parts = pl.pallas_call(
-        parts_kernel, out_shape=jax.ShapeDtypeStruct((BLOCKS, 48, 128), BF16)
+        parts_kernel,
+        out_shape=jax.ShapeDtypeStruct((BLOCKS, 48, 128), BF16),
+        compiler_params=pltpu.CompilerParams(vmem_limit_bytes=8 * 2**20),
     )(*deep, share_choice, cot_choice)
     parts, inputs = lax.optimization_barrier((parts, inputs))
     data = traded(parts, PLANE)
@@ -369,6 +373,7 @@
     fine = pl.pallas_call(
         fine_kernel,
         out_shape=jax.ShapeDtypeStruct((2, 2048, 256), BF16),
+        compiler_params=pltpu.CompilerParams(vmem_limit_bytes=16 * 2**20),
         cost_estimate=pl.CostEstimate(
             flops=300_000_000, bytes_accessed=4_000_000, transcendentals=0
         ),
@@ -376,6 +381,7 @@
     field = pl.pallas_call(
         field_kernel,
         out_shape=jax.ShapeDtypeStruct((SIZE_X, SIZE_Y, 512), BF16),
+        compiler_params=pltpu.CompilerParams(vmem_limit_bytes=8 * 2**20),
         cost_estimate=pl.CostEstimate(
             flops=60_000_000, bytes_accessed=4_000_000, transcendentals=0
         ),
@@ -392,10 +398,11 @@
     )(data, fine, own_head_matrix(head), *chosen)
     near = jnp.sum(traded(share.reshape(4, 8, SHARE[1]), NEAR), axis=0)
     field, near = lax.optimization_barrier((field, near))
-    field = with_y_rims(with_x_rims(field))
+    field = with_x_rims(field)
     far = jnp.sum(spread(near.astype(BF16), FAR).astype(F32), axis=0)
     field, far = lax.optimization_barrier((field, far))
-    column = spread(far.astype(BF16), NEAR).reshape(SHARE)
+    field = with_y_rims(field)
+    column = spread(far, NEAR).reshape(SHARE)
     field, column = lax.optimization_barrier((field, column))
     body, head_grad = pl.pallas_call(
         unpack_kernel,
@@ -404,7 +411,7 @@
             jax.ShapeDtypeStruct((C_VEL, 27, C_HID), F32),
         ),
         compiler_params=pltpu.CompilerParams(vmem_limit_bytes=16 * 2**20),
-    )(spread(column, PLANE), head_channels())
+    )(spread(column.astype(BF16), PLANE), head_channels())
     skip_grad, coarse_grad = pl.pallas_call(
         input_kernel,
         out_shape=(

time: 120 us -> 124 us (1.033)
  waiting for transfers between devices: 18.2 us -> 30 us
  blocking collectives: 15.6 us -> 7.67 us
  Pallas kernels: 17.8 us -> 11.1 us
  starting transfers between devices: 59.1 us -> 62.6 us
  local copies, waits for them, and re-layouts: 6.8 us -> 10.2 us
    all_to_all x4 -> x5, waiting for transfers between devices: 13.1 us -> 28 us  [traded(): return lax.all_to_all(parts, axes, 0, 0)]
    all_to_all x2 -> x1, blocking collectives: 15.6 us -> 7.67 us  [traded(): return lax.all_to_all(parts, axes, 0, 0)]
    all_to_all x4 -> x5, starting transfers between devices: 35.5 us -> 39.4 us  [traded(): return lax.all_to_all(parts, axes, 0, 0)]
    unnamed x26 -> x30, local copies, waits for them, and re-layouts: 2.25 us -> 5.62 us
    pallas_call x1, Pallas kernels: 3.24 us -> 0.54 us  [per_device(): pl.pallas_call(fine_kernel, out_shape=jax.ShapeDtypeStruct((2, 2048, 256)...]
    ppermute x3, waiting for transfers between devices: 4.06 us -> 1.47 us  [from_both(): lax.ppermute(to_next, axis, up)]
    pallas_call x1, Pallas kernels: 1.78 us -> 0.22 us  [per_device(): pl.pallas_call(field_kernel, out_shape=jax.ShapeDtypeStruct((SIZE_X, SIZE...]
    pallas_call x1, Pallas kernels: 1.58 us -> 0.1 us  [depth_rims(): pl.pallas_call(turn_kernel, out_shape=(jax.ShapeDtypeStruct((272, 128), B...]
  transfers between devices with their start and end apart: 10 -> 11, of which waited for: 6 -> 8; matrix products, arithmetic and copies ran while one was open for 3% -> 3% of each run, Pallas kernels for 9% -> 4%
where the time goes in v8:
time: 124 us; the launch traced here: 123 us
  starting transfers between devices  62.6 us (50%)
  waiting for transfers between devices  30 us (24%)
  Pallas kernels  11.1 us (9%)
  local copies, waits for them, and re-layouts  10.2 us (8%)
  blocking collectives  7.67 us (6%)
    all_to_all x5, starting transfers between devices, traded(): return lax.all_to_all(parts, axes, 0, 0)  39.4 us
    all_to_all x5, waiting for transfers between devices, traded(): return lax.all_to_all(parts, axes, 0, 0)  28 us
    ppermute x3, starting transfers between devices, from_both(): lax.ppermute(to_previous, axis, down)  16.7 us
    all_to_all x1, blocking collectives, traded(): return lax.all_to_all(parts, axes, 0, 0)  7.67 us
    ppermute x3, starting transfers between devices, from_both(): lax.ppermute(to_next, axis, up)  6.51 us
    unnamed x30, local copies, waits for them, and re-layouts  5.62 us
    pallas_call x1, Pallas kernels, per_device(): pl.pallas_call(share_kernel, out_shape=jax.ShapeDtypeStruct(SHARE, F32),...  4.02 us
    pallas_call x1, Pallas kernels, per_device(): pl.pallas_call(input_kernel, out_shape=(jax.ShapeDtypeStruct((SIZE_X, SIZ...  2.56 us
  transfers between devices with their start and end apart: 11, of which 8 were waited for; matrix products, arithmetic and copies ran while one was open for 3% of the time, Pallas kernels for 4%

profile of v8, /device:TPU:1, one launch (start us, length us, event | category | flops | bytes accessed | tf_op | source)
XLA Modules:
  0.0 123.1 jit_solution(16727202335034808850)
XLA Ops:
  0.6 0.8 copy-done.5
  1.5 0.7 copy-done.8
  2.2 1.3 %shard_map.158 = bf16[16,160,256]{2,1,0:T(8,128)(2,1)} custom-call(bf16[32,256]{1,0:T(8,128)(2,1)S(1)} %bitcast.20, bf16[128,256]{1,0:T(8,128)(2,1)S(1)} %bitcast.18), custom_call_target="tpu_custom_call" | custom-call | tf_op jit(solution)/shard_map/pallas_call | solution.py:67
  3.5 0.0 copy-start.13
  3.5 0.0 copy-start.6
  3.5 0.0 copy-start.14
  3.5 0.0 copy-start.2
  3.6 0.0 copy-start.4
  3.6 10.5 %all-to-all-start = ((bf16[16,160,256]{2,1,0:T(8,128)(2,1)}), bf16[16,160,256]{2,1,0:T(8,128)(2,1)S(1)}, u32[]{:S(2)}, u32[]{:S(2)}) async-start(bf16[16,160,256]{2,1,0:T(8,128)(2,1)} %shard_map.158), calls=%async_computation | async-start | bytes 2621440 | tf_op jit(solution)/shard_map/all_to_all | solution.py:352
  14.1 0.1 reshape.51
  14.2 0.0 copy-done.6
  14.2 0.1 shard_map.156
  14.3 1.9 %collective-permute-start = (bf16[80,128]{1,0:T(8,128)(2,1)S(1)}, bf16[80,128]{1,0:T(8,128)(2,1)S(1)}, u32[]{:S(2)}, u32[]{:S(2)}) collective-permute-start(bf16[80,128]{1,0:T(8,128)(2,1)S(1)} %get-tuple-element.22), channel_id=1, source_target_pairs={{0,1},{1,2},{2,3},{3,4},{4,5},{5,6},{6,7},{7,8},{8,9},{9,10},{10,1... | collective-permute-start | bytes 61448 | tf_op jit(solution)/shard_map/ppermute | solution.py:47
  16.3 9.9 %collective-permute-start.1 = (bf16[80,128]{1,0:T(8,128)(2,1)S(1)}, bf16[80,128]{1,0:T(8,128)(2,1)S(1)}, u32[]{:S(2)}, u32[]{:S(2)}) collective-permute-start(bf16[80,128]{1,0:T(8,128)(2,1)S(1)} %get-tuple-element.24), channel_id=1, source_target_pairs={{1,0},{2,1},{3,2},{4,3},{5,4},{6,5},{7,6},{8,7},{9,8},{10,9},{11,1... | collective-permute-start | bytes 61448 | tf_op jit(solution)/shard_map/ppermute | solution.py:47
  26.2 0.0 copy-done.14
  26.3 0.3 collective-permute-done.before_ref
  26.6 0.5 collective-permute-done.1.after_ref
  27.1 0.0 copy-done.2
  27.1 0.9 shard_map.157
  28.0 5.3 %all-to-all-done.input_ref = bf16[16,160,256]{2,1,0:T(8,128)(2,1)S(1)} async-done(((bf16[16,160,256]{2,1,0:T(8,128)(2,1)}), bf16[16,160,256]{2,1,0:T(8,128)(2,1)S(1)}, u32[]{:S(2)}, u32[]{:S(2)}) %all-to-all-start) | async-done | bytes 1310752 | tf_op jit(solution)/shard_map/all_to_all | solution.py:352
  33.3 4.5 %all-to-all-start.1 = ((bf16[16,48,128]{2,1,0:T(8,128)(2,1)}), bf16[16,48,128]{2,1,0:T(8,128)(2,1)}, u32[]{:S(2)}, u32[]{:S(2)}) async-start(bf16[16,48,128]{2,1,0:T(8,128)(2,1)} %shard_map.157), calls=%async_computation.1 | async-start | bytes 393216 | tf_op jit(solution)/shard_map/all_to_all | solution.py:352
  37.8 0.1 fusion.5
  37.9 0.2 concatenate.12.head_ref
  38.2 0.4 copy.25
  38.6 0.1 reshape.57.head_ref
  38.8 0.0 copy-done
  38.8 0.2 shard_map.160
  39.0 0.0 copy-start.7
  39.0 0.7 copy-done.7
  39.8 0.5 shard_map.159.fine_ref
  40.3 4.4 %all-to-all-done.1.data_ref = bf16[16,48,128]{2,1,0:T(8,128)(2,1)} async-done(((bf16[16,48,128]{2,1,0:T(8,128)(2,1)}), bf16[16,48,128]{2,1,0:T(8,128)(2,1)}, u32[]{:S(2)}, u32[]{:S(2)}) %all-to-all-start.1) | async-done | bytes 196640 | tf_op jit(solution)/shard_map/all_to_all | solution.py:352
  44.7 0.9 copy-done.9
  45.7 0.9 copy-done.10
  46.6 0.7 copy-done.11
  47.3 4.0 %shard_map.161 = f32[32,768]{1,0:T(8,128)S(1)} custom-call(bf16[16,48,128]{2,1,0:T(8,128)(2,1)} %all-to-all-done.1.data_ref, bf16[2,2048,256]{2,1,0:T(8,128)(2,1)S(1)} %shard_map.159.fine_ref, bf16[24,216]{1,0:T(8,128)(2,1)S(1)} %reshape.57.head_ref, bf16[2,256,216]{2,1,0:T(8,128)(2,1)S(1)} %copy-done.9, bf16[216,512]{1,0:T(8,128)(2,1)S(1)} %copy-done.10, ...), custom_call_target="tpu_custom_call" | custom-call | flops 1500000000 | bytes 2000000 | tf_op jit(solution)/shard_map/pallas_call | solution.py:390
  51.3 7.7 %all_to_all.30 = f32[4,8,768]{2,1,0:T(8,128)S(1)} all-to-all(f32[4,8,768]{2,1,0:T(8,128)S(1)} %bitcast.17), channel_id=1, replica_groups=mesh['gx'=4,'gy'=4,'gzh'=2,'gzm'=8,'gzl'=2] {'gzh','gzl'}, dimensions={0} | all-to-all | bytes 196608 | tf_op jit(solution)/shard_map/all_to_all | solution.py:352
  59.0 0.6 broadcast_in_dim.8
  59.7 12.5 %all-to-all-start.3 = ((bf16[8,8,768]{2,1,0:T(8,128)(2,1)}), bf16[8,8,768]{2,1,0:T(8,128)(2,1)S(1)}, u32[]{:S(2)}, u32[]{:S(2)}) async-start(bf16[8,8,768]{2,1,0:T(8,128)(2,1)} %broadcast_in_dim.8), calls=%async_computation.3 | async-start | bytes 196608 | tf_op jit(solution)/shard_map/all_to_all | solution.py:352
  72.1 4.2 %collective-permute-start.3 = (bf16[2,16,512]{2,1,0:T(8,128)(2,1)S(1)}, bf16[2,16,512]{2,1,0:T(8,128)(2,1)S(1)}, u32[]{:S(2)}, u32[]{:S(2)}) collective-permute-start(bf16[2,16,512]{2,1,0:T(8,128)(2,1)S(1)} %get-tuple-element.43), channel_id=1, source_target_pairs={{128,0},{256,128},{384,256},{0,384},{129,1},{257,129},{385,257},{1... | collective-permute-start | bytes 98312 | tf_op jit(solution)/shard_map/ppermute | solution.py:47
  76.3 1.9 %collective-permute-start.2 = (bf16[2,16,512]{2,1,0:T(8,128)(2,1)S(1)}, bf16[2,16,512]{2,1,0:T(8,128)(2,1)S(1)}, u32[]{:S(2)}, u32[]{:S(2)}) collective-permute-start(bf16[2,16,512]{2,1,0:T(8,128)(2,1)S(1)} %get-tuple-element.42), channel_id=1, source_target_pairs={{0,128},{128,256},{256,384},{384,0},{1,129},{129,257},{257,385},{3... | collective-permute-start | bytes 98312 | tf_op jit(solution)/shard_map/ppermute | solution.py:47
  78.2 0.0 collective-permute-done.3
  78.3 1.2 collective-permute-done.2
  79.4 5.4 %all-to-all-done.3 = bf16[8,8,768]{2,1,0:T(8,128)(2,1)S(1)} async-done(((bf16[8,8,768]{2,1,0:T(8,128)(2,1)}), bf16[8,8,768]{2,1,0:T(8,128)(2,1)S(1)}, u32[]{:S(2)}, u32[]{:S(2)}) %all-to-all-start.3) | async-done | bytes 98336 | tf_op jit(solution)/shard_map/all_to_all | solution.py:352
  84.9 2.6 %collective-permute-start.5 = (bf16[12,2,512]{2,1,0:T(2,128)(2,1)S(1)}, bf16[12,2,512]{2,1,0:T(2,128)(2,1)S(1)}, u32[]{:S(2)}, u32[]{:S(2)}) collective-permute-start(bf16[12,2,512]{2,1,0:T(2,128)(2,1)S(1)} %get-tuple-element.41), channel_id=1, source_target_pairs={{32,0},{64,32},{96,64},{0,96},{33,1},{65,33},{97,65},{1,97},{34,2}... | collective-permute-start | bytes 73736 | tf_op jit(solution)/shard_map/ppermute | solution.py:47
  87.5 2.7 %collective-permute-start.4 = (bf16[12,2,512]{2,1,0:T(2,128)(2,1)S(1)}, bf16[12,2,512]{2,1,0:T(2,128)(2,1)S(1)}, u32[]{:S(2)}, u32[]{:S(2)}) collective-permute-start(bf16[12,2,512]{2,1,0:T(2,128)(2,1)S(1)} %get-tuple-element.40), channel_id=1, source_target_pairs={{0,32},{32,64},{64,96},{96,0},{1,33},{33,65},{65,97},{97,1},{2,34}... | collective-permute-start | bytes 73736 | tf_op jit(solution)/shard_map/ppermute | solution.py:47
  90.2 0.1 pad.45.clone
  90.3 0.6 broadcast_in_dim.10
  90.9 3.3 %all-to-all-start.4 = ((bf16[4,8,768]{2,1,0:T(8,128)(2,1)}), bf16[4,8,768]{2,1,0:T(8,128)(2,1)S(1)}, u32[]{:S(2)}, u32[]{:S(2)}) async-start(bf16[4,8,768]{2,1,0:T(8,128)(2,1)} %broadcast_in_dim.10), calls=%async_computation.4 | async-start | bytes 98304 | tf_op jit(solution)/shard_map/all_to_all | solution.py:352
  94.2 0.0 collective-permute-done.5
  94.2 0.0 collective-permute-done.4
  94.2 0.2 maximum_maximum_fusion.field_ref
  94.4 0.0 copy-start.12
  94.4 4.9 %all-to-all-done.4 = bf16[4,8,768]{2,1,0:T(8,128)(2,1)S(1)} async-done(((bf16[4,8,768]{2,1,0:T(8,128)(2,1)}), bf16[4,8,768]{2,1,0:T(8,128)(2,1)S(1)}, u32[]{:S(2)}, u32[]{:S(2)}) %all-to-all-start.4) | async-done | bytes 49184 | tf_op jit(solution)/shard_map/all_to_all | solution.py:352
  99.3 1.0 broadcast_in_dim.11
  100.3 8.6 %all-to-all-start.5 = ((bf16[16,32,768]{2,1,0:T(8,128)(2,1)}), bf16[16,32,768]{2,1,0:T(8,128)(2,1)S(1)}, u32[]{:S(2)}, u32[]{:S(2)}) async-start(bf16[16,32,768]{2,1,0:T(8,128)(2,1)} %broadcast_in_dim.11), calls=%async_computation.5 | async-start | bytes 1572864 | tf_op jit(solution)/shard_map/all_to_all | solution.py:352
  108.8 0.0 copy-done.12
  108.9 1.0 reshape.60
  109.9 0.1 rev.7
  110.0 0.1 slice.25
  110.1 0.3 fusion.2.weight_ref
  110.4 0.6 copy-done.1
  111.0 2.6 %shard_map.162 = (bf16[8,16,256]{2,1,0:T(8,128)(2,1)}, bf16[32,256]{1,0:T(8,128)(2,1)}) custom-call(bf16[12,32,512]{2,1,0:T(8,128)(2,1)S(1)} %maximum_maximum_fusion.field_ref, bf16[9,32,384]{2,1,0:T(8,128)(2,1)S(1)} %copy-done.1, bf16[9,256,256]{2,1,0:T(8,128)(2,1)S(1)} %fusion.2.weight_ref), custom_call_target="tpu_custom_call" | custom-call | flops 700000000 | bytes 3000000 | tf_op jit(solution)/shard_map/pallas_call | solution.py:415
  113.6 8.1 %all-to-all-done.5.share_ref = bf16[16,32,768]{2,1,0:T(8,128)(2,1)S(1)} async-done(((bf16[16,32,768]{2,1,0:T(8,128)(2,1)}), bf16[16,32,768]{2,1,0:T(8,128)(2,1)S(1)}, u32[]{:S(2)}, u32[]{:S(2)}) %all-to-all-start.5) | async-done | bytes 786464 | tf_op jit(solution)/shard_map/all_to_all | solution.py:352
  121.7 1.4 %shard_map.163 = (f32[27,12288]{1,0:T(8,128)}, f32[3,27,64]{2,1,0:T(8,128)}) custom-call(bf16[16,32,768]{2,1,0:T(8,128)(2,1)S(1)} %all-to-all-done.5.share_ref, bf16[512,64]{1,0:T(8,128)(2,1)S(1)} %copy-done.3), custom_call_target="tpu_custom_call" | custom-call | tf_op jit(solution)/shard_map/pallas_call | solution.py:407
  (25 shorter events, 0.3 us)
Async XLA Ops:
  0.6 0.8 copy-start.5
  1.5 0.7 copy-start.8
  3.5 10.6 %copy-start.13 = (bf16[3,8,16,4]{2,3,1,0:T(4,128)(2,1)S(1)}, bf16[3,8,16,4]{2,3,1,0:T(4,128)(2,1)}, u32[]{:S(2)}) copy-start(bf16[3,8,16,4]{2,3,1,0:T(4,128)(2,1)} %param.16) | copy-start | bytes 9220
  3.5 10.7 %copy-start.6 = (bf16[8,16,256]{2,1,0:T(8,128)(2,1)S(1)}, bf16[8,16,256]{2,1,0:T(8,128)(2,1)}, u32[]{:S(2)}) copy-start(bf16[8,16,256]{2,1,0:T(8,128)(2,1)} %param.15) | copy-start | bytes 196612
  3.5 22.7 %copy-start.14 = (bf16[27,3,64]{2,0,1:T(8,128)(2,1)S(1)}, bf16[27,3,64]{2,0,1:T(8,128)(2,1)}, u32[]{:S(2)}) copy-start(bf16[27,3,64]{2,0,1:T(8,128)(2,1)} %param.18) | copy-start | bytes 31108
  3.5 23.5 %copy-start.2 = (bf16[384,384]{1,0:T(8,128)(2,1)S(1)}, bf16[384,384]{1,0:T(8,128)(2,1)}, u32[]{:S(2)}) copy-start(bf16[384,384]{1,0:T(8,128)(2,1)} %constant.38.clone.choice_ref) | copy-start | bytes 884740
  3.6 23.5 %copy-start.4 = (bf16[128,48]{1,0:T(8,128)(2,1)S(1)}, bf16[128,48]{1,0:T(8,128)(2,1)}, u32[]{:S(2)}) copy-start(bf16[128,48]{1,0:T(8,128)(2,1)} %constant.39.clone.cot_choice_ref) | copy-start | bytes 36868
  3.6 29.7 %all-to-all-start = ((bf16[16,160,256]{2,1,0:T(8,128)(2,1)}), bf16[16,160,256]{2,1,0:T(8,128)(2,1)S(1)}, u32[]{:S(2)}, u32[]{:S(2)}) async-start(bf16[16,160,256]{2,1,0:T(8,128)(2,1)} %shard_map.158), calls=%async_computation | async-start | bytes 2621440 | tf_op jit(solution)/shard_map/all_to_all | solution.py:352
  14.3 12.2 %collective-permute-start = (bf16[80,128]{1,0:T(8,128)(2,1)S(1)}, bf16[80,128]{1,0:T(8,128)(2,1)S(1)}, u32[]{:S(2)}, u32[]{:S(2)}) collective-permute-start(bf16[80,128]{1,0:T(8,128)(2,1)S(1)} %get-tuple-element.22), channel_id=1, source_target_pairs={{0,1},{1,2},{2,3},{3,4},{4,5},{5,6},{6,7},{7,8},{8,9},{9,10},{10,1... | collective-permute-start | bytes 61448 | tf_op jit(solution)/shard_map/ppermute | solution.py:47
  16.3 10.8 %collective-permute-start.1 = (bf16[80,128]{1,0:T(8,128)(2,1)S(1)}, bf16[80,128]{1,0:T(8,128)(2,1)S(1)}, u32[]{:S(2)}, u32[]{:S(2)}) collective-permute-start(bf16[80,128]{1,0:T(8,128)(2,1)S(1)} %get-tuple-element.24), channel_id=1, source_target_pairs={{1,0},{2,1},{3,2},{4,3},{5,4},{6,5},{7,6},{8,7},{9,8},{10,9},{11,1... | collective-permute-start | bytes 61448 | tf_op jit(solution)/shard_map/ppermute | solution.py:47
  33.3 11.4 %all-to-all-start.1 = ((bf16[16,48,128]{2,1,0:T(8,128)(2,1)}), bf16[16,48,128]{2,1,0:T(8,128)(2,1)}, u32[]{:S(2)}, u32[]{:S(2)}) async-start(bf16[16,48,128]{2,1,0:T(8,128)(2,1)} %shard_map.157), calls=%async_computation.1 | async-start | bytes 393216 | tf_op jit(solution)/shard_map/all_to_all | solution.py:352
  38.1 0.7 copy-start
  39.0 0.8 copy-start.7
  44.7 1.0 copy-start.9
  45.7 0.9 copy-start.10
  46.6 0.7 copy-start.11
  59.7 25.2 %all-to-all-start.3 = ((bf16[8,8,768]{2,1,0:T(8,128)(2,1)}), bf16[8,8,768]{2,1,0:T(8,128)(2,1)S(1)}, u32[]{:S(2)}, u32[]{:S(2)}) async-start(bf16[8,8,768]{2,1,0:T(8,128)(2,1)} %broadcast_in_dim.8), calls=%async_computation.3 | async-start | bytes 196608 | tf_op jit(solution)/shard_map/all_to_all | solution.py:352
  72.1 6.1 %collective-permute-start.3 = (bf16[2,16,512]{2,1,0:T(8,128)(2,1)S(1)}, bf16[2,16,512]{2,1,0:T(8,128)(2,1)S(1)}, u32[]{:S(2)}, u32[]{:S(2)}) collective-permute-start(bf16[2,16,512]{2,1,0:T(8,128)(2,1)S(1)} %get-tuple-element.43), channel_id=1, source_target_pairs={{128,0},{256,128},{384,256},{0,384},{129,1},{257,129},{385,257},{1... | collective-permute-start | bytes 98312 | tf_op jit(solution)/shard_map/ppermute | solution.py:47
  76.3 3.1 %collective-permute-start.2 = (bf16[2,16,512]{2,1,0:T(8,128)(2,1)S(1)}, bf16[2,16,512]{2,1,0:T(8,128)(2,1)S(1)}, u32[]{:S(2)}, u32[]{:S(2)}) collective-permute-start(bf16[2,16,512]{2,1,0:T(8,128)(2,1)S(1)} %get-tuple-element.42), channel_id=1, source_target_pairs={{0,128},{128,256},{256,384},{384,0},{1,129},{129,257},{257,385},{3... | collective-permute-start | bytes 98312 | tf_op jit(solution)/shard_map/ppermute | solution.py:47
  84.9 9.3 %collective-permute-start.5 = (bf16[12,2,512]{2,1,0:T(2,128)(2,1)S(1)}, bf16[12,2,512]{2,1,0:T(2,128)(2,1)S(1)}, u32[]{:S(2)}, u32[]{:S(2)}) collective-permute-start(bf16[12,2,512]{2,1,0:T(2,128)(2,1)S(1)} %get-tuple-element.41), channel_id=1, source_target_pairs={{32,0},{64,32},{96,64},{0,96},{33,1},{65,33},{97,65},{1,97},{34,2}... | collective-permute-start | bytes 73736 | tf_op jit(solution)/shard_map/ppermute | solution.py:47
  87.5 6.7 %collective-permute-start.4 = (bf16[12,2,512]{2,1,0:T(2,128)(2,1)S(1)}, bf16[12,2,512]{2,1,0:T(2,128)(2,1)S(1)}, u32[]{:S(2)}, u32[]{:S(2)}) collective-permute-start(bf16[12,2,512]{2,1,0:T(2,128)(2,1)S(1)} %get-tuple-element.40), channel_id=1, source_target_pairs={{0,32},{32,64},{64,96},{96,0},{1,33},{33,65},{65,97},{97,1},{2,34}... | collective-permute-start | bytes 73736 | tf_op jit(solution)/shard_map/ppermute | solution.py:47
  90.9 8.4 %all-to-all-start.4 = ((bf16[4,8,768]{2,1,0:T(8,128)(2,1)}), bf16[4,8,768]{2,1,0:T(8,128)(2,1)S(1)}, u32[]{:S(2)}, u32[]{:S(2)}) async-start(bf16[4,8,768]{2,1,0:T(8,128)(2,1)} %broadcast_in_dim.10), calls=%async_computation.4 | async-start | bytes 98304 | tf_op jit(solution)/shard_map/all_to_all | solution.py:352
  94.4 14.4 %copy-start.12 = (bf16[27,12288]{1,0:T(8,128)(2,1)S(1)}, bf16[27,12288]{1,0:T(8,128)(2,1)}, u32[]{:S(2)}) copy-start(bf16[27,12288]{1,0:T(8,128)(2,1)} %param.17) | copy-start | bytes 1990660
  100.3 21.4 %all-to-all-start.5 = ((bf16[16,32,768]{2,1,0:T(8,128)(2,1)}), bf16[16,32,768]{2,1,0:T(8,128)(2,1)S(1)}, u32[]{:S(2)}, u32[]{:S(2)}) async-start(bf16[16,32,768]{2,1,0:T(8,128)(2,1)} %broadcast_in_dim.11), calls=%async_computation.5 | async-start | bytes 1572864 | tf_op jit(solution)/shard_map/all_to_all | solution.py:352
  110.1 0.9 copy-start.1
  111.0 10.7 %copy-start.3 = (bf16[512,64]{1,0:T(8,128)(2,1)S(1)}, bf16[512,64]{1,0:T(8,128)(2,1)}, u32[]{:S(2)}) copy-start(bf16[512,64]{1,0:T(8,128)(2,1)} %constant.44.clone.choice_ref) | copy-start | bytes 196612

commit v9 on v8

--- a/solution.py
+++ b/solution.py
@@ -67,7 +67,8 @@
     parts = pl.pallas_call(
         message_kernel,
         out_shape=jax.ShapeDtypeStruct((BLOCKS, 160, 256), BF16),
-        out_specs=pl.BlockSpec(memory_space=pl.ANY),
+        in_specs=[pl.BlockSpec(memory_space=pltpu.HBM)] * 2,
+        out_specs=pl.BlockSpec(memory_space=pltpu.HBM),
         scratch_shapes=[pltpu.SemaphoreType.DMA((2, BLOCKS))],
         compiler_params=pltpu.CompilerParams(vmem_limit_bytes=8 * 2**20),
     )(coarse.reshape(32, 256), skip_features.reshape(128, 256))
@@ -122,9 +123,6 @@
                 tap_rows[z // 2, z % 2, own, tap, row] = 1.0
             for o in range(C_VEL):
                 head_columns[pair, z + 2 - c, o, z, 32 * o + tap] = 1.0
-    head_rows = np.zeros((32, 6, OWN), np.float32)
-    for own in range(OWN):
-        head_rows[27 + own, 1:5, own] = 1.0
     double = np.zeros((SIZE_X, SIZE_Y, SIZE_X // 2, SIZE_Y // 2), np.float32)
     for x in range(SIZE_X):
         for y in range(SIZE_Y):
@@ -132,7 +130,6 @@
     return (
         jnp.asarray(tap_rows.reshape(2, 256, 216), BF16),
         jnp.asarray(head_columns.reshape(216, 512), BF16),
-        jnp.asarray(head_rows.reshape(32, ROWS)),
     ), jnp.asarray(double.reshape(128, 32), BF16)
 
 
@@ -263,7 +260,15 @@
             fine_ref[pair, rows, 128:256] = input_ref[at, 32:160, lanes]
 
 
-def share_kernel(data_ref, fine_ref, head_ref, tap_ref, column_ref, row_ref, share_ref, stack_s):
+def share_kernel(
+    data_ref, fine_hbm, head_ref, tap_hbm, column_hbm, share_ref, stack_s, fine_ref, tap_ref, column_ref, sems
+):
+    column_copy = pltpu.make_async_copy(column_hbm, column_ref, sems.at[0])
+    tap_copy = pltpu.make_async_copy(tap_hbm, tap_ref, sems.at[1])
+    fine_copy = pltpu.make_async_copy(fine_hbm, fine_ref, sems.at[2])
+    column_copy.start()
+    fine_copy.start()
+    tap_copy.start()
     blocks = [data_ref[at].astype(F32) for at in range(BLOCKS)]
     stack_moved([block[ROWS:48] for block in blocks], stack_s)
     cot = stack_s[...].astype(BF16)
@@ -272,6 +277,7 @@
     d_pre = (d_hidden * gelu_slope(pre)).astype(BF16).astype(F32)
     hidden = gelu_value(pre).astype(BF16)
     pairs = lax.dot_general(hidden, cot, (((1,), (1,)), ((), ())), preferred_element_type=F32)
+    column_copy.wait()
     spans = jnp.dot(
         pairs, column_ref[...].astype(F32), precision=HIGHEST, preferred_element_type=F32
     )
@@ -279,10 +285,15 @@
     kept = jnp.zeros((ROWS, 128), F32)
     for z in range(SIZE_Z):
         kept = jnp.where(depth == z + 1, spans[:, 128 * z : 128 * z + 128], kept)
-    head = jnp.dot(row_ref[...], kept, precision=HIGHEST, preferred_element_type=F32)
+    row = lax.broadcasted_iota(jnp.int32, (32, ROWS), 0) - 27
+    source = lax.broadcasted_iota(jnp.int32, (32, ROWS), 1)
+    place = jnp.where(source % OWN == row, 1.0, 0.0).astype(F32)
+    head = jnp.dot(place, kept, precision=HIGHEST, preferred_element_type=F32)
 
     stack_moved([d_pre[:, 128 * at : 128 * at + 128] for at in range(BLOCKS)], stack_s)
     back = stack_s[...].astype(BF16)
+    fine_copy.wait()
+    tap_copy.wait()
     up = jnp.zeros((128, 128), F32)
     skip = jnp.zeros((128, 128), F32)
     for pair in range(2):
@@ -390,7 +401,20 @@
     share = pl.pallas_call(
         share_kernel,
         out_shape=jax.ShapeDtypeStruct(SHARE, F32),
-        scratch_shapes=[pltpu.VMEM((216, 2048), F32)],
+        in_specs=[
+            pl.BlockSpec(memory_space=pltpu.VMEM),
+            pl.BlockSpec(memory_space=pltpu.HBM),
+            pl.BlockSpec(memory_space=pltpu.VMEM),
+            pl.BlockSpec(memory_space=pltpu.HBM),
+            pl.BlockSpec(memory_space=pltpu.HBM),
+        ],
+        scratch_shapes=[
+            pltpu.VMEM((216, 2048), F32),
+            pltpu.VMEM((2, 2048, 256), BF16),
+            pltpu.VMEM((2, 256, 216), BF16),
+            pltpu.VMEM((216, 512), BF16),
+            pltpu.SemaphoreType.DMA((3,)),
+        ],
         compiler_params=pltpu.CompilerParams(vmem_limit_bytes=32 * 2**20),
         cost_estimate=pl.CostEstimate(
             flops=1_500_000_000, bytes_accessed=2_000_000, transcendentals=200_000
@@ -400,10 +424,10 @@
     field, near = lax.optimization_barrier((field, near))
     field = with_x_rims(field)
     far = jnp.sum(spread(near.astype(BF16), FAR).astype(F32), axis=0)
-    field, far = lax.optimization_barrier((field, far))
+    column = spread(far.astype(BF16), NEAR).reshape(SHARE)
+    weights = input_matrix(weight_one)
+    field, column, weights = lax.optimization_barrier((field, column, weights))
     field = with_y_rims(field)
-    column = spread(far, NEAR).reshape(SHARE)
-    field, column = lax.optimization_barrier((field, column))
     body, head_grad = pl.pallas_call(
         unpack_kernel,
         out_shape=(
@@ -411,7 +435,7 @@
             jax.ShapeDtypeStruct((C_VEL, 27, C_HID), F32),
         ),
         compiler_params=pltpu.CompilerParams(vmem_limit_bytes=16 * 2**20),
-    )(spread(column.astype(BF16), PLANE), head_channels())
+    )(spread(column, PLANE), head_channels())
     skip_grad, coarse_grad = pl.pallas_call(
         input_kernel,
         out_shape=(
@@ -428,7 +452,7 @@
         cost_estimate=pl.CostEstimate(
             flops=700_000_000, bytes_accessed=3_000_000, transcendentals=100_000
         ),
-    )(field, head, input_matrix(weight_one))
+    )(field, head, weights)
     return coarse_grad.reshape(4, 8, 256), skip_grad, body, jnp.transpose(head_grad, (1, 0, 2))
 
 

time: 124 us -> 120 us (0.968)
  waiting for transfers between devices: 30 us -> 24.9 us
    all_to_all x5, waiting for transfers between devices: 28 us -> 18.7 us  [traded(): return lax.all_to_all(parts, axes, 0, 0)]
    ppermute x3, waiting for transfers between devices: 0.51 us -> 5.27 us  [from_both(): lax.ppermute(to_previous, axis, down)]
    ppermute x3, starting transfers between devices: 16.7 us -> 18.6 us  [from_both(): lax.ppermute(to_previous, axis, down)]
    unnamed x30 -> x26, local copies, waits for them, and re-layouts: 5.62 us -> 4.28 us
  transfers between devices with their start and end apart: 11 -> 11, of which waited for: 8 -> 8; matrix products, arithmetic and copies ran while one was open for 3% -> 4% of each run, Pallas kernels for 4% -> 4%
where the time goes in v9:
time: 120 us; the launch traced here: 119 us
  starting transfers between devices  63.1 us (53%)
  waiting for transfers between devices  24.9 us (21%)
  Pallas kernels  11.7 us (10%)
  local copies, waits for them, and re-layouts  9.94 us (8%)
  blocking collectives  7.68 us (6%)
    all_to_all x5, starting transfers between devices, traded(): return lax.all_to_all(parts, axes, 0, 0)  38.8 us
    all_to_all x5, waiting for transfers between devices, traded(): return lax.all_to_all(parts, axes, 0, 0)  18.7 us
    ppermute x3, starting transfers between devices, from_both(): lax.ppermute(to_previous, axis, down)  18.6 us
    all_to_all x1, blocking collectives, traded(): return lax.all_to_all(parts, axes, 0, 0)  7.68 us
    ppermute x3, starting transfers between devices, from_both(): lax.ppermute(to_next, axis, up)  5.76 us
    ppermute x3, waiting for transfers between devices, from_both(): lax.ppermute(to_previous, axis, down)  5.27 us
    pallas_call x1, Pallas kernels, per_device(): pl.pallas_call(share_kernel, out_shape=jax.ShapeDtypeStruct(SHARE, F32),...  4.65 us
    unnamed x26, local copies, waits for them, and re-layouts  4.28 us
  transfers between devices with their start and end apart: 11, of which 8 were waited for; matrix products, arithmetic and copies ran while one was open for 4% of the time, Pallas kernels for 4%

profile of v9, /device:TPU:1, one launch (start us, length us, event | category | flops | bytes accessed | tf_op | source)
XLA Modules:
  0.0 118.9 jit_solution(11965899581693593607)
XLA Ops:
  0.6 0.0 copy-start.5
  0.6 0.8 copy-done.5
  1.5 0.7 copy-done.8
  2.2 1.3 %shard_map.149 = bf16[16,160,256]{2,1,0:T(8,128)(2,1)} custom-call(bf16[32,256]{1,0:T(8,128)(2,1)S(1)} %bitcast.20, bf16[128,256]{1,0:T(8,128)(2,1)S(1)} %bitcast.18), custom_call_target="tpu_custom_call" | custom-call | tf_op jit(solution)/shard_map/pallas_call | solution.py:67
  3.5 0.0 copy-start.11
  3.5 0.0 copy-start.6
  3.5 0.0 copy-start.12
  3.5 0.0 copy-start.2
  3.6 0.0 copy-start.4
  3.6 10.5 %all-to-all-start = ((bf16[16,160,256]{2,1,0:T(8,128)(2,1)}), bf16[16,160,256]{2,1,0:T(8,128)(2,1)S(1)}, u32[]{:S(2)}, u32[]{:S(2)}) async-start(bf16[16,160,256]{2,1,0:T(8,128)(2,1)} %shard_map.149), calls=%async_computation | async-start | bytes 2621440 | tf_op jit(solution)/shard_map/all_to_all | solution.py:363
  14.1 0.0 copy-done.11
  14.1 0.1 reshape.51
  14.2 0.0 copy-done.6
  14.2 0.1 shard_map.147
  14.3 1.9 %collective-permute-start = (bf16[80,128]{1,0:T(8,128)(2,1)S(1)}, bf16[80,128]{1,0:T(8,128)(2,1)S(1)}, u32[]{:S(2)}, u32[]{:S(2)}) collective-permute-start(bf16[80,128]{1,0:T(8,128)(2,1)S(1)} %get-tuple-element.21), channel_id=1, source_target_pairs={{0,1},{1,2},{2,3},{3,4},{4,5},{5,6},{6,7},{7,8},{8,9},{9,10},{10,1... | collective-permute-start | bytes 61448 | tf_op jit(solution)/shard_map/ppermute | solution.py:47
  16.3 9.9 %collective-permute-start.1 = (bf16[80,128]{1,0:T(8,128)(2,1)S(1)}, bf16[80,128]{1,0:T(8,128)(2,1)S(1)}, u32[]{:S(2)}, u32[]{:S(2)}) collective-permute-start(bf16[80,128]{1,0:T(8,128)(2,1)S(1)} %get-tuple-element.23), channel_id=1, source_target_pairs={{1,0},{2,1},{3,2},{4,3},{5,4},{6,5},{7,6},{8,7},{9,8},{10,9},{11,1... | collective-permute-start | bytes 61448 | tf_op jit(solution)/shard_map/ppermute | solution.py:47
  26.2 0.0 copy-done.12
  26.3 0.3 collective-permute-done.before_ref
  26.6 0.5 collective-permute-done.1.after_ref
  27.1 0.0 copy-done.2
  27.1 0.0 copy-done.4
  27.1 0.9 shard_map.148
  28.0 5.3 %all-to-all-done.input_ref = bf16[16,160,256]{2,1,0:T(8,128)(2,1)S(1)} async-done(((bf16[16,160,256]{2,1,0:T(8,128)(2,1)}), bf16[16,160,256]{2,1,0:T(8,128)(2,1)S(1)}, u32[]{:S(2)}, u32[]{:S(2)}) %all-to-all-start) | async-done | bytes 1310752 | tf_op jit(solution)/shard_map/all_to_all | solution.py:363
  33.3 4.5 %all-to-all-start.1 = ((bf16[16,48,128]{2,1,0:T(8,128)(2,1)}), bf16[16,48,128]{2,1,0:T(8,128)(2,1)}, u32[]{:S(2)}, u32[]{:S(2)}) async-start(bf16[16,48,128]{2,1,0:T(8,128)(2,1)} %shard_map.148), calls=%async_computation.1 | async-start | bytes 393216 | tf_op jit(solution)/shard_map/all_to_all | solution.py:363
  37.8 0.1 fusion.5
  37.9 0.2 concatenate.12.head_ref
  38.2 0.4 copy.24
  38.6 0.1 reshape.57.head_ref
  38.8 0.0 copy-done
  38.8 0.2 shard_map.151
  39.0 0.0 copy-start.7
  39.0 0.7 copy-done.7
  39.8 0.5 shard_map.150.fine_hbm
  40.3 4.4 %all-to-all-done.1.data_ref = bf16[16,48,128]{2,1,0:T(8,128)(2,1)} async-done(((bf16[16,48,128]{2,1,0:T(8,128)(2,1)}), bf16[16,48,128]{2,1,0:T(8,128)(2,1)}, u32[]{:S(2)}, u32[]{:S(2)}) %all-to-all-start.1) | async-done | bytes 196640 | tf_op jit(solution)/shard_map/all_to_all | solution.py:363
  44.7 0.9 copy-done.9
  45.7 0.9 copy-done.10
  46.6 4.6 %shard_map.152 = f32[32,768]{1,0:T(8,128)S(1)} custom-call(bf16[16,48,128]{2,1,0:T(8,128)(2,1)} %all-to-all-done.1.data_ref, bf16[2,2048,256]{2,1,0:T(8,128)(2,1)S(1)} %shard_map.150.fine_hbm, bf16[24,216]{1,0:T(8,128)(2,1)S(1)} %reshape.57.head_ref, bf16[2,256,216]{2,1,0:T(8,128)(2,1)S(1)} %copy-done.9, bf16[216,512]{1,0:T(8,128)(2,1)S(1)} %copy-done.10), custom_call_target="tpu_custom_call" | custom-call | flops 1500000000 | bytes 2000000 | tf_op jit(solution)/shard_map/pallas_call | solution.py:401
  51.2 7.7 %all_to_all.30 = f32[4,8,768]{2,1,0:T(8,128)S(1)} all-to-all(f32[4,8,768]{2,1,0:T(8,128)S(1)} %bitcast.17), channel_id=1, replica_groups=mesh['gx'=4,'gy'=4,'gzh'=2,'gzm'=8,'gzl'=2] {'gzh','gzl'}, dimensions={0} | all-to-all | bytes 196608 | tf_op jit(solution)/shard_map/all_to_all | solution.py:363
  58.9 0.6 broadcast_in_dim.8
  59.6 12.5 %all-to-all-start.3 = ((bf16[8,8,768]{2,1,0:T(8,128)(2,1)}), bf16[8,8,768]{2,1,0:T(8,128)(2,1)S(1)}, u32[]{:S(2)}, u32[]{:S(2)}) async-start(bf16[8,8,768]{2,1,0:T(8,128)(2,1)} %broadcast_in_dim.8), calls=%async_computation.3 | async-start | bytes 196608 | tf_op jit(solution)/shard_map/all_to_all | solution.py:363
  72.1 2.1 %reshape.60 = bf16[9,3,64,192]{3,2,1,0:T(8,128)(2,1)S(1)} reshape(bf16[27,12288]{1,0:T(8,128)(2,1)} %param.16) | data formatting | bytes 1327104 | tf_op jit(solution)/shard_map/reshape | solution.py:189
  74.2 0.1 rev.7
  74.3 0.1 slice.25
  74.4 4.2 %collective-permute-start.3 = (bf16[2,16,512]{2,1,0:T(8,128)(2,1)S(1)}, bf16[2,16,512]{2,1,0:T(8,128)(2,1)S(1)}, u32[]{:S(2)}, u32[]{:S(2)}) collective-permute-start(bf16[2,16,512]{2,1,0:T(8,128)(2,1)S(1)} %get-tuple-element.41), channel_id=1, source_target_pairs={{128,0},{256,128},{384,256},{0,384},{129,1},{257,129},{385,257},{1... | collective-permute-start | bytes 98312 | tf_op jit(solution)/shard_map/ppermute | solution.py:47
  78.5 1.9 %collective-permute-start.2 = (bf16[2,16,512]{2,1,0:T(8,128)(2,1)S(1)}, bf16[2,16,512]{2,1,0:T(8,128)(2,1)S(1)}, u32[]{:S(2)}, u32[]{:S(2)}) collective-permute-start(bf16[2,16,512]{2,1,0:T(8,128)(2,1)S(1)} %get-tuple-element.40), channel_id=1, source_target_pairs={{0,128},{128,256},{256,384},{384,0},{1,129},{129,257},{257,385},{3... | collective-permute-start | bytes 98312 | tf_op jit(solution)/shard_map/ppermute | solution.py:47
  80.5 4.3 %all-to-all-done.3 = bf16[8,8,768]{2,1,0:T(8,128)(2,1)S(1)} async-done(((bf16[8,8,768]{2,1,0:T(8,128)(2,1)}), bf16[8,8,768]{2,1,0:T(8,128)(2,1)S(1)}, u32[]{:S(2)}, u32[]{:S(2)}) %all-to-all-start.3) | async-done | bytes 98336 | tf_op jit(solution)/shard_map/all_to_all | solution.py:363
  84.8 0.6 broadcast_in_dim.9
  85.4 3.3 %all-to-all-start.4 = ((bf16[4,8,768]{2,1,0:T(8,128)(2,1)}), bf16[4,8,768]{2,1,0:T(8,128)(2,1)S(1)}, u32[]{:S(2)}, u32[]{:S(2)}) async-start(bf16[4,8,768]{2,1,0:T(8,128)(2,1)} %broadcast_in_dim.9), calls=%async_computation.4 | async-start | bytes 98304 | tf_op jit(solution)/shard_map/all_to_all | solution.py:363
  88.7 0.3 fusion.2.weight_ref
  89.0 0.0 collective-permute-done.3
  89.0 0.0 collective-permute-done.2
  89.1 4.8 %all-to-all-done.4 = bf16[4,8,768]{2,1,0:T(8,128)(2,1)S(1)} async-done(((bf16[4,8,768]{2,1,0:T(8,128)(2,1)}), bf16[4,8,768]{2,1,0:T(8,128)(2,1)S(1)}, u32[]{:S(2)}, u32[]{:S(2)}) %all-to-all-start.4) | async-done | bytes 49184 | tf_op jit(solution)/shard_map/all_to_all | solution.py:363
  93.8 1.0 broadcast_in_dim.11
  94.8 7.9 %all-to-all-start.5 = ((bf16[16,32,768]{2,1,0:T(8,128)(2,1)}), bf16[16,32,768]{2,1,0:T(8,128)(2,1)S(1)}, u32[]{:S(2)}, u32[]{:S(2)}) async-start(bf16[16,32,768]{2,1,0:T(8,128)(2,1)} %broadcast_in_dim.11), calls=%async_computation.5 | async-start | bytes 1572864 | tf_op jit(solution)/shard_map/all_to_all | solution.py:363
  102.8 4.5 %collective-permute-start.5 = (bf16[12,2,512]{2,1,0:T(2,128)(2,1)S(1)}, bf16[12,2,512]{2,1,0:T(2,128)(2,1)S(1)}, u32[]{:S(2)}, u32[]{:S(2)}) collective-permute-start(bf16[12,2,512]{2,1,0:T(2,128)(2,1)S(1)} %get-tuple-element.39), channel_id=1, source_target_pairs={{32,0},{64,32},{96,64},{0,96},{33,1},{65,33},{97,65},{1,97},{34,2}... | collective-permute-start | bytes 73736 | tf_op jit(solution)/shard_map/ppermute | solution.py:47
  107.3 1.9 %collective-permute-start.4 = (bf16[12,2,512]{2,1,0:T(2,128)(2,1)S(1)}, bf16[12,2,512]{2,1,0:T(2,128)(2,1)S(1)}, u32[]{:S(2)}, u32[]{:S(2)}) collective-permute-start(bf16[12,2,512]{2,1,0:T(2,128)(2,1)S(1)} %get-tuple-element.38), channel_id=1, source_target_pairs={{0,32},{32,64},{64,96},{96,0},{1,33},{33,65},{65,97},{97,1},{2,34}... | collective-permute-start | bytes 73736 | tf_op jit(solution)/shard_map/ppermute | solution.py:47
  109.2 0.1 pad.43.clone
  109.3 4.8 %collective-permute-done.5 = bf16[12,2,512]{2,1,0:T(2,128)(2,1)S(1)} collective-permute-done((bf16[12,2,512]{2,1,0:T(2,128)(2,1)S(1)}, bf16[12,2,512]{2,1,0:T(2,128)(2,1)S(1)}, u32[]{:S(2)}, u32[]{:S(2)}) %collective-permute-start.5) | collective-permute-done | bytes 24608 | tf_op jit(solution)/shard_map/ppermute | solution.py:47
  114.1 0.6 collective-permute-done.4
  114.7 0.2 maximum_maximum_fusion.field_ref
  114.9 0.0 copy-start.3
  114.9 2.5 %shard_map.153 = (bf16[8,16,256]{2,1,0:T(8,128)(2,1)}, bf16[32,256]{1,0:T(8,128)(2,1)}) custom-call(bf16[12,32,512]{2,1,0:T(8,128)(2,1)S(1)} %maximum_maximum_fusion.field_ref, bf16[9,32,384]{2,1,0:T(8,128)(2,1)S(1)} %copy-done.1, bf16[9,256,256]{2,1,0:T(8,128)(2,1)S(1)} %fusion.2.weight_ref), custom_call_target="tpu_custom_call" | custom-call | flops 700000000 | bytes 3000000 | tf_op jit(solution)/shard_map/pallas_call | solution.py:439
  117.5 0.0 all-to-all-done.5.share_ref
  117.5 1.4 %shard_map.154 = (f32[27,12288]{1,0:T(8,128)}, f32[3,27,64]{2,1,0:T(8,128)}) custom-call(bf16[16,32,768]{2,1,0:T(8,128)(2,1)S(1)} %all-to-all-done.5.share_ref, bf16[512,64]{1,0:T(8,128)(2,1)S(1)} %copy-done.3), custom_call_target="tpu_custom_call" | custom-call | tf_op jit(solution)/shard_map/pallas_call | solution.py:431
  (21 shorter events, 0.3 us)
Async XLA Ops:
  0.6 0.8 copy-start.5
  1.5 0.7 copy-start.8
  3.5 10.6 %copy-start.11 = (bf16[3,8,16,4]{2,3,1,0:T(4,128)(2,1)S(1)}, bf16[3,8,16,4]{2,3,1,0:T(4,128)(2,1)}, u32[]{:S(2)}) copy-start(bf16[3,8,16,4]{2,3,1,0:T(4,128)(2,1)} %param.15) | copy-start | bytes 9220
  3.5 10.7 %copy-start.6 = (bf16[8,16,256]{2,1,0:T(8,128)(2,1)S(1)}, bf16[8,16,256]{2,1,0:T(8,128)(2,1)}, u32[]{:S(2)}) copy-start(bf16[8,16,256]{2,1,0:T(8,128)(2,1)} %param.14) | copy-start | bytes 196612
  3.5 22.7 %copy-start.12 = (bf16[27,3,64]{2,0,1:T(8,128)(2,1)S(1)}, bf16[27,3,64]{2,0,1:T(8,128)(2,1)}, u32[]{:S(2)}) copy-start(bf16[27,3,64]{2,0,1:T(8,128)(2,1)} %param.17) | copy-start | bytes 31108
  3.5 23.5 %copy-start.2 = (bf16[384,384]{1,0:T(8,128)(2,1)S(1)}, bf16[384,384]{1,0:T(8,128)(2,1)}, u32[]{:S(2)}) copy-start(bf16[384,384]{1,0:T(8,128)(2,1)} %constant.37.clone.choice_ref) | copy-start | bytes 884740
  3.6 23.5 %copy-start.4 = (bf16[128,48]{1,0:T(8,128)(2,1)S(1)}, bf16[128,48]{1,0:T(8,128)(2,1)}, u32[]{:S(2)}) copy-start(bf16[128,48]{1,0:T(8,128)(2,1)} %constant.38.clone.cot_choice_ref) | copy-start | bytes 36868
  3.6 29.7 %all-to-all-start = ((bf16[16,160,256]{2,1,0:T(8,128)(2,1)}), bf16[16,160,256]{2,1,0:T(8,128)(2,1)S(1)}, u32[]{:S(2)}, u32[]{:S(2)}) async-start(bf16[16,160,256]{2,1,0:T(8,128)(2,1)} %shard_map.149), calls=%async_computation | async-start | bytes 2621440 | tf_op jit(solution)/shard_map/all_to_all | solution.py:363
  14.3 12.2 %collective-permute-start = (bf16[80,128]{1,0:T(8,128)(2,1)S(1)}, bf16[80,128]{1,0:T(8,128)(2,1)S(1)}, u32[]{:S(2)}, u32[]{:S(2)}) collective-permute-start(bf16[80,128]{1,0:T(8,128)(2,1)S(1)} %get-tuple-element.21), channel_id=1, source_target_pairs={{0,1},{1,2},{2,3},{3,4},{4,5},{5,6},{6,7},{7,8},{8,9},{9,10},{10,1... | collective-permute-start | bytes 61448 | tf_op jit(solution)/shard_map/ppermute | solution.py:47
  16.3 10.8 %collective-permute-start.1 = (bf16[80,128]{1,0:T(8,128)(2,1)S(1)}, bf16[80,128]{1,0:T(8,128)(2,1)S(1)}, u32[]{:S(2)}, u32[]{:S(2)}) collective-permute-start(bf16[80,128]{1,0:T(8,128)(2,1)S(1)} %get-tuple-element.23), channel_id=1, source_target_pairs={{1,0},{2,1},{3,2},{4,3},{5,4},{6,5},{7,6},{8,7},{9,8},{10,9},{11,1... | collective-permute-start | bytes 61448 | tf_op jit(solution)/shard_map/ppermute | solution.py:47
  33.3 11.4 %all-to-all-start.1 = ((bf16[16,48,128]{2,1,0:T(8,128)(2,1)}), bf16[16,48,128]{2,1,0:T(8,128)(2,1)}, u32[]{:S(2)}, u32[]{:S(2)}) async-start(bf16[16,48,128]{2,1,0:T(8,128)(2,1)} %shard_map.148), calls=%async_computation.1 | async-start | bytes 393216 | tf_op jit(solution)/shard_map/all_to_all | solution.py:363
  38.1 0.7 copy-start
  39.0 0.8 copy-start.7
  44.7 1.0 copy-start.9
  45.7 0.9 copy-start.10
  59.6 25.2 %all-to-all-start.3 = ((bf16[8,8,768]{2,1,0:T(8,128)(2,1)}), bf16[8,8,768]{2,1,0:T(8,128)(2,1)S(1)}, u32[]{:S(2)}, u32[]{:S(2)}) async-start(bf16[8,8,768]{2,1,0:T(8,128)(2,1)} %broadcast_in_dim.8), calls=%async_computation.3 | async-start | bytes 196608 | tf_op jit(solution)/shard_map/all_to_all | solution.py:363
  74.4 14.6 %collective-permute-start.3 = (bf16[2,16,512]{2,1,0:T(8,128)(2,1)S(1)}, bf16[2,16,512]{2,1,0:T(8,128)(2,1)S(1)}, u32[]{:S(2)}, u32[]{:S(2)}) collective-permute-start(bf16[2,16,512]{2,1,0:T(8,128)(2,1)S(1)} %get-tuple-element.41), channel_id=1, source_target_pairs={{128,0},{256,128},{384,256},{0,384},{129,1},{257,129},{385,257},{1... | collective-permute-start | bytes 98312 | tf_op jit(solution)/shard_map/ppermute | solution.py:47
  78.5 10.5 %collective-permute-start.2 = (bf16[2,16,512]{2,1,0:T(8,128)(2,1)S(1)}, bf16[2,16,512]{2,1,0:T(8,128)(2,1)S(1)}, u32[]{:S(2)}, u32[]{:S(2)}) collective-permute-start(bf16[2,16,512]{2,1,0:T(8,128)(2,1)S(1)} %get-tuple-element.40), channel_id=1, source_target_pairs={{0,128},{128,256},{256,384},{384,0},{1,129},{129,257},{257,385},{3... | collective-permute-start | bytes 98312 | tf_op jit(solution)/shard_map/ppermute | solution.py:47
  85.4 8.4 %all-to-all-start.4 = ((bf16[4,8,768]{2,1,0:T(8,128)(2,1)}), bf16[4,8,768]{2,1,0:T(8,128)(2,1)S(1)}, u32[]{:S(2)}, u32[]{:S(2)}) async-start(bf16[4,8,768]{2,1,0:T(8,128)(2,1)} %broadcast_in_dim.9), calls=%async_computation.4 | async-start | bytes 98304 | tf_op jit(solution)/shard_map/all_to_all | solution.py:363
  94.8 20.1 %copy-start.1 = (bf16[9,32,384]{2,1,0:T(8,128)(2,1)S(1)}, bf16[9,32,384]{2,1,0:T(8,128)(2,1)}, u32[]{:S(2)}) copy-start(bf16[9,32,384]{2,1,0:T(8,128)(2,1)} %copy-done) | copy-start | bytes 663556
  94.8 22.7 %all-to-all-start.5 = ((bf16[16,32,768]{2,1,0:T(8,128)(2,1)}), bf16[16,32,768]{2,1,0:T(8,128)(2,1)S(1)}, u32[]{:S(2)}, u32[]{:S(2)}) async-start(bf16[16,32,768]{2,1,0:T(8,128)(2,1)} %broadcast_in_dim.11), calls=%async_computation.5 | async-start | bytes 1572864 | tf_op jit(solution)/shard_map/all_to_all | solution.py:363
  102.8 11.3 %collective-permute-start.5 = (bf16[12,2,512]{2,1,0:T(2,128)(2,1)S(1)}, bf16[12,2,512]{2,1,0:T(2,128)(2,1)S(1)}, u32[]{:S(2)}, u32[]{:S(2)}) collective-permute-start(bf16[12,2,512]{2,1,0:T(2,128)(2,1)S(1)} %get-tuple-element.39), channel_id=1, source_target_pairs={{32,0},{64,32},{96,64},{0,96},{33,1},{65,33},{97,65},{1,97},{34,2}... | collective-permute-start | bytes 73736 | tf_op jit(solution)/shard_map/ppermute | solution.py:47
  107.3 7.4 %collective-permute-start.4 = (bf16[12,2,512]{2,1,0:T(2,128)(2,1)S(1)}, bf16[12,2,512]{2,1,0:T(2,128)(2,1)S(1)}, u32[]{:S(2)}, u32[]{:S(2)}) collective-permute-start(bf16[12,2,512]{2,1,0:T(2,128)(2,1)S(1)} %get-tuple-element.38), channel_id=1, source_target_pairs={{0,32},{32,64},{64,96},{96,0},{1,33},{33,65},{65,97},{97,1},{2,34}... | collective-permute-start | bytes 73736 | tf_op jit(solution)/shard_map/ppermute | solution.py:47
  114.9 2.6 %copy-start.3 = (bf16[512,64]{1,0:T(8,128)(2,1)S(1)}, bf16[512,64]{1,0:T(8,128)(2,1)}, u32[]{:S(2)}) copy-start(bf16[512,64]{1,0:T(8,128)(2,1)} %constant.42.clone.choice_ref) | copy-start | bytes 196612

commit v10 on v8

--- a/solution.py
+++ b/solution.py
@@ -57,7 +57,6 @@
             jax.ShapeDtypeStruct((80, 128), BF16),
             jax.ShapeDtypeStruct((80, 128), BF16),
         ),
-        compiler_params=pltpu.CompilerParams(vmem_limit_bytes=8 * 2**20),
     )(pre_act.reshape(128, SIZE_Z * C_HID), cot)
     before, after = from_both(high, low, GZ)
     return before, rows, after
@@ -67,9 +66,6 @@
     parts = pl.pallas_call(
         message_kernel,
         out_shape=jax.ShapeDtypeStruct((BLOCKS, 160, 256), BF16),
-        out_specs=pl.BlockSpec(memory_space=pl.ANY),
-        scratch_shapes=[pltpu.SemaphoreType.DMA((2, BLOCKS))],
-        compiler_params=pltpu.CompilerParams(vmem_limit_bytes=8 * 2**20),
     )(coarse.reshape(32, 256), skip_features.reshape(128, 256))
     return traded(parts, PLANE)
 
@@ -133,7 +129,8 @@
         jnp.asarray(tap_rows.reshape(2, 256, 216), BF16),
         jnp.asarray(head_columns.reshape(216, 512), BF16),
         jnp.asarray(head_rows.reshape(32, ROWS)),
-    ), jnp.asarray(double.reshape(128, 32), BF16)
+        jnp.asarray(double.reshape(128, 32), BF16),
+    )
 
 
 def head_channels():
@@ -238,32 +235,23 @@
                 stack_ref[start : start + ROWS, 128 * at : 128 * at + 128] = block
 
 
-def message_kernel(coarse_ref, skip_ref, parts_ref, sems):
-    copies = []
-    for at in range(BLOCKS):
-        copies.append(
-            pltpu.make_async_copy(coarse_ref, parts_ref.at[at, 0:32, :], sems.at[0, at])
-        )
-        copies.append(
-            pltpu.make_async_copy(skip_ref, parts_ref.at[at, 32:160, :], sems.at[1, at])
-        )
-    for copy in copies:
-        copy.start()
-    for copy in copies:
-        copy.wait()
-
-
-def fine_kernel(input_ref, double_ref, fine_ref):
+def message_kernel(coarse_ref, skip_ref, parts_ref):
+    for at in range(BLOCKS):
+        parts_ref[at, 0:32, :] = coarse_ref[...]
+        parts_ref[at, 32:160, :] = skip_ref[...]
+
+
+def share_kernel(
+    data_ref, input_ref, head_ref, tap_ref, column_ref, row_ref, double_ref, share_ref, stack_s, fine_s
+):
     for at in range(BLOCKS):
         rows = slice(128 * at, 128 * at + 128)
         fine = jnp.dot(double_ref[...], input_ref[at, 0:32, :], preferred_element_type=F32)
         for pair in range(2):
             lanes = slice(128 * pair, 128 * pair + 128)
-            fine_ref[pair, rows, 0:128] = fine[:, lanes].astype(BF16)
-            fine_ref[pair, rows, 128:256] = input_ref[at, 32:160, lanes]
-
-
-def share_kernel(data_ref, fine_ref, head_ref, tap_ref, column_ref, row_ref, share_ref, stack_s):
+            fine_s[pair, rows, 0:128] = fine[:, lanes].astype(BF16)
+            fine_s[pair, rows, 128:256] = input_ref[at, 32:160, lanes]
+
     blocks = [data_ref[at].astype(F32) for at in range(BLOCKS)]
     stack_moved([block[ROWS:48] for block in blocks], stack_s)
     cot = stack_s[...].astype(BF16)
@@ -286,7 +274,7 @@
     up = jnp.zeros((128, 128), F32)
     skip = jnp.zeros((128, 128), F32)
     for pair in range(2):
-        result = jnp.dot(back, fine_ref[pair], preferred_element_type=F32)
+        result = jnp.dot(back, fine_s[pair], preferred_element_type=F32)
         taps = jnp.dot(
             tap_ref[pair].astype(F32), result, precision=HIGHEST, preferred_element_type=F32
         )
@@ -369,15 +357,6 @@
     )(*deep, share_choice, cot_choice)
     parts, inputs = lax.optimization_barrier((parts, inputs))
     data = traded(parts, PLANE)
-    chosen, double = choices()
-    fine = pl.pallas_call(
-        fine_kernel,
-        out_shape=jax.ShapeDtypeStruct((2, 2048, 256), BF16),
-        compiler_params=pltpu.CompilerParams(vmem_limit_bytes=16 * 2**20),
-        cost_estimate=pl.CostEstimate(
-            flops=300_000_000, bytes_accessed=4_000_000, transcendentals=0
-        ),
-    )(inputs, double)
     field = pl.pallas_call(
         field_kernel,
         out_shape=jax.ShapeDtypeStruct((SIZE_X, SIZE_Y, 512), BF16),
@@ -386,24 +365,24 @@
             flops=60_000_000, bytes_accessed=4_000_000, transcendentals=0
         ),
     )(*deep, cot_choice)
-    data, fine, field = lax.optimization_barrier((data, fine, field))
+    data, field = lax.optimization_barrier((data, field))
     share = pl.pallas_call(
         share_kernel,
         out_shape=jax.ShapeDtypeStruct(SHARE, F32),
-        scratch_shapes=[pltpu.VMEM((216, 2048), F32)],
+        scratch_shapes=[pltpu.VMEM((216, 2048), F32), pltpu.VMEM((2, 2048, 256), BF16)],
         compiler_params=pltpu.CompilerParams(vmem_limit_bytes=32 * 2**20),
         cost_estimate=pl.CostEstimate(
             flops=1_500_000_000, bytes_accessed=2_000_000, transcendentals=200_000
         ),
-    )(data, fine, own_head_matrix(head), *chosen)
+    )(data, inputs, own_head_matrix(head), *choices())
     near = jnp.sum(traded(share.reshape(4, 8, SHARE[1]), NEAR), axis=0)
     field, near = lax.optimization_barrier((field, near))
     field = with_x_rims(field)
     far = jnp.sum(spread(near.astype(BF16), FAR).astype(F32), axis=0)
-    field, far = lax.optimization_barrier((field, far))
+    column = spread(far.astype(BF16), NEAR).reshape(SHARE)
+    weights = input_matrix(weight_one)
+    field, column, weights = lax.optimization_barrier((field, column, weights))
     field = with_y_rims(field)
-    column = spread(far, NEAR).reshape(SHARE)
-    field, column = lax.optimization_barrier((field, column))
     body, head_grad = pl.pallas_call(
         unpack_kernel,
         out_shape=(
@@ -411,7 +390,7 @@
             jax.ShapeDtypeStruct((C_VEL, 27, C_HID), F32),
         ),
         compiler_params=pltpu.CompilerParams(vmem_limit_bytes=16 * 2**20),
-    )(spread(column.astype(BF16), PLANE), head_channels())
+    )(spread(column, PLANE), head_channels())
     skip_grad, coarse_grad = pl.pallas_call(
         input_kernel,
         out_shape=(
@@ -428,7 +407,7 @@
         cost_estimate=pl.CostEstimate(
             flops=700_000_000, bytes_accessed=3_000_000, transcendentals=100_000
         ),
-    )(field, head, input_matrix(weight_one))
+    )(field, head, weights)
     return coarse_grad.reshape(4, 8, 256), skip_grad, body, jnp.transpose(head_grad, (1, 0, 2))
 
 

time: 124 us -> 115 us (0.927)
  waiting for transfers between devices: 30 us -> 22.4 us
  local copies, waits for them, and re-layouts: 10.2 us -> 7.75 us
    all_to_all x5, waiting for transfers between devices: 28 us -> 16 us  [traded(): return lax.all_to_all(parts, axes, 0, 0)]
    ppermute x3, waiting for transfers between devices: 0.51 us -> 5.77 us  [from_both(): lax.ppermute(to_previous, axis, down)]
    unnamed x30 -> x24, local copies, waits for them, and re-layouts: 5.62 us -> 0.94 us
    ppermute x3, starting transfers between devices: 16.7 us -> 18.6 us  [from_both(): lax.ppermute(to_previous, axis, down)]
    slice x2, local copies, waits for them, and re-layouts: 0.43 us -> 2.1 us  [own_head_matrix(): split = head[:, :24].reshape(9, 24, 6, BLOCKS, OWN)]
    pallas_call x1, Pallas kernels: 0.1 us -> 1.58 us  [depth_rims(): pl.pallas_call(turn_kernel, out_shape=(jax.ShapeDtypeStruct((272, 128), B...]
    all_to_all x5, starting transfers between devices: 39.4 us -> 38 us  [traded(): return lax.all_to_all(parts, axes, 0, 0)]
  transfers between devices with their start and end apart: 11 -> 11, of which waited for: 8 -> 7; matrix products, arithmetic and copies ran while one was open for 3% -> 5% of each run, Pallas kernels for 4% -> 5%
where the time goes in v10:
time: 115 us; the launch traced here: 114 us
  starting transfers between devices  62.3 us (54%)
  waiting for transfers between devices  22.4 us (19%)
  Pallas kernels  12 us (10%)
  blocking collectives  7.85 us (7%)
  local copies, waits for them, and re-layouts  7.75 us (7%)
    all_to_all x5, starting transfers between devices, traded(): return lax.all_to_all(parts, axes, 0, 0)  38 us
    ppermute x3, starting transfers between devices, from_both(): lax.ppermute(to_previous, axis, down)  18.6 us
    all_to_all x5, waiting for transfers between devices, traded(): return lax.all_to_all(parts, axes, 0, 0)  16 us
    all_to_all x1, blocking collectives, traded(): return lax.all_to_all(parts, axes, 0, 0)  7.85 us
    ppermute x3, waiting for transfers between devices, from_both(): lax.ppermute(to_previous, axis, down)  5.77 us
    ppermute x3, starting transfers between devices, from_both(): lax.ppermute(to_next, axis, up)  5.75 us
    pallas_call x1, Pallas kernels, per_device(): pl.pallas_call(share_kernel, out_shape=jax.ShapeDtypeStruct(SHARE, F32),...  3.3 us
    pallas_call x1, Pallas kernels, per_device(): pl.pallas_call(input_kernel, out_shape=(jax.ShapeDtypeStruct((SIZE_X, SIZ...  2.55 us
  transfers between devices with their start and end apart: 11, of which 7 were waited for; matrix products, arithmetic and copies ran while one was open for 5% of the time, Pallas kernels for 5%

profile of v10, /device:TPU:1, one launch (start us, length us, event | category | flops | bytes accessed | tf_op | source)
XLA Modules:
  0.0 113.9 jit_solution(2655176646697514339)
XLA Ops:
  0.6 2.0 %shard_map.158 = bf16[16,160,256]{2,1,0:T(8,128)(2,1)} custom-call(bf16[32,256]{1,0:T(8,128)(2,1)} %bitcast.26, bf16[128,256]{1,0:T(8,128)(2,1)} %bitcast.23), custom_call_target="tpu_custom_call" | custom-call | tf_op jit(solution)/shard_map/pallas_call | solution.py:66
  2.6 10.5 %all-to-all-start = ((bf16[16,160,256]{2,1,0:T(8,128)(2,1)}), bf16[16,160,256]{2,1,0:T(8,128)(2,1)S(1)}, u32[]{:S(2)}, u32[]{:S(2)}) async-start(bf16[16,160,256]{2,1,0:T(8,128)(2,1)} %shard_map.158), calls=%async_computation | async-start | bytes 2621440 | tf_op jit(solution)/shard_map/all_to_all | solution.py:340
  13.2 0.0 copy-done.10
  13.2 0.1 reshape.51
  13.3 0.6 pad.32.cot_ref
  13.9 1.6 %shard_map.156 = (bf16[272,128]{1,0:T(8,128)(2,1)}, bf16[80,128]{1,0:T(8,128)(2,1)}, bf16[80,128]{1,0:T(8,128)(2,1)}) custom-call(bf16[128,256]{1,0:T(8,128)(2,1)} %bitcast.24, bf16[16,128]{1,0:T(8,128)(2,1)} %pad.32.cot_ref), custom_call_target="tpu_custom_call" | custom-call | tf_op jit(solution)/shard_map/pallas_call | solution.py:53
  15.5 1.9 %collective-permute-start = (bf16[80,128]{1,0:T(8,128)(2,1)}, bf16[80,128]{1,0:T(8,128)(2,1)S(1)}, u32[]{:S(2)}, u32[]{:S(2)}) collective-permute-start(bf16[80,128]{1,0:T(8,128)(2,1)} %get-tuple-element.20), channel_id=1, source_target_pairs={{0,1},{1,2},{2,3},{3,4},{4,5},{5,6},{6,7},{7,8},{8,9},{9,10},{10,1... | collective-permute-start | bytes 61448 | tf_op jit(solution)/shard_map/ppermute | solution.py:47
  17.4 9.9 %collective-permute-start.1 = (bf16[80,128]{1,0:T(8,128)(2,1)}, bf16[80,128]{1,0:T(8,128)(2,1)S(1)}, u32[]{:S(2)}, u32[]{:S(2)}) collective-permute-start(bf16[80,128]{1,0:T(8,128)(2,1)} %get-tuple-element.22), channel_id=1, source_target_pairs={{1,0},{2,1},{3,2},{4,3},{5,4},{6,5},{7,6},{8,7},{9,8},{10,9},{11,1... | collective-permute-start | bytes 61448 | tf_op jit(solution)/shard_map/ppermute | solution.py:47
  27.3 0.0 copy-done.11
  27.4 0.0 collective-permute-done.before_ref
  27.4 1.0 collective-permute-done.1.after_ref
  28.4 0.0 copy-done
  28.4 0.0 copy-done.4
  28.4 0.9 copy-done.1
  29.3 0.9 shard_map.157
  30.3 2.0 %all-to-all-done.input_ref = bf16[16,160,256]{2,1,0:T(8,128)(2,1)S(1)} async-done(((bf16[16,160,256]{2,1,0:T(8,128)(2,1)}), bf16[16,160,256]{2,1,0:T(8,128)(2,1)S(1)}, u32[]{:S(2)}, u32[]{:S(2)}) %all-to-all-start) | async-done | bytes 1310752 | tf_op jit(solution)/shard_map/all_to_all | solution.py:340
  32.2 4.0 %all-to-all-start.1 = ((bf16[16,48,128]{2,1,0:T(8,128)(2,1)}), bf16[16,48,128]{2,1,0:T(8,128)(2,1)S(1)}, u32[]{:S(2)}, u32[]{:S(2)}) async-start(bf16[16,48,128]{2,1,0:T(8,128)(2,1)} %shard_map.157), calls=%async_computation.1 | async-start | bytes 393216 | tf_op jit(solution)/shard_map/all_to_all | solution.py:340
  36.2 0.1 fusion.5
  36.3 0.0 copy-start.2
  36.3 0.0 copy-start.5
  36.3 0.0 copy-start.6
  36.3 0.0 copy-start.7
  36.4 0.0 copy-start.8
  36.4 0.2 concatenate.12.head_ref
  36.6 0.7 slice.24
  37.2 1.4 %copy.25 = bf16[9,24,384]{1,2,0:T(8,128)(2,1)S(1)} copy(bf16[9,24,384]{2,1,0:T(8,128)(2,1)} %slice.24) | data formatting | bytes 331776 | tf_op jit(solution)/shard_map/slice | solution.py:92
  38.7 0.1 reshape.57.head_ref
  38.9 0.0 copy-done.2
  38.9 0.2 shard_map.159
  39.1 0.0 copy-start.9
  39.1 3.9 %all-to-all-done.1.data_ref = bf16[16,48,128]{2,1,0:T(8,128)(2,1)S(1)} async-done(((bf16[16,48,128]{2,1,0:T(8,128)(2,1)}), bf16[16,48,128]{2,1,0:T(8,128)(2,1)S(1)}, u32[]{:S(2)}, u32[]{:S(2)}) %all-to-all-start.1) | async-done | bytes 196640 | tf_op jit(solution)/shard_map/all_to_all | solution.py:340
  43.0 0.0 copy-done.5
  43.0 0.0 copy-done.6
  43.0 0.0 copy-done.7
  43.0 0.0 copy-done.8
  43.0 3.3 %shard_map.160 = f32[32,768]{1,0:T(8,128)S(1)} custom-call(bf16[16,48,128]{2,1,0:T(8,128)(2,1)S(1)} %all-to-all-done.1.data_ref, bf16[16,160,256]{2,1,0:T(8,128)(2,1)S(1)} %all-to-all-done.input_ref, bf16[24,216]{1,0:T(8,128)(2,1)S(1)} %reshape.57.head_ref, bf16[2,256,216]{2,1,0:T(8,128)(2,1)S(1)} %copy-done.5, bf16[216,512]{1,0:T(8,128)(2,1)S(1)} %copy-done.6, ...), custom_call_target="tpu_custom_call" | custom-call | flops 1500000000 | bytes 2000000 | tf_op jit(solution)/shard_map/pallas_call | solution.py:369
  46.3 7.8 %all_to_all.30 = f32[4,8,768]{2,1,0:T(8,128)S(1)} all-to-all(f32[4,8,768]{2,1,0:T(8,128)S(1)} %bitcast.17), channel_id=1, replica_groups=mesh['gx'=4,'gy'=4,'gzh'=2,'gzm'=8,'gzl'=2] {'gzh','gzl'}, dimensions={0} | all-to-all | bytes 196608 | tf_op jit(solution)/shard_map/all_to_all | solution.py:340
  54.2 0.6 broadcast_in_dim.8
  54.8 12.4 %all-to-all-start.3 = ((bf16[8,8,768]{2,1,0:T(8,128)(2,1)}), bf16[8,8,768]{2,1,0:T(8,128)(2,1)S(1)}, u32[]{:S(2)}, u32[]{:S(2)}) async-start(bf16[8,8,768]{2,1,0:T(8,128)(2,1)} %broadcast_in_dim.8), calls=%async_computation.3 | async-start | bytes 196608 | tf_op jit(solution)/shard_map/all_to_all | solution.py:340
  67.2 1.0 reshape.60
  68.2 0.1 rev.7
  68.3 0.1 slice.25
  68.4 4.2 %collective-permute-start.3 = (bf16[2,16,512]{2,1,0:T(8,128)(2,1)S(1)}, bf16[2,16,512]{2,1,0:T(8,128)(2,1)S(1)}, u32[]{:S(2)}, u32[]{:S(2)}) collective-permute-start(bf16[2,16,512]{2,1,0:T(8,128)(2,1)S(1)} %get-tuple-element.39), channel_id=1, source_target_pairs={{128,0},{256,128},{384,256},{0,384},{129,1},{257,129},{385,257},{1... | collective-permute-start | bytes 98312 | tf_op jit(solution)/shard_map/ppermute | solution.py:47
  72.6 1.9 %collective-permute-start.2 = (bf16[2,16,512]{2,1,0:T(8,128)(2,1)S(1)}, bf16[2,16,512]{2,1,0:T(8,128)(2,1)S(1)}, u32[]{:S(2)}, u32[]{:S(2)}) collective-permute-start(bf16[2,16,512]{2,1,0:T(8,128)(2,1)S(1)} %get-tuple-element.38), channel_id=1, source_target_pairs={{0,128},{128,256},{256,384},{384,0},{1,129},{129,257},{257,385},{3... | collective-permute-start | bytes 98312 | tf_op jit(solution)/shard_map/ppermute | solution.py:47
  74.5 5.4 %all-to-all-done.3 = bf16[8,8,768]{2,1,0:T(8,128)(2,1)S(1)} async-done(((bf16[8,8,768]{2,1,0:T(8,128)(2,1)}), bf16[8,8,768]{2,1,0:T(8,128)(2,1)S(1)}, u32[]{:S(2)}, u32[]{:S(2)}) %all-to-all-start.3) | async-done | bytes 98336 | tf_op jit(solution)/shard_map/all_to_all | solution.py:340
  79.9 0.6 broadcast_in_dim.9
  80.6 3.3 %all-to-all-start.4 = ((bf16[4,8,768]{2,1,0:T(8,128)(2,1)}), bf16[4,8,768]{2,1,0:T(8,128)(2,1)S(1)}, u32[]{:S(2)}, u32[]{:S(2)}) async-start(bf16[4,8,768]{2,1,0:T(8,128)(2,1)} %broadcast_in_dim.9), calls=%async_computation.4 | async-start | bytes 98304 | tf_op jit(solution)/shard_map/all_to_all | solution.py:340
  83.8 0.3 fusion.2.weight_ref
  84.1 0.0 collective-permute-done.3
  84.2 0.0 collective-permute-done.2
  84.2 4.8 %all-to-all-done.4 = bf16[4,8,768]{2,1,0:T(8,128)(2,1)S(1)} async-done(((bf16[4,8,768]{2,1,0:T(8,128)(2,1)}), bf16[4,8,768]{2,1,0:T(8,128)(2,1)S(1)}, u32[]{:S(2)}, u32[]{:S(2)}) %all-to-all-start.4) | async-done | bytes 49184 | tf_op jit(solution)/shard_map/all_to_all | solution.py:340
  89.0 1.0 broadcast_in_dim.11
  89.9 7.8 %all-to-all-start.5 = ((bf16[16,32,768]{2,1,0:T(8,128)(2,1)}), bf16[16,32,768]{2,1,0:T(8,128)(2,1)S(1)}, u32[]{:S(2)}, u32[]{:S(2)}) async-start(bf16[16,32,768]{2,1,0:T(8,128)(2,1)} %broadcast_in_dim.11), calls=%async_computation.5 | async-start | bytes 1572864 | tf_op jit(solution)/shard_map/all_to_all | solution.py:340
  97.8 4.5 %collective-permute-start.5 = (bf16[12,2,512]{2,1,0:T(2,128)(2,1)S(1)}, bf16[12,2,512]{2,1,0:T(2,128)(2,1)S(1)}, u32[]{:S(2)}, u32[]{:S(2)}) collective-permute-start(bf16[12,2,512]{2,1,0:T(2,128)(2,1)S(1)} %get-tuple-element.37), channel_id=1, source_target_pairs={{32,0},{64,32},{96,64},{0,96},{33,1},{65,33},{97,65},{1,97},{34,2}... | collective-permute-start | bytes 73736 | tf_op jit(solution)/shard_map/ppermute | solution.py:47
  102.3 1.9 %collective-permute-start.4 = (bf16[12,2,512]{2,1,0:T(2,128)(2,1)S(1)}, bf16[12,2,512]{2,1,0:T(2,128)(2,1)S(1)}, u32[]{:S(2)}, u32[]{:S(2)}) collective-permute-start(bf16[12,2,512]{2,1,0:T(2,128)(2,1)S(1)} %get-tuple-element.36), channel_id=1, source_target_pairs={{0,32},{32,64},{64,96},{96,0},{1,33},{33,65},{65,97},{97,1},{2,34}... | collective-permute-start | bytes 73736 | tf_op jit(solution)/shard_map/ppermute | solution.py:47
  104.2 0.1 pad.43.clone
  104.3 4.8 %collective-permute-done.5 = bf16[12,2,512]{2,1,0:T(2,128)(2,1)S(1)} collective-permute-done((bf16[12,2,512]{2,1,0:T(2,128)(2,1)S(1)}, bf16[12,2,512]{2,1,0:T(2,128)(2,1)S(1)}, u32[]{:S(2)}, u32[]{:S(2)}) %collective-permute-start.5) | collective-permute-done | bytes 24608 | tf_op jit(solution)/shard_map/ppermute | solution.py:47
  109.1 0.6 collective-permute-done.4
  109.7 0.2 maximum_maximum_fusion.field_ref
  109.9 0.0 copy-start.3
  109.9 2.6 %shard_map.161 = (bf16[8,16,256]{2,1,0:T(8,128)(2,1)}, bf16[32,256]{1,0:T(8,128)(2,1)}) custom-call(bf16[12,32,512]{2,1,0:T(8,128)(2,1)S(1)} %maximum_maximum_fusion.field_ref, bf16[9,32,384]{2,1,0:T(8,128)(2,1)S(1)} %concatenate.12.head_ref, bf16[9,256,256]{2,1,0:T(8,128)(2,1)S(1)} %fusion.2.weight_ref), custom_call_target="tpu_custom_call" | custom-call | flops 700000000 | bytes 3000000 | tf_op jit(solution)/shard_map/pallas_call | solution.py:394
  112.5 0.0 all-to-all-done.5.share_ref
  112.5 0.0 copy-done.3
  112.5 1.4 %shard_map.162 = (f32[27,12288]{1,0:T(8,128)}, f32[3,27,64]{2,1,0:T(8,128)}) custom-call(bf16[16,32,768]{2,1,0:T(8,128)(2,1)S(1)} %all-to-all-done.5.share_ref, bf16[512,64]{1,0:T(8,128)(2,1)S(1)} %copy-done.3), custom_call_target="tpu_custom_call" | custom-call | tf_op jit(solution)/shard_map/pallas_call | solution.py:386
  (18 shorter events, 0.2 us)
Async XLA Ops:
  2.6 10.6 %copy-start.10 = (bf16[3,8,16,4]{2,3,1,0:T(4,128)(2,1)S(1)}, bf16[3,8,16,4]{2,3,1,0:T(4,128)(2,1)}, u32[]{:S(2)}) copy-start(bf16[3,8,16,4]{2,3,1,0:T(4,128)(2,1)} %param.16) | copy-start | bytes 9220
  2.6 24.7 %copy-start.11 = (bf16[27,3,64]{2,0,1:T(8,128)(2,1)S(1)}, bf16[27,3,64]{2,0,1:T(8,128)(2,1)}, u32[]{:S(2)}) copy-start(bf16[27,3,64]{2,0,1:T(8,128)(2,1)} %param.18) | copy-start | bytes 31108
  2.6 25.8 %copy-start = (bf16[384,384]{1,0:T(8,128)(2,1)S(1)}, bf16[384,384]{1,0:T(8,128)(2,1)}, u32[]{:S(2)}) copy-start(bf16[384,384]{1,0:T(8,128)(2,1)} %constant.39.clone.choice_ref) | copy-start | bytes 884740
  2.6 25.8 %copy-start.4 = (bf16[128,48]{1,0:T(8,128)(2,1)S(1)}, bf16[128,48]{1,0:T(8,128)(2,1)}, u32[]{:S(2)}) copy-start(bf16[128,48]{1,0:T(8,128)(2,1)} %constant.40.clone.cot_choice_ref) | copy-start | bytes 36868
  2.6 29.6 %all-to-all-start = ((bf16[16,160,256]{2,1,0:T(8,128)(2,1)}), bf16[16,160,256]{2,1,0:T(8,128)(2,1)S(1)}, u32[]{:S(2)}, u32[]{:S(2)}) async-start(bf16[16,160,256]{2,1,0:T(8,128)(2,1)} %shard_map.158), calls=%async_computation | async-start | bytes 2621440 | tf_op jit(solution)/shard_map/all_to_all | solution.py:340
  15.5 11.9 %collective-permute-start = (bf16[80,128]{1,0:T(8,128)(2,1)}, bf16[80,128]{1,0:T(8,128)(2,1)S(1)}, u32[]{:S(2)}, u32[]{:S(2)}) collective-permute-start(bf16[80,128]{1,0:T(8,128)(2,1)} %get-tuple-element.20), channel_id=1, source_target_pairs={{0,1},{1,2},{2,3},{3,4},{4,5},{5,6},{6,7},{7,8},{8,9},{9,10},{10,1... | collective-permute-start | bytes 61448 | tf_op jit(solution)/shard_map/ppermute | solution.py:47
  17.4 11.0 %collective-permute-start.1 = (bf16[80,128]{1,0:T(8,128)(2,1)}, bf16[80,128]{1,0:T(8,128)(2,1)S(1)}, u32[]{:S(2)}, u32[]{:S(2)}) collective-permute-start(bf16[80,128]{1,0:T(8,128)(2,1)} %get-tuple-element.22), channel_id=1, source_target_pairs={{1,0},{2,1},{3,2},{4,3},{5,4},{6,5},{7,6},{8,7},{9,8},{10,9},{11,1... | collective-permute-start | bytes 61448 | tf_op jit(solution)/shard_map/ppermute | solution.py:47
  28.4 0.9 copy-start.1
  32.2 10.7 %all-to-all-start.1 = ((bf16[16,48,128]{2,1,0:T(8,128)(2,1)}), bf16[16,48,128]{2,1,0:T(8,128)(2,1)S(1)}, u32[]{:S(2)}, u32[]{:S(2)}) async-start(bf16[16,48,128]{2,1,0:T(8,128)(2,1)} %shard_map.157), calls=%async_computation.1 | async-start | bytes 393216 | tf_op jit(solution)/shard_map/all_to_all | solution.py:340
  36.3 2.6 %copy-start.2 = (bf16[272,128]{1,0:T(8,128)(2,1)S(1)}, bf16[272,128]{1,0:T(8,128)(2,1)}, u32[]{:S(2)}) copy-start(bf16[272,128]{1,0:T(8,128)(2,1)} %get-tuple-element.21.rows_ref) | copy-start | bytes 208900
  36.3 6.7 %copy-start.5 = (bf16[2,256,216]{2,1,0:T(8,128)(2,1)S(1)}, bf16[2,256,216]{2,1,0:T(8,128)(2,1)}, u32[]{:S(2)}) copy-start(bf16[2,256,216]{2,1,0:T(8,128)(2,1)} %constant.41.clone.tap_ref) | copy-start | bytes 663556
  36.3 6.7 %copy-start.6 = (bf16[216,512]{1,0:T(8,128)(2,1)S(1)}, bf16[216,512]{1,0:T(8,128)(2,1)}, u32[]{:S(2)}) copy-start(bf16[216,512]{1,0:T(8,128)(2,1)} %constant.42.clone.column_ref) | copy-start | bytes 663556
  36.3 6.6 %copy-start.7 = (bf16[128,32]{1,0:T(8,128)(2,1)S(1)}, bf16[128,32]{1,0:T(8,128)(2,1)}, u32[]{:S(2)}) copy-start(bf16[128,32]{1,0:T(8,128)(2,1)} %constant.44.clone.double_ref) | copy-start | bytes 24580
  36.4 6.6 %copy-start.8 = (f32[32,24]{1,0:T(8,128)S(1)}, f32[32,24]{1,0:T(8,128)}, u32[]{:S(2)}) copy-start(f32[32,24]{1,0:T(8,128)} %constant.43.clone.row_ref) | copy-start | bytes 9220
  39.1 28.1 %copy-start.9 = (bf16[27,12288]{1,0:T(8,128)(2,1)S(1)}, bf16[27,12288]{1,0:T(8,128)(2,1)}, u32[]{:S(2)}) copy-start(bf16[27,12288]{1,0:T(8,128)(2,1)} %param.17) | copy-start | bytes 1990660
  54.8 25.1 %all-to-all-start.3 = ((bf16[8,8,768]{2,1,0:T(8,128)(2,1)}), bf16[8,8,768]{2,1,0:T(8,128)(2,1)S(1)}, u32[]{:S(2)}, u32[]{:S(2)}) async-start(bf16[8,8,768]{2,1,0:T(8,128)(2,1)} %broadcast_in_dim.8), calls=%async_computation.3 | async-start | bytes 196608 | tf_op jit(solution)/shard_map/all_to_all | solution.py:340
  68.4 15.8 %collective-permute-start.3 = (bf16[2,16,512]{2,1,0:T(8,128)(2,1)S(1)}, bf16[2,16,512]{2,1,0:T(8,128)(2,1)S(1)}, u32[]{:S(2)}, u32[]{:S(2)}) collective-permute-start(bf16[2,16,512]{2,1,0:T(8,128)(2,1)S(1)} %get-tuple-element.39), channel_id=1, source_target_pairs={{128,0},{256,128},{384,256},{0,384},{129,1},{257,129},{385,257},{1... | collective-permute-start | bytes 98312 | tf_op jit(solution)/shard_map/ppermute | solution.py:47
  72.6 11.6 %collective-permute-start.2 = (bf16[2,16,512]{2,1,0:T(8,128)(2,1)S(1)}, bf16[2,16,512]{2,1,0:T(8,128)(2,1)S(1)}, u32[]{:S(2)}, u32[]{:S(2)}) collective-permute-start(bf16[2,16,512]{2,1,0:T(8,128)(2,1)S(1)} %get-tuple-element.38), channel_id=1, source_target_pairs={{0,128},{128,256},{256,384},{384,0},{1,129},{129,257},{257,385},{3... | collective-permute-start | bytes 98312 | tf_op jit(solution)/shard_map/ppermute | solution.py:47
  80.6 8.4 %all-to-all-start.4 = ((bf16[4,8,768]{2,1,0:T(8,128)(2,1)}), bf16[4,8,768]{2,1,0:T(8,128)(2,1)S(1)}, u32[]{:S(2)}, u32[]{:S(2)}) async-start(bf16[4,8,768]{2,1,0:T(8,128)(2,1)} %broadcast_in_dim.9), calls=%async_computation.4 | async-start | bytes 98304 | tf_op jit(solution)/shard_map/all_to_all | solution.py:340
  89.9 22.6 %all-to-all-start.5 = ((bf16[16,32,768]{2,1,0:T(8,128)(2,1)}), bf16[16,32,768]{2,1,0:T(8,128)(2,1)S(1)}, u32[]{:S(2)}, u32[]{:S(2)}) async-start(bf16[16,32,768]{2,1,0:T(8,128)(2,1)} %broadcast_in_dim.11), calls=%async_computation.5 | async-start | bytes 1572864 | tf_op jit(solution)/shard_map/all_to_all | solution.py:340
  97.8 11.3 %collective-permute-start.5 = (bf16[12,2,512]{2,1,0:T(2,128)(2,1)S(1)}, bf16[12,2,512]{2,1,0:T(2,128)(2,1)S(1)}, u32[]{:S(2)}, u32[]{:S(2)}) collective-permute-start(bf16[12,2,512]{2,1,0:T(2,128)(2,1)S(1)} %get-tuple-element.37), channel_id=1, source_target_pairs={{32,0},{64,32},{96,64},{0,96},{33,1},{65,33},{97,65},{1,97},{34,2}... | collective-permute-start | bytes 73736 | tf_op jit(solution)/shard_map/ppermute | solution.py:47
  102.3 7.4 %collective-permute-start.4 = (bf16[12,2,512]{2,1,0:T(2,128)(2,1)S(1)}, bf16[12,2,512]{2,1,0:T(2,128)(2,1)S(1)}, u32[]{:S(2)}, u32[]{:S(2)}) collective-permute-start(bf16[12,2,512]{2,1,0:T(2,128)(2,1)S(1)} %get-tuple-element.36), channel_id=1, source_target_pairs={{0,32},{32,64},{64,96},{96,0},{1,33},{33,65},{65,97},{97,1},{2,34}... | collective-permute-start | bytes 73736 | tf_op jit(solution)/shard_map/ppermute | solution.py:47
  109.9 2.6 %copy-start.3 = (bf16[512,64]{1,0:T(8,128)(2,1)S(1)}, bf16[512,64]{1,0:T(8,128)(2,1)}, u32[]{:S(2)}) copy-start(bf16[512,64]{1,0:T(8,128)(2,1)} %constant.45.clone.choice_ref) | copy-start | bytes 196612
